TPU v7x, 32 devices: a whole 2x2x4 slice. The times are simulated.
32 devices in a mesh: dp: 4 (over x, core), seq: 8 (over z, y).
Axes of the slice: x: 2, y: 2, z: 4, core: 2. Of those that a mesh axis runs over, the one named last changes fastest.
Arguments:
- inputs: bfloat16 [8, 4096, 512], P('dp', 'seq'), may hold values from -6 to 6
- starts: int32 [8, 8], P('dp', 'seq'), may hold values from 0 to 1, as said below
- attn_gain: float32 [512], replicated, may hold values from 0.5 to 1.5
- attn_shift: float32 [512], replicated, may hold values from -1.2 to 1.2
- query_weight: bfloat16 [512, 512], replicated, may hold values from -0.125 to 0.125
- key_weight: bfloat16 [512, 512], replicated, may hold values from -0.25 to 0.25
- value_weight: bfloat16 [512, 512], replicated, may hold values from -0.25 to 0.25
- control_weight: bfloat16 [512, 512], replicated, may hold values from -0.375 to 0.375
- output_weight: bfloat16 [512, 512], replicated, may hold values from -3 to 3
- ffn_gain: float32 [512], replicated, may hold values from 0.5 to 1.5
- ffn_shift: float32 [512], replicated, may hold values from -1.2 to 1.2
- up_weight: bfloat16 [512, 2048], replicated, may hold values from -0.25 to 0.25
- up_bias: float32 [2048], replicated, may hold values from -3 to 3
- down_weight: bfloat16 [2048, 512], replicated, may hold values from -0.125 to 0.125
- down_bias: float32 [512], replicated, may hold values from -1.8 to 1.8
- slot_means: float32 [8, 64], replicated, may hold values from 0.5 to 1.5
- cotangent: bfloat16 [8, 4096, 512], P('dp', 'seq'), may hold values from -6 to 6
Outputs:
- result: bfloat16 [8, 4096, 512], P('dp', 'seq')
- input_grad: float32 [8, 4096, 512], P('dp', 'seq')
- attn_gain_grad: float32 [512], replicated
- attn_shift_grad: float32 [512], replicated
- query_weight_grad: float32 [512, 512], replicated
- key_weight_grad: float32 [512, 512], replicated
- value_weight_grad: float32 [512, 512], replicated
- control_weight_grad: float32 [512, 512], replicated
- output_weight_grad: float32 [512, 512], replicated
- ffn_gain_grad: float32 [512], replicated
- ffn_shift_grad: float32 [512], replicated
- up_weight_grad: float32 [512, 2048], replicated
- up_bias_grad: float32 [2048], replicated
- down_weight_grad: float32 [2048, 512], replicated
- down_bias_grad: float32 [512], replicated
- new_means: float32 [8, 64], replicated
Inputs may be any that keep to these rules, and one draw needn't show every extreme that they name: `starts`: 1 marks a block of 512 tokens at which a stream's memory begins anew; of the streams 2 p .. 2 p + 1 on one index of dp, one, drawn, has no mark at all.
All inputs are finite; a program needn't handle non-finite values.
Results may differ from a plain program's by a relative error of at most 0.014.
The roundings to bfloat16 on the way count: a program that leaves them out, or rounds other values in their place, can miss the bound.
Values sent between devices are 32-bit elements; how exact they have to be, the bound alone decides.
A program may use at most 256 MiB of HBM per device.

v0:
```python
import jax
import jax.numpy as jnp
from jax import lax
from jax.sharding import PartitionSpec as P

HEADS = 8
HEAD = 64
SLOTS = 64


EPSILON = 1e-05
HUGE_VALUE = 1e30
HIGHEST = lax.Precision.HIGHEST


def carried_in(part, axis, combine, identity, reverse):
    count = lax.axis_size(axis)
    place = lax.axis_index(axis)
    ahead = count - 1 - place if reverse else place
    gathered = jax.tree.map(lambda a: lax.all_gather(a, axis), part)
    state = jax.tree.map(lambda a, e: jnp.zeros_like(a) + jnp.asarray(e, a.dtype), part, identity)

    def one(step, state):
        source = count - 1 - step if reverse else step
        return combine(
            state, jax.tree.map(lambda a: lax.dynamic_index_in_dim(a, source, 0, False), gathered)
        )

    return lax.fori_loop(0, ahead, one, state)


def product(form, left, right):
    return jnp.einsum(form, left, right, preferred_element_type=jnp.float32)


def exact_product(form, left, right):
    return jnp.einsum(form, left, right, precision=HIGHEST, preferred_element_type=jnp.float32)


def contract_rows(left, right):
    return lax.dot_general(
        left, right, (((0,), (0,)), ((), ())), preferred_element_type=jnp.float32
    )


def against_rows(left, right):
    return lax.dot_general(
        left, right, (((1,), (1,)), ((), ())), preferred_element_type=jnp.float32
    )


def norm_forward(values, gain, shift):
    centre = values - jnp.mean(values, axis=-1, keepdims=True)
    inverse = lax.rsqrt(jnp.mean(centre * centre, axis=-1, keepdims=True) + EPSILON)
    scaled = centre * inverse
    return (scaled * gain + shift, scaled, inverse)


def norm_backward(upstream, scaled, inverse, gain):
    inside = upstream * gain
    first = jnp.mean(inside, axis=-1, keepdims=True)
    second = jnp.mean(inside * scaled, axis=-1, keepdims=True)
    return (
        inverse * (inside - first - scaled * second),
        jnp.sum(upstream * scaled, axis=0),
        jnp.sum(upstream, axis=0),
    )


def advance(earlier, later):
    flag_old, max_old, total_old, memory_old = earlier
    flag_new, max_new, total_new, memory_new = later
    ceiling = jnp.maximum(max_old, max_new)
    old_factor = (1.0 - flag_new)[:, None, None] * jnp.exp(max_old - ceiling)
    new_factor = jnp.exp(max_new - ceiling)
    flagged = flag_old + flag_new - flag_old * flag_new
    return (
        flagged,
        ceiling,
        old_factor * total_old + new_factor * total_new,
        old_factor[..., None] * memory_old + new_factor[..., None] * memory_new,
    )


def retreat(earlier, later):
    flag_high, floor_high, total_high, memory_high = earlier
    flag_near, floor_near, total_near, memory_near = later
    lowest = jnp.minimum(floor_high, floor_near)
    near_factor = jnp.exp(lowest - floor_near)
    far_factor = (1.0 - flag_near)[:, None, None] * jnp.exp(lowest - floor_high)
    flagged = flag_near + flag_high - flag_near * flag_high
    return (
        flagged,
        lowest,
        near_factor * total_near + far_factor * total_high,
        near_factor[..., None] * memory_near + far_factor[..., None] * memory_high,
    )


def shards(
    inputs,
    starts,
    attn_gain,
    attn_shift,
    query_weight,
    key_weight,
    value_weight,
    control_weight,
    output_weight,
    ffn_gain,
    ffn_shift,
    up_weight,
    up_bias,
    down_weight,
    down_bias,
    slot_means,
    cotangent,
):
    streams, length, width = inputs.shape
    heads, head_size, slot_count = (HEADS, HEAD, SLOTS)
    row_count = streams * length
    tokens = inputs.astype(jnp.float32).reshape(row_count, width)
    normed, scaled_one, inverse_one = norm_forward(tokens, attn_gain, attn_shift)
    normed_low = normed.astype(jnp.bfloat16)
    queries = (
        jnp.dot(normed_low, query_weight, preferred_element_type=jnp.float32)
        .astype(jnp.bfloat16)
        .reshape(streams, length, heads, head_size)
    )
    keys_now = (
        jnp.dot(normed_low, key_weight, preferred_element_type=jnp.float32)
        .astype(jnp.bfloat16)
        .reshape(streams, length, heads, head_size)
    )
    values_now = (
        jnp.dot(normed_low, value_weight, preferred_element_type=jnp.float32)
        .astype(jnp.bfloat16)
        .reshape(streams, length, heads, head_size)
    )
    control = jnp.dot(normed_low, control_weight, preferred_element_type=jnp.float32).reshape(
        streams, length, heads, slot_count
    )
    block_max = jnp.floor(jnp.max(control, axis=1))
    local_weights = jnp.exp(control - block_max[:, None])
    local_total = jnp.sum(local_weights, axis=1)
    pair_rows = jnp.concatenate([keys_now, values_now], axis=-1).astype(jnp.float32)
    local_memory = exact_product("bthn,bthd->bhnd", local_weights, pair_rows)
    flags = starts[:, 0].astype(jnp.float32)
    forward_identity = (
        jnp.zeros_like(flags),
        jnp.full_like(block_max, -HUGE_VALUE),
        jnp.zeros_like(local_total),
        jnp.zeros_like(local_memory),
    )
    prefix = carried_in(
        (flags, block_max, local_total, local_memory), "seq", advance, forward_identity, False
    )
    prior_max = prefix[1]
    keeping = (1.0 - flags)[:, None, None]
    ceiling = jnp.maximum(prior_max, block_max)
    carried = keeping * jnp.exp(prior_max - ceiling)
    prior_total = carried * prefix[2]
    prior_memory = (carried[..., None] * prefix[3]).astype(jnp.bfloat16)
    prior_keys = prior_memory[..., :head_size]
    prior_values = prior_memory[..., head_size:]
    weights_now = jnp.exp(control - ceiling[:, None])
    causal = (
        lax.broadcasted_iota(jnp.int32, (length, length), 0)
        >= lax.broadcasted_iota(jnp.int32, (length, length), 1)
    ).astype(jnp.float32)
    totals = prior_total[:, None] + jnp.cumsum(weights_now, axis=1)
    weights_low = weights_now.astype(jnp.bfloat16)
    scores = (product("bthd,bshd->bhts", queries, keys_now) * causal).astype(jnp.bfloat16)
    numerator = product("bthd,bhnd->bthn", queries, prior_keys) + product(
        "bhts,bshn->bthn", scores, weights_low
    )
    logits = numerator / totals
    probabilities = jax.nn.softmax(logits, axis=-1)
    shares = (probabilities / totals).astype(jnp.bfloat16)
    mixing = (product("bthn,bshn->bhts", shares, weights_low) * causal).astype(jnp.bfloat16)
    attended = product("bthn,bhnd->bthd", shares, prior_values) + product(
        "bhts,bshd->bthd", mixing, values_now
    )
    writes = jnp.sum(weights_now / totals, axis=(0, 1))
    mixed = attended.reshape(row_count, width).astype(jnp.bfloat16)
    hidden = tokens + jnp.dot(mixed, output_weight, preferred_element_type=jnp.float32)
    normed_ffn, scaled_two, inverse_two = norm_forward(hidden, ffn_gain, ffn_shift)
    normed_ffn_low = normed_ffn.astype(jnp.bfloat16)
    raised = jnp.dot(normed_ffn_low, up_weight, preferred_element_type=jnp.float32) + up_bias
    activated, gelu_pull = jax.vjp(jax.nn.gelu, raised)
    activated_low = activated.astype(jnp.bfloat16)
    result = (
        hidden + jnp.dot(activated_low, down_weight, preferred_element_type=jnp.float32) + down_bias
    )
    upstream = cotangent.reshape(row_count, width)
    upstream_wide = upstream.astype(jnp.float32)
    down_bias_grad = jnp.sum(upstream_wide, axis=0)
    down_weight_grad = contract_rows(activated_low, upstream)
    activated_grad = against_rows(upstream, down_weight)
    raised_grad = gelu_pull(activated_grad)[0].astype(jnp.bfloat16)
    up_weight_grad = contract_rows(normed_ffn_low, raised_grad)
    up_bias_grad = jnp.sum(raised_grad.astype(jnp.float32), axis=0)
    hidden_part, ffn_gain_grad, ffn_shift_grad = norm_backward(
        against_rows(raised_grad, up_weight), scaled_two, inverse_two, ffn_gain
    )
    hidden_grad = upstream_wide + hidden_part
    branch_grad = hidden_grad.astype(jnp.bfloat16)
    output_weight_grad = contract_rows(mixed, branch_grad)
    ffn_summed = lax.psum(
        (
            output_weight_grad,
            ffn_gain_grad,
            ffn_shift_grad,
            up_weight_grad,
            up_bias_grad,
            down_weight_grad,
            down_bias_grad,
            writes,
        ),
        ("dp", "seq"),
    )
    attended_grad = (
        against_rows(branch_grad, output_weight)
        .astype(jnp.bfloat16)
        .reshape(streams, length, heads, head_size)
    )
    mixing_grad = (product("bthd,bshd->bhts", attended_grad, values_now) * causal).astype(
        jnp.bfloat16
    )
    share_grad = product("bthd,bhnd->bthn", attended_grad, prior_values) + product(
        "bhts,bshn->bthn", mixing_grad, weights_low
    )
    prior_values_grad = product("bthn,bthd->bhnd", shares, attended_grad)
    values_grad = product("bhts,bthd->bshd", mixing, attended_grad)
    weights_grad = product("bhts,bthn->bshn", mixing_grad, shares)
    prob_grad = share_grad / totals
    logit_grad = probabilities * (
        prob_grad - jnp.sum(probabilities * prob_grad, axis=-1, keepdims=True)
    )
    totals_grad = -share_grad * probabilities / (totals * totals) - logit_grad * logits / totals
    numerator_grad = (logit_grad / totals).astype(jnp.bfloat16)
    scores_grad = (product("bthn,bshn->bhts", numerator_grad, weights_low) * causal).astype(
        jnp.bfloat16
    )
    queries_grad = product("bthn,bhnd->bthd", numerator_grad, prior_keys) + product(
        "bhts,bshd->bthd", scores_grad, keys_now
    )
    keys_grad = product("bhts,bthd->bshd", scores_grad, queries)
    prior_keys_grad = product("bthn,bthd->bhnd", numerator_grad, queries)
    weights_grad = (
        weights_grad
        + product("bhts,bthn->bshn", scores, numerator_grad)
        + lax.cumsum(totals_grad, axis=1, reverse=True)
    )
    prior_total_grad = jnp.sum(totals_grad, axis=1)
    memory_grad = jnp.concatenate([prior_keys_grad, prior_values_grad], axis=-1)
    backward_identity = (
        jnp.zeros_like(flags),
        jnp.full_like(ceiling, HUGE_VALUE),
        jnp.zeros_like(prior_total_grad),
        jnp.zeros_like(memory_grad),
    )
    suffix = carried_in(
        (flags, ceiling, keeping * prior_total_grad, keeping[..., None] * memory_grad),
        "seq",
        retreat,
        backward_identity,
        True,
    )
    reach = jnp.exp(block_max - suffix[1])
    local_total_grad = reach * suffix[2]
    local_memory_grad = reach[..., None] * suffix[3]
    local_weights_grad = (
        exact_product("bhnd,bthd->bthn", local_memory_grad, pair_rows) + local_total_grad[:, None]
    )
    pair_rows_grad = exact_product("bthn,bhnd->bthd", local_weights, local_memory_grad)
    control_grad = weights_grad * weights_now + local_weights_grad * local_weights
    queries_low = queries_grad.astype(jnp.bfloat16).reshape(row_count, width)
    keys_low = (
        (keys_grad + pair_rows_grad[..., :head_size]).astype(jnp.bfloat16).reshape(row_count, width)
    )
    values_low = (
        (values_grad + pair_rows_grad[..., head_size:])
        .astype(jnp.bfloat16)
        .reshape(row_count, width)
    )
    control_low = control_grad.astype(jnp.bfloat16).reshape(row_count, heads * slot_count)
    query_weight_grad = contract_rows(normed_low, queries_low)
    key_weight_grad = contract_rows(normed_low, keys_low)
    value_weight_grad = contract_rows(normed_low, values_low)
    control_weight_grad = contract_rows(normed_low, control_low)
    normed_grad = (
        against_rows(queries_low, query_weight)
        + against_rows(keys_low, key_weight)
        + against_rows(values_low, value_weight)
        + against_rows(control_low, control_weight)
    )
    token_part, attn_gain_grad, attn_shift_grad = norm_backward(
        normed_grad, scaled_one, inverse_one, attn_gain
    )
    input_grad = (hidden_grad + token_part).reshape(streams, length, width)
    attn_summed = lax.psum(
        (
            attn_gain_grad,
            attn_shift_grad,
            query_weight_grad,
            key_weight_grad,
            value_weight_grad,
            control_weight_grad,
        ),
        ("dp", "seq"),
    )
    new_means = 0.9 * slot_means + 0.1 * ffn_summed[7] / (streams * lax.axis_size("dp"))
    return (
        result.reshape(streams, length, width).astype(jnp.bfloat16),
        input_grad,
        attn_summed[0],
        attn_summed[1],
        attn_summed[2],
        attn_summed[3],
        attn_summed[4],
        attn_summed[5],
        ffn_summed[0],
        ffn_summed[1],
        ffn_summed[2],
        ffn_summed[3],
        ffn_summed[4],
        ffn_summed[5],
        ffn_summed[6],
        new_means,
    )


def solution(mesh):
    return jax.shard_map(
        shards,
        mesh=mesh,
        in_specs=(
            P("dp", "seq", None),
            P("dp", "seq"),
            P(),
            P(),
            P(),
            P(),
            P(),
            P(),
            P(),
            P(),
            P(),
            P(),
            P(),
            P(),
            P(),
            P(),
            P("dp", "seq", None),
        ),
        out_specs=(
            P("dp", "seq", None),
            P("dp", "seq", None),
            P(),
            P(),
            P(),
            P(),
            P(),
            P(),
            P(),
            P(),
            P(),
            P(),
            P(),
            P(),
            P(),
            P(),
        ),
        check_vma=False,
    )
```

profile of v0, /device:TPU:0, one launch (start us, length us, event | category | flops | bytes accessed | tf_op | source)
XLA Modules:
  0.0 1561.1 jit_solution(3636810099419250422)
XLA Ops:
  10.6 2.0 copy.88
  17.0 2.1 reshape.394
  19.1 4.0 reshape.395
  23.1 2.0 fusion.99
  25.5 1.9 copy-done.24
  29.5 3.2 fusion.57
  34.2 23.4 %all-reduce = f32[16]{0:T(128)S(1)} all-reduce(f32[16]{0:T(128)S(1)} %bitcast_dynamic-update-slice_fusion), channel_id=3, replica_groups=mesh['dp'=4,'seq'=8] {'seq'}, use_global_device_ids=true, to_apply=%add | all-reduce | flops 16 | bytes 128
  57.7 2.1 convolution_convert_fusion.1
  59.8 2.1 reshape.392
  61.8 3.3 copy.94
  65.1 31.0 %all-gather = f32[16,8,64]{2,1,0:T(8,128)S(1)} all-gather(f32[2,8,64]{2,1,0:T(8,128)S(1)} %floor.17), channel_id=2, replica_groups=mesh['dp'=4,'seq'=8] {'seq'}, dimensions={0}, use_global_device_ids=true | all-gather | bytes 36864 | tf_op jit(solution)/shard_map/all_gather | solution.py:20
  96.1 2.2 fusion.58
  98.3 30.7 %all-gather.2 = f32[16,8,64]{2,1,0:T(8,128)S(1)} all-gather(f32[2,8,64]{2,1,0:T(8,128)S(1)} %fusion.58), channel_id=4, replica_groups=mesh['dp'=4,'seq'=8] {'seq'}, dimensions={0}, use_global_device_ids=true | all-gather | bytes 36864 | tf_op jit(solution)/shard_map/all_gather | solution.py:20
  129.2 5.8 multiply_convert_fusion.3
  135.9 3.0 fusion.52
  140.6 2.9 reshape.368
  143.5 4.1 copy.97
  147.6 266.1 %reduce-window.14 = f32[2,64,8,4,128]{4,2,3,1,0:T(8,128)} reduce-window(f32[2,64,8,4,128]{4,2,3,1,0:T(8,128)} %copy.97, f32[]{:T(128)} %constant.111.clone.1), window={size=1x1x1x1x128 pad=0_0x0_0x0_0x0_0x127_0}, to_apply=%region_6.7 | reduce-window | flops 66584576 | bytes 4194308 | tf_op jit(solution)/shard_map/reduce-window
  413.7 3.5 slice.34
  417.2 2.6 copy.98
  420.2 2.2 broadcast_add_fusion.1
  422.4 1.9 copy.100
  424.3 3.0 reduce_window_sum.30
  430.4 6.2 fusion.94
  436.7 2.2 divide_reduce_fusion
  440.9 2.5 multiply_convert_fusion.2
  443.4 2.7 fusion.55
  449.8 5.9 multiply_convert_fusion.4
  455.7 8.6 convert_reduce_fusion
  464.3 3.5 multiply_reduce_fusion
  470.6 3.9 reshape.393
  474.5 2.6 copy.105
  478.3 1.8 fusion.76
  480.2 3.8 multiply_convert_fusion.1
  484.1 4.9 multiply_reduce_fusion.1
  489.1 2.2 divide_convert_fusion
  493.8 4.2 fusion.24
  497.9 1.9 reshape.375
  499.9 2.6 copy.117
  502.5 633.7 %reduce-window.16 = f32[2,64,8,4,128]{4,2,3,1,0:T(8,128)S(1)} reduce-window(f32[2,64,8,4,128]{4,2,3,1,0:T(8,128)} %copy.117, f32[]{:T(128)} %constant.111.clone.1), window={size=1x1x1x1x128 pad=0_0x0_0x0_0x0_0x0_127}, to_apply=%region_18.19 | reduce-window | flops 66584576 | bytes 4194308 | tf_op jit(solution)/shard_map/reduce-window.2
  1140.0 2.0 copy.120
  1141.9 3.3 reduce_window_sum.32
  1146.8 2.5 multiply_convert_fusion
  1149.3 2.7 fusion.56
  1153.9 42.9 %all-gather.4 = f32[16,8,64]{2,1,0:T(8,128)S(1)} all-gather(f32[2,8,64]{2,1,0:T(8,128)S(1)} %get-tuple-element.310), channel_id=6, replica_groups=mesh['dp'=4,'seq'=8] {'seq'}, dimensions={0}, use_global_device_ids=true | all-gather | bytes 36864 | tf_op jit(solution)/shard_map/all_gather | solution.py:20
  1196.9 30.7 %all_gather.44 = f32[8,2,8,64]{3,2,1,0:T(8,128)S(1)} all-gather(f32[1,2,8,64]{3,2,1,0:T(8,128)S(1)} %bitcast_multiply_fusion.5), channel_id=1, replica_groups=mesh['dp'=4,'seq'=8] {'seq'}, dimensions={0}, use_global_device_ids=true | all-gather | bytes 36864 | tf_op jit(solution)/shard_map/all_gather | solution.py:20
  1231.1 6.4 fusion.104
  1237.6 4.4 fusion.109
  1242.0 4.7 fusion.92
  1246.7 16.8 %while.35 = (s32[]{:T(128)}, f32[2,8,64]{2,1,0:T(8,128)S(1)}, f32[2,8,64]{2,1,0:T(8,128)S(1)}, f32[2,8,64,128]{3,2,1,0:T(8,128)S(1)}, s32[]{:T(128)}, /*index=5*...) while((s32[]{:T(128)}, f32[2,8,64]{2,1,0:T(8,128)S(1)}, ...), condition=%wide.region_17.18_spmd, body=%wide.region_16.17_spmd.sunk | while | flops 400392 | bytes 1614039 | solution.py:29
  1263.5 5.2 fusion.67
  1268.8 4.1 convolution_bitcast_fusion
  1272.9 5.0 fusion.17
  1282.0 2.2 fusion.20
  1286.5 1.8 fusion.108
  1295.9 2.0 fusion.101
  1298.7 5.6 add_convert_fusion.1
  1307.5 3.1 fusion.50
  1310.7 38.9 %all-reduce.1 = (f32[512]{0:T(512)}, f32[512]{0:T(512)}, f32[512]{0:T(512)}, f32[512]{0:T(512)}, f32[2048]{0:T(1024)}, /*index=5*/f32[512]{0:T(512)}, f32[8,64]{1,0:T(8,128)S(1)}) all-reduce(f32[512]{0:T(512)S(1)} %get-tuple-element.240, f32[512]{0:T(512)S(1)} %get-tuple-element.247, ...), channel_id=1, replica_groups=mesh['dp'=4,'seq'=8] {'dp','seq'}, use_global_device_ids=true, to_apply=%region_23.24 | all-reduce | flops 5120 | bytes 40960 | tf_op jit(solution)/shard_map/psum | solution.py:302
  1350.2 3.6 fusion.49
  1353.8 187.1 %all-reduce.5.cloned.1.call-done = (f32[512,512]{1,0:T(8,128)}, f32[512,512]{1,0:T(8,128)}, f32[512,512]{1,0:T(8,128)}, f32[512,512]{1,0:T(8,128)}, f32[512,512]...) async-done(((f32[512,512]{1,0:T(8,128)}, f32[512,512]{1,0:T(8,128)}, f32[512,512]{1,0:T(8,128)}, f32[512,512]{1,0:T(8,128)}, f32[512,512]{1,0:T(8,128)}, ...) | async-done | bytes 13631504 | tf_op jit(solution)/shard_map/psum | solution.py:302
  1540.9 2.4 copy.182
  1547.5 2.1 copy.187
  1551.2 2.1 copy.188
  (328 shorter events, 81.5 us)
Async XLA Ops:
  7.2 442.3 %copy-start = (bf16[512,2048]{1,0:T(8,128)(2,1)S(1)}, bf16[512,2048]{1,0:T(8,128)(2,1)}, u32[]{:S(2)}) copy-start(bf16[512,2048]{1,0:T(8,128)(2,1)} %param.32) | copy-start | bytes 6291460
  7.2 5.5 copy-start.13
  7.2 5.5 copy-start.83
  7.2 5.5 copy-start.91
  7.2 127.7 %all-gather.10.cloned.1.call-start = ((), (), s32[]{:S(2)}) async-start(), calls=%async_computation.1 | async-start | bytes 4718592 | tf_op jit(solution)/shard_map/all_gather | solution.py:20
  8.9 5.2 copy-start.79
  10.6 4.0 copy-start.81
  19.1 4.0 copy-start.51
  29.5 3.3 copy-start.104
  29.5 4.6 copy-start.103
  32.8 1213.9 %all-gather.8.cloned.1.call-start = ((), (), s32[]{:S(2)}) async-start(), calls=%async_computation | async-start | bytes 4718592 | tf_op jit(solution)/shard_map/all_gather | solution.py:20
  65.1 64.0 %copy-start.25 = (bf16[2,512,8,64]{3,2,1,0:T(8,128)(2,1)S(1)}, bf16[2,512,8,64]{3,2,1,0:T(8,128)(2,1)}, u32[]{:S(2)}) copy-start(bf16[2,512,8,64]{3,2,1,0:T(8,128)(2,1)} %reshape.394) | copy-start | bytes 3145732
  65.1 64.0 %copy-start.34 = (bf16[2,512,8,64]{1,3,2,0:T(8,128)(2,1)S(1)}, bf16[2,512,8,64]{1,3,2,0:T(8,128)(2,1)}, u32[]{:S(2)}) copy-start(bf16[2,512,8,64]{1,3,2,0:T(8,128)(2,1)} %copy.94) | copy-start | bytes 3145732
  129.2 6.6 copy-start.92
  135.8 4.8 copy-start.96
  135.8 3.1 copy-start.3
  427.3 3.0 copy-start.6
  427.3 3.0 copy-start.41
  430.4 6.3 copy-start.4
  443.3 3.3 copy-start.8
  449.0 18.8 %copy-start.16 = (f32[1024,512]{1,0:T(8,128)}, f32[1024,512]{1,0:T(8,128)S(1)}, u32[]{:S(2)}) copy-start(f32[1024,512]{1,0:T(8,128)S(1)} %get-tuple-element.322) | copy-start | bytes 6291460
  449.8 5.9 copy-start.62
  449.8 5.9 copy-start.99
  464.3 3.5 copy-start.45
  480.2 3.8 copy-start.7
  480.2 3.8 copy-start.12
  480.2 3.8 copy-start.42
  484.1 4.9 copy-start.10
  489.0 3.2 copy-start.35
  493.7 1047.2 %all-reduce.5.cloned.1.call-start = ((), (), s32[]{:S(2)}) async-start(), calls=%async_computation.2 | async-start | bytes 27262976 | tf_op jit(solution)/shard_map/psum | solution.py:302
  1141.9 3.4 copy-start.31
  1149.3 3.3 copy-start.9
  1152.6 44.3 %copy-start.94 = (f32[2]{0:T(128)S(1)}, f32[2]{0:T(128)}, u32[]{:S(2)}) copy-start(f32[2]{0:T(128)} %copy-done.92) | copy-start | bytes 28
  1152.6 75.1 %copy-start.52 = (bf16[2,512,512]{2,1,0:T(8,128)(2,1)S(1)}, bf16[2,512,512]{2,1,0:T(8,128)(2,1)}, u32[]{:S(2)}) copy-start(bf16[2,512,512]{2,1,0:T(8,128)(2,1)} %fusion.38) | copy-start | bytes 3145732
  1153.9 75.5 %copy-start.54 = (bf16[64,8,2,512]{3,1,2,0:T(8,128)(2,1)}, bf16[64,8,2,512]{3,1,2,0:T(8,128)(2,1)S(1)}, u32[]{:S(2)}) copy-start(bf16[64,8,2,512]{3,1,2,0:T(8,128)(2,1)S(1)} %copy.136) | copy-start | bytes 3145732
  1153.9 75.5 %copy-start.23 = (f32[1024,512]{1,0:T(8,128)S(1)}, f32[1024,512]{1,0:T(8,128)}, u32[]{:S(2)}) copy-start(f32[1024,512]{1,0:T(8,128)} %copy-done.22) | copy-start | bytes 6291460
  1153.9 75.5 %copy-start.48 = (bf16[64,8,2,512]{3,1,2,0:T(8,128)(2,1)S(1)}, bf16[64,8,2,512]{3,1,2,0:T(8,128)(2,1)}, u32[]{:S(2)}) copy-start(bf16[64,8,2,512]{3,1,2,0:T(8,128)(2,1)} %copy-done.47) | copy-start | bytes 3145732
  1231.1 6.4 copy-start.63
  1231.1 6.4 copy-start.105
  1237.5 4.5 copy-start.17
  1237.5 4.5 copy-start.46
  1237.5 4.5 copy-start.86
  1237.5 4.5 copy-start.89
  1263.5 5.2 copy-start.5
  1268.8 4.1 copy-start.38
  1268.8 9.2 slice-start.2
  1272.9 5.0 slice-start.3
  1272.9 5.0 copy-start.36
  1272.9 6.6 slice-start
  1278.0 3.4 copy-start.44
  1278.0 4.0 copy-start.50
  1289.6 2.8 copy-start.56
  1298.7 5.6 copy-start.57
  1298.7 5.6 copy-start.76
  1307.5 3.2 copy-start.87
  1307.5 3.2 copy-start.90
  1307.5 3.2 copy-start.97
  1307.5 3.2 copy-start.98
  1307.5 42.1 %copy-start.95 = (f32[8,64]{1,0:T(8,128)S(1)}, f32[8,64]{1,0:T(8,128)}, u32[]{:S(2)}) copy-start(f32[8,64]{1,0:T(8,128)} %param.36) | copy-start | bytes 6148
  1540.9 3.4 copy-start.72
  1543.3 2.9 copy-start.70
  1544.3 3.2 copy-start.61
  1547.5 3.7 copy-start.60
  1551.2 3.1 copy-start.1
  (49 other events, 85.5 us)
Sparse Core Ops, SparseCore 0:
  32.9 77.3 all-gather.9
  493.9 86.9 all-gather.7
  1294.5 246.3 all-reduce.4
where the time goes:
time: 1590 us; the launch traced here: 1560 us
  other arithmetic  950 us (60%)
  blocking collectives  198 us (12%)
  waiting for transfers between devices  187 us (12%)
  matrix products  122 us (8%)
  local copies, waits for them, and re-layouts  87.5 us (6%)
  between operations  15.9 us (1%)
    another operation x5, other arithmetic  902 us
    psum x1, waiting for transfers between devices, shards(): lax.psum((attn_gain_grad, attn_shift_grad, query_weight_grad, key_weight_...  187 us
    all_gather x4, blocking collectives, carried_in(): gathered = jax.tree.map(lambda a: lax.all_gather(a, axis), part)  135 us
    dot_general x18, matrix products, product(): return jnp.einsum(form, left, right, preferred_element_type=jnp.float32)  52.3 us
    psum x1, blocking collectives, shards(): lax.psum((attn_gain_grad, attn_shift_grad, query_weight_grad, key_weight_...  38.9 us
    unnamed x237, local copies, waits for them, and re-layouts  32.4 us
  transfers between devices with their start and end apart: 3, of which 1 were waited for; matrix products, arithmetic and copies ran while one was open for 45% of the time, Pallas kernels for 0%

commit v1 on v0

--- a/solution.py
+++ b/solution.py
@@ -35,6 +35,13 @@
 
 def exact_product(form, left, right):
     return jnp.einsum(form, left, right, precision=HIGHEST, preferred_element_type=jnp.float32)
+
+
+def running_sum(form, mask, values):
+    high = values.astype(jnp.bfloat16)
+    rest = (values - high.astype(jnp.float32)).astype(jnp.bfloat16)
+    mask = mask.astype(jnp.bfloat16)
+    return product(form, mask, high) + product(form, mask, rest)
 
 
 def contract_rows(left, right):
@@ -168,7 +175,7 @@
         lax.broadcasted_iota(jnp.int32, (length, length), 0)
         >= lax.broadcasted_iota(jnp.int32, (length, length), 1)
     ).astype(jnp.float32)
-    totals = prior_total[:, None] + jnp.cumsum(weights_now, axis=1)
+    totals = prior_total[:, None] + running_sum("ts,bshn->bthn", causal, weights_now)
     weights_low = weights_now.astype(jnp.bfloat16)
     scores = (product("bthd,bshd->bhts", queries, keys_now) * causal).astype(jnp.bfloat16)
     numerator = product("bthd,bhnd->bthn", queries, prior_keys) + product(
@@ -250,7 +257,7 @@
     weights_grad = (
         weights_grad
         + product("bhts,bthn->bshn", scores, numerator_grad)
-        + lax.cumsum(totals_grad, axis=1, reverse=True)
+        + running_sum("ts,bthn->bshn", causal, totals_grad)
     )
     prior_total_grad = jnp.sum(totals_grad, axis=1)
     memory_grad = jnp.concatenate([prior_keys_grad, prior_values_grad], axis=-1)

time: 1590 us -> 632 us (0.40); the launches traced: 1560 us -> 623 us
  other arithmetic: 950 us -> 40.5 us
  local copies, waits for them, and re-layouts: 87.5 us -> 63.5 us
    another operation x6 -> x0, other arithmetic: 904 us -> none
    another operation x15 -> x4, local copies, waits for them, and re-layouts: 17.8 us -> 0.89 us
    unnamed x237 -> x265, local copies, waits for them, and re-layouts: 32.4 us -> 38.3 us
    dot_general x18 -> x22, matrix products: 52.3 us -> 46.7 us  [product(): return jnp.einsum(form, left, right, preferred_element_type=jnp.float32)]
  transfers between devices with their start and end apart: 3 -> 3, of which waited for: 1 -> 1; matrix products, arithmetic and copies ran while one was open for 45% -> 10% of each run, Pallas kernels for 0% -> 0%
where the time goes in v1:
time: 632 us; the launch traced here: 623 us
  blocking collectives  199 us (31%)
  waiting for transfers between devices  188 us (30%)
  matrix products  116 us (18%)
  local copies, waits for them, and re-layouts  63.5 us (10%)
  other arithmetic  40.5 us (6%)
  between operations  15.9 us (3%)
    psum x1, waiting for transfers between devices, shards(): lax.psum((attn_gain_grad, attn_shift_grad, query_weight_grad, key_weight_...  187 us
    all_gather x4, blocking collectives, carried_in(): gathered = jax.tree.map(lambda a: lax.all_gather(a, axis), part)  136 us
    dot_general x22, matrix products, product(): return jnp.einsum(form, left, right, preferred_element_type=jnp.float32)  46.7 us
    psum x1, blocking collectives, shards(): lax.psum((attn_gain_grad, attn_shift_grad, query_weight_grad, key_weight_...  38.8 us
    unnamed x265, local copies, waits for them, and re-layouts  38.3 us
    unnamed x1, blocking collectives  23.4 us
    dot_general x7, matrix products, against_rows(): lax.dot_general(left, right, (((1,), (1,)), ((), ())), preferred_element_...  20.3 us
    dot_general x7, matrix products, contract_rows(): lax.dot_general(left, right, (((0,), (0,)), ((), ())), preferred_element_...  17.9 us
  transfers between devices with their start and end apart: 3, of which 1 were waited for; matrix products, arithmetic and copies ran while one was open for 10% of the time, Pallas kernels for 0%

profile of v1, /device:TPU:0, one launch (start us, length us, event | category | flops | bytes accessed | tf_op | source)
XLA Modules:
  0.0 623.0 jit_solution(15846903297373830293)
XLA Ops:
  7.3 1.6 convert_reduce_fusion.1
  8.9 1.7 fusion.31
  10.6 2.0 copy.76
  14.6 1.7 convolution_convert_fusion.2
  17.0 2.1 reshape.371
  19.1 4.0 reshape.372
  23.1 2.0 fusion.107
  25.5 1.9 copy-done.23
  29.6 3.2 fusion.53
  34.3 23.4 %all-reduce = f32[16]{0:T(128)S(1)} all-reduce(f32[16]{0:T(128)S(1)} %bitcast_dynamic-update-slice_fusion), channel_id=3, replica_groups=mesh['dp'=4,'seq'=8] {'seq'}, use_global_device_ids=true, to_apply=%add | all-reduce | flops 16 | bytes 128
  57.8 2.1 convolution_convert_fusion.1
  59.9 2.1 reshape.369
  61.9 3.3 copy.82
  65.2 31.0 %all-gather = f32[16,8,64]{2,1,0:T(8,128)S(1)} all-gather(f32[2,8,64]{2,1,0:T(8,128)S(1)} %floor.17), channel_id=2, replica_groups=mesh['dp'=4,'seq'=8] {'seq'}, dimensions={0}, use_global_device_ids=true | all-gather | bytes 36864 | tf_op jit(solution)/shard_map/all_gather | solution.py:20
  96.2 2.2 fusion.54
  98.4 30.8 %all-gather.2 = f32[16,8,64]{2,1,0:T(8,128)S(1)} all-gather(f32[2,8,64]{2,1,0:T(8,128)S(1)} %fusion.54), channel_id=4, replica_groups=mesh['dp'=4,'seq'=8] {'seq'}, dimensions={0}, use_global_device_ids=true | all-gather | bytes 36864 | tf_op jit(solution)/shard_map/all_gather | solution.py:20
  129.3 5.8 multiply_convert_fusion.3
  136.0 2.1 fusion.55
  142.5 2.6 bitcast_divide_fusion.4
  145.1 3.6 fusion.108
  151.0 2.5 multiply_convert_fusion.2
  153.5 2.7 fusion.51
  160.0 5.9 multiply_convert_fusion.4
  165.9 8.6 %convert_reduce_fusion = (f32[2048]{0:T(1024)}, bf16[1024,2048]{1,0:T(8,128)(2,1)S(1)}) fusion(f32[1024,2048]{1,0:T(8,128)S(1)} %get-tuple-element.324, f32[2048]{0:T(1024)S(1)} %copy-done.111, bf16[1024,512]{1,0:T(8,128)(2,1)S(1)} %bitcast.312, bf16[2048,512]{1,0:T(8,128)(2,1)S(1)} %copy-done.109), kind=kOutput, calls=%fused_computation.37 | convolution fusion | flops 2195716096 | bytes 15745024 | tf_op jit(solution)/shard_map/dot_general | solution.py:54
  174.5 3.4 multiply_reduce_fusion
  179.1 1.7 convolution_convert_fusion
  180.8 3.9 reshape.370
  184.7 2.6 copy.89
  188.7 1.9 fusion.87
  190.9 2.4 multiply_convert_fusion.1
  193.4 2.6 convolution_add_fusion
  196.0 1.6 copy-done.2
  199.8 3.8 fusion.104
  205.9 1.9 fusion.83
  207.8 2.5 multiply_convert_fusion
  210.3 2.7 fusion.52
  215.0 43.5 %all-gather.4 = f32[16,8,64]{2,1,0:T(8,128)S(1)} all-gather(f32[2,8,64]{2,1,0:T(8,128)} %copy-done.83), channel_id=6, replica_groups=mesh['dp'=4,'seq'=8] {'seq'}, dimensions={0}, use_global_device_ids=true | all-gather | bytes 36864 | tf_op jit(solution)/shard_map/all_gather | solution.py:20
  258.6 31.1 %all_gather.44 = f32[8,2,8,64]{3,2,1,0:T(8,128)S(1)} all-gather(f32[1,2,8,64]{3,2,1,0:T(8,128)S(1)} %bitcast_multiply_fusion.8), channel_id=1, replica_groups=mesh['dp'=4,'seq'=8] {'seq'}, dimensions={0}, use_global_device_ids=true | all-gather | bytes 36864 | tf_op jit(solution)/shard_map/all_gather | solution.py:20
  289.7 1.8 fusion.115
  291.5 1.7 fusion.70
  293.2 2.0 fusion.63
  295.2 2.9 fusion.113
  298.2 2.9 fusion.114
  301.1 4.6 fusion.119
  305.7 4.7 fusion.99
  310.4 16.8 %while.35 = (s32[]{:T(128)}, f32[2,8,64]{2,1,0:T(8,128)S(1)}, f32[2,8,64]{2,1,0:T(8,128)S(1)}, f32[2,8,64,128]{3,2,1,0:T(8,128)S(1)}, s32[]{:T(128)}, /*index=5*...) while((s32[]{:T(128)}, f32[2,8,64]{2,1,0:T(8,128)S(1)}, ...), condition=%wide.region_15.16_spmd, body=%wide.region_14.15_spmd.sunk | while | flops 400392 | bytes 1614039 | solution.py:29
  311.2 1.5 fusion.198
  327.2 5.0 fusion.73
  332.3 4.1 convolution_bitcast_fusion
  336.4 5.0 fusion.19
  344.9 1.6 fusion.22
  348.8 1.7 fusion.118
  351.9 1.7 fusion.117
  355.0 1.7 fusion.116
  358.2 2.1 fusion.110
  361.2 5.6 add_convert_fusion.1
  370.0 2.9 fusion.46
  372.9 38.8 %all-reduce.1 = (f32[512]{0:T(512)}, f32[512]{0:T(512)}, f32[512]{0:T(512)}, f32[512]{0:T(512)}, f32[2048]{0:T(1024)}, /*index=5*/f32[512]{0:T(512)}, f32[8,64]{1,0:T(8,128)S(1)}) all-reduce(f32[512]{0:T(512)S(1)} %get-tuple-element.240, f32[512]{0:T(512)S(1)} %get-tuple-element.245, ...), channel_id=1, replica_groups=mesh['dp'=4,'seq'=8] {'dp','seq'}, use_global_device_ids=true, to_apply=%region_19.20 | all-reduce | flops 5120 | bytes 40960 | tf_op jit(solution)/shard_map/psum | solution.py:309
  412.4 3.1 fusion.45
  415.4 187.5 %all-reduce.5.cloned.1.call-done = (f32[512,512]{1,0:T(8,128)}, f32[512,512]{1,0:T(8,128)}, f32[512,512]{1,0:T(8,128)}, f32[512,512]{1,0:T(8,128)}, f32[512,512]...) async-done(((f32[512,512]{1,0:T(8,128)}, f32[512,512]{1,0:T(8,128)}, f32[512,512]{1,0:T(8,128)}, f32[512,512]{1,0:T(8,128)}, f32[512,512]{1,0:T(8,128)}, ...) | async-done | bytes 13631504 | tf_op jit(solution)/shard_map/psum | solution.py:309
  602.9 2.4 copy.161
  609.5 2.1 copy.166
  611.7 1.6 copy-done.65
  613.2 2.1 copy.167
  (339 shorter events, 61.0 us)
Async XLA Ops:
  7.2 152.5 %copy-start = (bf16[512,2048]{1,0:T(8,128)(2,1)S(1)}, bf16[512,2048]{1,0:T(8,128)(2,1)}, u32[]{:S(2)}) copy-start(bf16[512,2048]{1,0:T(8,128)(2,1)} %param.32) | copy-start | bytes 6291460
  7.2 5.5 copy-start.8
  7.2 5.5 copy-start.93
  7.2 5.5 copy-start.101
  7.2 127.8 %all-gather.10.cloned.1.call-start = ((), (), s32[]{:S(2)}) async-start(), calls=%async_computation.1 | async-start | bytes 4718592 | tf_op jit(solution)/shard_map/all_gather | solution.py:20
  8.9 5.2 copy-start.89
  10.6 4.0 copy-start.91
  19.1 4.0 copy-start.56
  25.1 110.8 %copy-start.87 = (f32[2,8,64]{2,1,0:T(8,128)}, f32[2,8,64]{2,1,0:T(8,128)S(1)}, u32[]{:S(2)}) copy-start(f32[2,8,64]{2,1,0:T(8,128)S(1)} %get-tuple-element.317) | copy-start | bytes 12292
  29.6 3.3 copy-start.114
  29.6 4.6 copy-start.113
  32.8 277.5 %all-gather.8.cloned.1.call-start = ((), (), s32[]{:S(2)}) async-start(), calls=%async_computation | async-start | bytes 4718592 | tf_op jit(solution)/shard_map/all_gather | solution.py:20
  65.2 64.0 %copy-start.24 = (bf16[2,512,8,64]{3,2,1,0:T(8,128)(2,1)S(1)}, bf16[2,512,8,64]{3,2,1,0:T(8,128)(2,1)}, u32[]{:S(2)}) copy-start(bf16[2,512,8,64]{3,2,1,0:T(8,128)(2,1)} %reshape.371) | copy-start | bytes 3145732
  65.2 64.0 %copy-start.29 = (bf16[2,512,8,64]{1,3,2,0:T(8,128)(2,1)S(1)}, bf16[2,512,8,64]{1,3,2,0:T(8,128)(2,1)}, u32[]{:S(2)}) copy-start(bf16[2,512,8,64]{1,3,2,0:T(8,128)(2,1)} %copy.82) | copy-start | bytes 3145732
  129.3 74.8 %copy-start.102 = (f32[2]{0:T(128)}, f32[2]{0:T(128)S(1)}, u32[]{:S(2)}) copy-start(f32[2]{0:T(128)S(1)} %subtract_bitcast_fusion) | copy-start | bytes 28
  136.0 60.0 %copy-start.83 = (f32[2,8,64]{2,1,0:T(8,128)}, f32[2,8,64]{2,1,0:T(8,128)S(1)}, u32[]{:S(2)}) copy-start(f32[2,8,64]{2,1,0:T(8,128)S(1)} %get-tuple-element.312) | copy-start | bytes 12292
  136.0 6.0 slice-start
  138.1 12.7 %copy-start.11 = (bf16[2,512,8,64]{1,3,2,0:T(8,128)(2,1)}, bf16[2,512,8,64]{1,3,2,0:T(8,128)(2,1)S(1)}, u32[]{:S(2)}) copy-start(bf16[2,512,8,64]{1,3,2,0:T(8,128)(2,1)S(1)} %fusion.55) | copy-start | bytes 3145732
  142.5 6.3 %copy-start.39 = (f32[2,8,64,512]{3,2,1,0:T(8,128)}, f32[2,8,64,512]{3,2,1,0:T(8,128)S(1)}, u32[]{:S(2)}) copy-start(f32[2,8,64,512]{3,2,1,0:T(8,128)S(1)} %add_add_fusion.1) | copy-start | bytes 6291460
  145.1 3.7 copy-start.49
  153.5 3.4 copy-start.6
  159.2 18.7 %copy-start.14 = (f32[1024,512]{1,0:T(8,128)}, f32[1024,512]{1,0:T(8,128)S(1)}, u32[]{:S(2)}) copy-start(f32[1024,512]{1,0:T(8,128)S(1)} %get-tuple-element.322) | copy-start | bytes 6291460
  160.0 17.9 %copy-start.85 = (f32[1024]{0:T(1024)}, f32[1024]{0:T(1024)S(1)}, u32[]{:S(2)}) copy-start(f32[1024]{0:T(1024)S(1)} %add_rsqrt_fusion) | copy-start | bytes 12292
  160.0 5.9 copy-start.67
  160.0 5.9 copy-start.109
  174.5 3.4 copy-start.45
  184.7 3.6 copy-start.18
  193.3 4.3 copy-start.2
  193.4 4.2 copy-start.5
  193.4 5.2 copy-start.40
  193.4 5.9 copy-start.50
  193.4 6.5 %copy-start.52 = (f32[2,512,8,64]{1,3,2,0:T(8,128)S(1)}, f32[2,512,8,64]{1,3,2,0:T(8,128)}, u32[]{:S(2)}) copy-start(f32[2,512,8,64]{1,3,2,0:T(8,128)} %copy-done.51) | copy-start | bytes 6291460
  199.8 3.8 copy-start.31
  205.6 397.3 %all-reduce.5.cloned.1.call-start = ((), (), s32[]{:S(2)}) async-start(), calls=%async_computation.2 | async-start | bytes 27262976 | tf_op jit(solution)/shard_map/psum | solution.py:309
  210.3 3.4 copy-start.7
  210.3 79.4 %copy-start.57 = (bf16[2,512,512]{2,1,0:T(8,128)(2,1)S(1)}, bf16[2,512,512]{2,1,0:T(8,128)(2,1)}, u32[]{:S(2)}) copy-start(bf16[2,512,512]{2,1,0:T(8,128)(2,1)} %fusion.34) | copy-start | bytes 3145732
  213.6 44.9 %copy-start.99 = (f32[2,8,64]{2,1,0:T(8,128)S(1)}, f32[2,8,64]{2,1,0:T(8,128)}, u32[]{:S(2)}) copy-start(f32[2,8,64]{2,1,0:T(8,128)} %get-tuple-element.306) | copy-start | bytes 12292
  213.6 44.9 %copy-start.103 = (f32[2]{0:T(128)S(1)}, f32[2]{0:T(128)}, u32[]{:S(2)}) copy-start(f32[2]{0:T(128)} %copy-done.102) | copy-start | bytes 28
  213.6 81.6 %slice-start.4 = ((s8[8388608]{0:T(1024)(128)(4,1)}), s8[4194304]{0:T(1024)(128)(4,1)S(1)}, s32[]{:S(2)}) async-start(s8[8388608]{0:T(1024)(128)(4,1)} %bitcast.291), calls=%async_computation.7 | async-start | bytes 8388608
  215.0 78.2 %copy-start.59 = (bf16[64,8,2,512]{3,1,2,0:T(8,128)(2,1)}, bf16[64,8,2,512]{3,1,2,0:T(8,128)(2,1)S(1)}, u32[]{:S(2)}) copy-start(bf16[64,8,2,512]{3,1,2,0:T(8,128)(2,1)S(1)} %copy.117) | copy-start | bytes 3145732
  215.0 76.5 %copy-start.21 = (f32[1024,512]{1,0:T(8,128)S(1)}, f32[1024,512]{1,0:T(8,128)}, u32[]{:S(2)}) copy-start(f32[1024,512]{1,0:T(8,128)} %copy-done.20) | copy-start | bytes 6291460
  215.0 76.5 %copy-start.48 = (bf16[64,8,2,512]{3,1,2,0:T(8,128)(2,1)S(1)}, bf16[64,8,2,512]{3,1,2,0:T(8,128)(2,1)}, u32[]{:S(2)}) copy-start(bf16[64,8,2,512]{3,1,2,0:T(8,128)(2,1)} %copy-done.47) | copy-start | bytes 3145732
  289.7 3.5 copy-start.53
  291.5 3.7 slice-start.5
  291.5 3.7 copy-start.19
  293.2 4.9 slice-start.2
  301.1 4.6 copy-start.15
  301.1 4.6 copy-start.46
  301.1 4.6 copy-start.86
  301.1 4.6 copy-start.96
  301.1 4.6 copy-start.98
  310.4 16.8 %copy-start.88 = (f32[2,8,64]{2,1,0:T(8,128)S(1)}, f32[2,8,64]{2,1,0:T(8,128)}, u32[]{:S(2)}) copy-start(f32[2,8,64]{2,1,0:T(8,128)} %copy-done.87) | copy-start | bytes 12292
  332.3 4.1 copy-start.35
  332.3 9.1 %slice-start.6 = ((s8[8388608]{0:T(1024)(128)(4,1)}), s8[4194304]{0:T(1024)(128)(4,1)S(1)}, s32[]{:S(2)}) async-start(s8[8388608]{0:T(1024)(128)(4,1)} %bitcast.293), calls=%async_computation.9 | async-start | bytes 8388608
  336.4 5.0 slice-start.7
  336.4 5.0 copy-start.32
  341.5 3.4 copy-start.55
  341.5 3.4 copy-start.84
  361.2 5.6 copy-start.62
  361.2 5.6 copy-start.80
  370.0 41.8 %copy-start.104 = (f32[8,64]{1,0:T(8,128)S(1)}, f32[8,64]{1,0:T(8,128)}, u32[]{:S(2)}) copy-start(f32[8,64]{1,0:T(8,128)} %param.36) | copy-start | bytes 6148
  370.0 42.4 %copy-start.22 = (f32[1024,512]{1,0:T(8,128)S(1)}, f32[1024,512]{1,0:T(8,128)}, u32[]{:S(2)}) copy-start(f32[1024,512]{1,0:T(8,128)} %copy-done.20) | copy-start | bytes 6291460
  602.9 3.4 copy-start.76
  609.5 3.7 copy-start.65
  (63 other events, 125.5 us)
Sparse Core Ops, SparseCore 0:
  33.0 77.4 all-gather.9
  205.7 87.9 all-gather.7
  356.8 246.0 all-reduce.4

commit v2 on v1

--- a/solution.py
+++ b/solution.py
@@ -1,16 +1,381 @@
+import functools
+
 import jax
 import jax.numpy as jnp
 from jax import lax
+from jax.experimental import pallas as pl
+from jax.experimental.pallas import tpu as pltpu
 from jax.sharding import PartitionSpec as P
 
 HEADS = 8
 HEAD = 64
 SLOTS = 64
-
-
 EPSILON = 1e-05
 HUGE_VALUE = 1e30
+MESH = pl.DeviceIdType.MESH
+F32 = jnp.float32
+BF16 = jnp.bfloat16
+LANES = 128
+HALF = 256
+
+
+def mm(left, right):
+    return lax.dot_general(left, right, (((1,), (0,)), ((), ())), preferred_element_type=F32)
+
+
+def mm_lanes(left, right):
+    return lax.dot_general(left, right, (((1,), (1,)), ((), ())), preferred_element_type=F32)
+
+
+def mm_rows(left, right):
+    return lax.dot_general(left, right, (((0,), (0,)), ((), ())), preferred_element_type=F32)
+
+
+def iota(shape, axis):
+    return lax.broadcasted_iota(jnp.int32, shape, axis)
+
+
+def first_head(shape):
+    return iota(shape, len(shape) - 1) < HEAD
+
+
+def only_head(values, head):
+    keep = first_head(values.shape) if head == 0 else jnp.logical_not(first_head(values.shape))
+    return jnp.where(keep, values, jnp.zeros_like(values))
+
+
+def both_blocks(rows):
+    doubled = jnp.concatenate([rows, rows], axis=0)
+    inside = (iota(doubled.shape, 0) < HEAD) == first_head(doubled.shape)
+    return jnp.where(inside, doubled, jnp.zeros_like(doubled))
+
+
+def one_block(square):
+    return jnp.where(first_head((HEAD, LANES)), square[:HEAD], square[HEAD:])
+
+
+def lower(shape=(HALF, HALF)):
+    return iota(shape, 0) >= iota(shape, 1)
+
+
+def upper(shape=(HALF, HALF)):
+    return iota(shape, 0) <= iota(shape, 1)
+
+
+def head_reduce(values, operation, empty):
+    here = first_head(values.shape)
+    one = operation(jnp.where(here, values, empty), axis=1, keepdims=True)
+    two = operation(jnp.where(here, empty, values), axis=1, keepdims=True)
+    return jnp.where(here, one, two)
+
+
+def parts_of(values):
+    high = values.astype(BF16)
+    return jnp.concatenate([high, (values - high.astype(F32)).astype(BF16)], axis=1)
+
+
+def add_parts(product):
+    return product[:, :LANES] + product[:, LANES:]
+
+
+def normalized(values):
+    centre = values - jnp.mean(values, axis=-1, keepdims=True)
+    inverse = lax.rsqrt(jnp.mean(centre * centre, axis=-1, keepdims=True) + EPSILON)
+    return centre * inverse, inverse
+
+
 HIGHEST = lax.Precision.HIGHEST
+class Exchange:
+    def __init__(self, size, sent, landed, send_sem, recv_sem):
+        self.size, self.sent, self.landed = size, sent, landed
+        self.send_sem, self.recv_sem = send_sem, recv_sem
+        self.me = lax.axis_index("seq")
+
+    def copy(self, to, slot):
+        return pltpu.make_async_remote_copy(
+            src_ref=self.sent.at[to],
+            dst_ref=self.landed.at[slot],
+            send_sem=self.send_sem.at[to],
+            recv_sem=self.recv_sem.at[slot],
+            device_id={"seq": to},
+            device_id_type=MESH,
+        )
+
+    def send(self, to):
+        @pl.when(to != self.me)
+        def _():
+            self.copy(to, self.me).start()
+
+        @pl.when(to == self.me)
+        def _():
+            self.landed[self.me] = self.sent[self.me]
+
+    def receive(self, slot):
+        @pl.when(slot != self.me)
+        def _():
+            self.copy(slot, slot).wait_recv()
+
+    def finish(self):
+        def one(to, unused):
+            @pl.when(to != self.me)
+            def _():
+                self.copy(to, self.me).wait_send()
+
+            return unused
+
+        lax.fori_loop(0, self.size, one, 0)
+
+
+def greet(dp, seq):
+    barrier = pltpu.get_barrier_semaphore()
+    me = lax.axis_index("seq")
+    for step in range(1, seq):
+        pl.semaphore_signal(
+            barrier, inc=1, device_id={"seq": lax.rem(me + step, seq)}, device_id_type=MESH
+        )
+    pl.semaphore_wait(barrier, seq - 1)
+
+
+def block_of(combo):
+    stream, pair = combo // 4, lax.rem(combo, 4)
+    return (
+        pl.multiple_of(stream * 512, 512),
+        pl.multiple_of(pair * LANES, LANES),
+    )
+
+
+def forward_kernel(
+    seq,
+    tokens,
+    flags,
+    attn_gain,
+    attn_shift,
+    wq,
+    wk,
+    wv,
+    wc,
+    normed,
+    queries,
+    keys,
+    values,
+    local,
+    weights,
+    inverse_totals,
+    logits,
+    chances,
+    shares,
+    mixed,
+    prior,
+    notes,
+    writes,
+    numerators,
+    sums,
+    out_one,
+    land_one,
+    out_two,
+    land_two,
+    send_one,
+    recv_one,
+    send_two,
+    recv_two,
+):
+    groups = seq // 8
+    part = LANES // groups
+    greet(4, seq)
+    there = Exchange(seq, out_one, land_one, send_one, recv_one)
+    back = Exchange(seq, out_two, land_two, send_two, recv_two)
+    me = there.me
+
+    def project(step, unused):
+        rows = pl.ds(pl.multiple_of(step * HALF, HALF), HALF)
+        scaled, _ = normalized(tokens[rows, :].astype(F32))
+        low = (scaled * attn_gain[...] + attn_shift[...]).astype(BF16)
+        normed[rows, :] = low
+        local[rows, :] = mm(low, wc[...])
+        keys[rows, :] = mm(low, wk[...]).astype(BF16)
+        values[rows, :] = mm(low, wv[...]).astype(BF16)
+        return unused
+
+    def summarize(combo, unused):
+        row, col = block_of(combo)
+        rows, cols = pl.ds(row, 512), pl.ds(col, LANES)
+        control = local[rows, cols]
+        block_max = jnp.floor(jnp.max(control, axis=0, keepdims=True))
+        spread = jnp.exp(control - block_max)
+        local[rows, cols] = spread
+        pair_rows = jnp.concatenate([keys[rows, cols], values[rows, cols]], axis=1)
+        memory = add_parts(mm_rows(pair_rows, parts_of(spread)))
+        memory = jnp.concatenate([one_block(memory[:LANES]), one_block(memory[LANES:])], axis=0)
+        total = jnp.sum(spread, axis=0, keepdims=True)
+        flag = flags[pl.ds(combo // 4, 1), :]
+        line = iota((8, LANES), 0)
+        small = jnp.where(line == 0, block_max, jnp.where(line == 1, total, flag))
+        notes[combo] = small
+        for group in range(groups):
+            to = combo * groups + group
+            out_one[to, :part] = memory[group * part : (group + 1) * part]
+            out_one[to, part:] = small
+            there.send(to)
+        return unused
+
+    for stream in range(2):
+        lax.fori_loop(2 * stream, 2 * stream + 2, project, 0)
+        lax.fori_loop(4 * stream, 4 * stream + 4, summarize, 0)
+
+    def project_query(step, unused):
+        rows = pl.ds(pl.multiple_of(step * HALF, HALF), HALF)
+        queries[rows, :] = mm(normed[rows, :], wq[...]).astype(BF16)
+        return unused
+
+    lax.fori_loop(0, 4, project_query, 0)
+
+    def inside(combo, unused):
+        row, col = block_of(combo)
+        cols = pl.ds(col, LANES)
+        spread = local[pl.ds(row, 512), cols]
+        low = spread.astype(BF16)
+        triangle = lower()
+        ones = jnp.where(triangle, 1.0, 0.0).astype(BF16)
+        first = add_parts(mm(ones, parts_of(spread[:HALF])))
+        second = add_parts(mm(ones, parts_of(spread[HALF:]))) + first[HALF - 1 :]
+        sums[pl.ds(row, HALF), cols] = first
+        sums[pl.ds(row + HALF, HALF), cols] = second
+        for at in range(2):
+            rows = pl.ds(row + at * HALF, HALF)
+            width = (at + 1) * HALF
+            total = None
+            for head in range(2):
+                query = only_head(queries[rows, cols], head)
+                found = []
+                for other in range(at + 1):
+                    score = mm_lanes(query, keys[pl.ds(row + other * HALF, HALF), cols])
+                    if other == at:
+                        score = jnp.where(triangle, score, 0.0)
+                    found.append(score.astype(BF16))
+                score = found[0] if at == 0 else jnp.concatenate(found, axis=1)
+                term = mm(score, only_head(low[:width], head))
+                total = term if total is None else total + term
+            numerators[rows, cols] = total
+        return unused
+
+    lax.fori_loop(0, 4, inside, 0)
+
+    prior_max = jnp.full((1, LANES), -HUGE_VALUE, F32)
+    raw_total = jnp.zeros((1, LANES), F32)
+    raw_memory = jnp.zeros((part, LANES), F32)
+    for source in range(seq):
+        out_two[source, :part] = raw_memory
+        line = iota((8, LANES), 0)
+        out_two[source, part:] = jnp.where(line == 0, prior_max, raw_total)
+        back.send(source)
+        if source == seq - 1:
+            there.receive(source)
+            break
+        there.receive(source)
+        block_max = land_one[source, part : part + 1]
+        total = land_one[source, part + 1 : part + 2]
+        flag = land_one[source, part + 2 : part + 3]
+        ceiling = jnp.maximum(prior_max, block_max)
+        old = (1.0 - flag) * jnp.exp(prior_max - ceiling)
+        new = jnp.exp(block_max - ceiling)
+        raw_total = old * raw_total + new * total
+        raw_memory = old * raw_memory + new * land_one[source, :part]
+        prior_max = ceiling
+
+    lax.fori_loop(4, 8, inside, 0)
+
+    def attend(combo, unused):
+        row, col = block_of(combo)
+        cols = pl.ds(col, LANES)
+        for group in range(groups):
+            back.receive(combo * groups + group)
+        if groups == 1:
+            memory = land_two[combo, :LANES]
+        else:
+            memory = jnp.concatenate(
+                [land_two[combo * groups + group, :part] for group in range(groups)], axis=0
+            )
+        past_max = land_two[combo * groups, part : part + 1]
+        past_total = land_two[combo * groups, part + 1 : part + 2]
+        block_max = notes[combo, 0:1]
+        flag = notes[combo, 2:3]
+        ceiling = jnp.maximum(past_max, block_max)
+        carried = (1.0 - flag) * jnp.exp(past_max - ceiling)
+        factor = jnp.exp(block_max - ceiling)
+        notes[combo, 1:2] = ceiling
+        memory = (carried * memory).astype(BF16)
+        prior[combo] = memory
+        prior_keys = both_blocks(memory[:HEAD])
+        prior_values = both_blocks(memory[HEAD:])
+        triangle = lower()
+        written = jnp.zeros((1, LANES), F32)
+        for at in range(2):
+            rows = pl.ds(row + at * HALF, HALF)
+            weight = local[rows, cols] * factor
+            weights[rows, cols] = weight.astype(BF16)
+            inverse = 1.0 / (carried * past_total + factor * sums[rows, cols])
+            inverse_totals[rows, cols] = inverse
+            written = written + jnp.sum(weight * inverse, axis=0, keepdims=True)
+            logit = (mm(queries[rows, cols], prior_keys) + factor * numerators[rows, cols]) * inverse
+            logits[rows, cols] = logit
+            top = head_reduce(logit, jnp.max, -HUGE_VALUE)
+            raised = jnp.exp(logit - top)
+            chance = raised / head_reduce(raised, jnp.sum, 0.0)
+            chances[rows, cols] = chance
+            share = (chance * inverse).astype(BF16)
+            shares[rows, cols] = share
+            attended = mm_lanes(share, prior_values)
+            for head in range(2):
+                own = only_head(share, head)
+                for other in range(at + 1):
+                    these = pl.ds(row + other * HALF, HALF)
+                    mixing = mm_lanes(own, weights[these, cols])
+                    if other == at:
+                        mixing = jnp.where(triangle, mixing, 0.0)
+                    attended = attended + mm(
+                        mixing.astype(BF16), only_head(values[these, cols], head)
+                    )
+            mixed[rows, cols] = attended.astype(BF16)
+        writes[combo] = jnp.broadcast_to(written, (8, LANES))
+        return unused
+
+    lax.fori_loop(0, 8, attend, 0)
+    there.finish()
+    back.finish()
+
+
+def vmem():
+    return pl.BlockSpec(memory_space=pltpu.VMEM)
+
+
+def forward_call(seq, tokens, flags, attn_gain, attn_shift, wq, wk, wv, wc):
+    rows, width = tokens.shape
+    part = LANES // (seq // 8)
+    wide = jax.ShapeDtypeStruct((rows, width), F32)
+    slim = jax.ShapeDtypeStruct((rows, width), BF16)
+    small = jax.ShapeDtypeStruct((8, 8, LANES), F32)
+    blocks = pltpu.VMEM((seq, part + 8, LANES), F32)
+    outs = [slim, slim, slim, slim, wide, slim, wide, wide, wide, slim, slim]
+    outs += [jax.ShapeDtypeStruct((8, LANES, LANES), BF16), small, small]
+    return pl.pallas_call(
+        functools.partial(forward_kernel, seq),
+        out_shape=outs,
+        in_specs=[vmem()] * 8,
+        out_specs=[vmem()] * len(outs),
+        scratch_shapes=[
+            pltpu.VMEM((rows, width), F32),
+            pltpu.VMEM((rows, width), F32),
+            blocks,
+            blocks,
+            blocks,
+            blocks,
+        ]
+        + [pltpu.SemaphoreType.DMA((seq,))] * 4,
+        compiler_params=pltpu.CompilerParams(
+            collective_id=1, has_side_effects=True, vmem_limit_bytes=60 * 2**20
+        ),
+        name="forward",
+    )(tokens, flags, attn_gain, attn_shift, wq, wk, wv, wc)
 
 
 def carried_in(part, axis, combine, identity, reverse):
@@ -126,70 +491,31 @@
     streams, length, width = inputs.shape
     heads, head_size, slot_count = (HEADS, HEAD, SLOTS)
     row_count = streams * length
-    tokens = inputs.astype(jnp.float32).reshape(row_count, width)
-    normed, scaled_one, inverse_one = norm_forward(tokens, attn_gain, attn_shift)
-    normed_low = normed.astype(jnp.bfloat16)
-    queries = (
-        jnp.dot(normed_low, query_weight, preferred_element_type=jnp.float32)
-        .astype(jnp.bfloat16)
-        .reshape(streams, length, heads, head_size)
-    )
-    keys_now = (
-        jnp.dot(normed_low, key_weight, preferred_element_type=jnp.float32)
-        .astype(jnp.bfloat16)
-        .reshape(streams, length, heads, head_size)
-    )
-    values_now = (
-        jnp.dot(normed_low, value_weight, preferred_element_type=jnp.float32)
-        .astype(jnp.bfloat16)
-        .reshape(streams, length, heads, head_size)
-    )
-    control = jnp.dot(normed_low, control_weight, preferred_element_type=jnp.float32).reshape(
-        streams, length, heads, slot_count
-    )
-    block_max = jnp.floor(jnp.max(control, axis=1))
-    local_weights = jnp.exp(control - block_max[:, None])
-    local_total = jnp.sum(local_weights, axis=1)
+    tokens_low = inputs.reshape(row_count, width)
+    tokens = tokens_low.astype(jnp.float32)
+    flags = starts[:, 0].astype(jnp.float32)
+    (normed_low, queries, keys_now, values_now, local_weights, weights_low, inverse_totals, logits, probabilities, shares, mixed, prior, notes, writes) = forward_call(
+        lax.axis_size("seq"), tokens_low, jnp.broadcast_to(flags[:, None], (2, LANES)), attn_gain[None], attn_shift[None],
+        query_weight, key_weight, value_weight, control_weight)
+    _, scaled_one, inverse_one = norm_forward(tokens, attn_gain, attn_shift)
+    def split(a): return a.reshape(streams, length, heads, head_size)
+    queries, keys_now, values_now, local_weights, weights_low, inverse_totals, logits, probabilities, shares = [split(a) for a in (queries, keys_now, values_now, local_weights, weights_low, inverse_totals, logits, probabilities, shares)]
+    totals = 1.0 / inverse_totals
+    def row(i): return notes[:, i].reshape(streams, heads, slot_count)
+    block_max, ceiling = row(0), row(1)
+    keeping = (1.0 - flags)[:, None, None]
+    weights_now = local_weights * jnp.exp(block_max - ceiling)[:, None]
+    prior = prior.reshape(streams, 4, 2, head_size, 2, slot_count)
+    prior = jnp.transpose(prior, (2, 0, 1, 4, 5, 3)).reshape(2, streams, heads, slot_count, head_size)
+    prior_keys, prior_values = prior[0], prior[1]
+    writes = jnp.sum(writes[:, 0].reshape(streams, heads, slot_count), axis=0)
     pair_rows = jnp.concatenate([keys_now, values_now], axis=-1).astype(jnp.float32)
-    local_memory = exact_product("bthn,bthd->bhnd", local_weights, pair_rows)
-    flags = starts[:, 0].astype(jnp.float32)
-    forward_identity = (
-        jnp.zeros_like(flags),
-        jnp.full_like(block_max, -HUGE_VALUE),
-        jnp.zeros_like(local_total),
-        jnp.zeros_like(local_memory),
-    )
-    prefix = carried_in(
-        (flags, block_max, local_total, local_memory), "seq", advance, forward_identity, False
-    )
-    prior_max = prefix[1]
-    keeping = (1.0 - flags)[:, None, None]
-    ceiling = jnp.maximum(prior_max, block_max)
-    carried = keeping * jnp.exp(prior_max - ceiling)
-    prior_total = carried * prefix[2]
-    prior_memory = (carried[..., None] * prefix[3]).astype(jnp.bfloat16)
-    prior_keys = prior_memory[..., :head_size]
-    prior_values = prior_memory[..., head_size:]
-    weights_now = jnp.exp(control - ceiling[:, None])
     causal = (
         lax.broadcasted_iota(jnp.int32, (length, length), 0)
         >= lax.broadcasted_iota(jnp.int32, (length, length), 1)
     ).astype(jnp.float32)
-    totals = prior_total[:, None] + running_sum("ts,bshn->bthn", causal, weights_now)
-    weights_low = weights_now.astype(jnp.bfloat16)
     scores = (product("bthd,bshd->bhts", queries, keys_now) * causal).astype(jnp.bfloat16)
-    numerator = product("bthd,bhnd->bthn", queries, prior_keys) + product(
-        "bhts,bshn->bthn", scores, weights_low
-    )
-    logits = numerator / totals
-    probabilities = jax.nn.softmax(logits, axis=-1)
-    shares = (probabilities / totals).astype(jnp.bfloat16)
     mixing = (product("bthn,bshn->bhts", shares, weights_low) * causal).astype(jnp.bfloat16)
-    attended = product("bthn,bhnd->bthd", shares, prior_values) + product(
-        "bhts,bshd->bthd", mixing, values_now
-    )
-    writes = jnp.sum(weights_now / totals, axis=(0, 1))
-    mixed = attended.reshape(row_count, width).astype(jnp.bfloat16)
     hidden = tokens + jnp.dot(mixed, output_weight, preferred_element_type=jnp.float32)
     normed_ffn, scaled_two, inverse_two = norm_forward(hidden, ffn_gain, ffn_shift)
     normed_ffn_low = normed_ffn.astype(jnp.bfloat16)

time: 632 us -> 645 us (1.021)
  blocking collectives: 199 us -> 134 us
  local copies, waits for them, and re-layouts: 63.5 us -> 119 us
  Pallas kernels: 0 us -> 42.1 us
  other arithmetic: 40.5 us -> 30 us
    all_gather x4 -> x2, blocking collectives: 136 us -> 61.4 us  [carried_in(): gathered = jax.tree.map(lambda a: lax.all_gather(a, axis), part)]
    reshape x6 -> x19, local copies, waits for them, and re-layouts: 12.2 us -> 71 us  [the longest x18 69 us: split(): return a.reshape(streams, length, heads, head_size)]
    pallas_call x0 -> x1, Pallas kernels: none -> 42.1 us  [forward_call(): pl.pallas_call(functools.partial(forward_kernel, seq), out_shape=outs, in...]
    unnamed x265 -> x145, local copies, waits for them, and re-layouts: 38.3 us -> 26.3 us
    unnamed x1, blocking collectives: 23.4 us -> 34 us
    dot_general x22 -> x14, matrix products: 46.7 us -> 46.7 us  [product(): return jnp.einsum(form, left, right, preferred_element_type=jnp.float32)]
  transfers between devices with their start and end apart: 3 -> 2, of which waited for: 1 -> 1; matrix products, arithmetic and copies ran while one was open for 10% -> 11% of each run, Pallas kernels for 0% -> 0%
where the time goes in v2:
time: 645 us; the launch traced here: 640 us
  waiting for transfers between devices  186 us (29%)
  blocking collectives  134 us (21%)
  local copies, waits for them, and re-layouts  119 us (18%)
  matrix products  113 us (18%)
  Pallas kernels  42.1 us (7%)
  other arithmetic  30 us (5%)
  between operations  15.6 us (2%)
    psum x1, waiting for transfers between devices, shards(): lax.psum((attn_gain_grad, attn_shift_grad, query_weight_grad, key_weight_...  186 us
    reshape x18, local copies, waits for them, and re-layouts, split(): return a.reshape(streams, length, heads, head_size)  69 us
    all_gather x2, blocking collectives, carried_in(): gathered = jax.tree.map(lambda a: lax.all_gather(a, axis), part)  61.4 us
    dot_general x14, matrix products, product(): return jnp.einsum(form, left, right, preferred_element_type=jnp.float32)  46.7 us
    pallas_call x1, Pallas kernels, forward_call(): pl.pallas_call(functools.partial(forward_kernel, seq), out_shape=outs, in...  42.1 us
    psum x1, blocking collectives, shards(): lax.psum((attn_gain_grad, attn_shift_grad, query_weight_grad, key_weight_...  38.6 us
    unnamed x1, blocking collectives  34 us
    unnamed x145, local copies, waits for them, and re-layouts  26.3 us
  transfers between devices with their start and end apart: 2, of which 1 were waited for; matrix products, arithmetic and copies ran while one was open for 11% of the time, Pallas kernels for 0%

profile of v2, /device:TPU:0, one launch (start us, length us, event | category | flops | bytes accessed | tf_op | source)
XLA Modules:
  0.0 640.0 jit_solution(12211297437937210012)
XLA Ops:
  9.4 42.1 %forward.1 = (bf16[1024,512]{1,0:T(8,128)(2,1)}, bf16[1024,512]{1,0:T(8,128)(2,1)}, bf16[1024,512]{1,0:T(8,128)(2,1)}, bf16[1024,512]{1,0:T(8,128)(2,1)}, f32[10...) custom-call(bf16[1024,512]{1,0:T(8,128)(2,1)} %bitcast.177, ...), custom_call_target="tpu_custom_call" | custom-call | tf_op jit(solution)/shard_map/forward/pallas_call | solution.py:360
  53.6 2.1 fusion.77
  57.5 3.9 reshape.299
  61.4 3.9 reshape.282
  65.2 3.3 copy.110
  68.5 3.9 reshape.284
  72.4 3.3 copy.121
  75.7 3.9 reshape.285
  79.6 3.3 copy.129
  82.9 2.5 fusion.78
  87.2 4.4 reshape.280
  91.5 3.8 copy.114
  95.4 4.4 reshape.283
  99.7 3.9 copy.112
  103.6 4.4 reshape.279
  108.0 4.0 copy.125
  112.1 7.4 %multiply_convert_fusion.6 = (bf16[1024,2048]{1,0:T(8,128)(2,1)}, f32[1024,2048]{1,0:T(8,128)S(1)}) fusion(f32[2048]{0:T(1024)S(1)} %copy-done.58, bf16[512,2048]{1,0:T(8,128)(2,1)S(1)} %copy-done, f32[1024,512]{1,0:T(8,128)} %copy-done.4, f32[512]{0:T(512)S(1)} %copy-done.53, f32[512]{0:T(512)S(1)} %copy-done.51, f32[1024]{0:T(1024)S(1)} %add_rsqrt_fusion, ...), kind=kOutput, calls=%fused_computation.30 | convolution fusion | flops 2171076608 | bytes 16797696 | tf_op jit(solution)/shard_map/dot_general | solution.py:522
  119.5 8.0 %convert_reduce_fusion = (f32[2048]{0:T(1024)S(1)}, bf16[1024,2048]{1,0:T(8,128)(2,1)S(1)}) fusion(f32[1024,2048]{1,0:T(8,128)S(1)} %get-tuple-element.249, f32[2048]{0:T(1024)S(1)} %copy-done.58, bf16[1024,512]{1,0:T(8,128)(2,1)S(1)} %bitcast.189, bf16[2048,512]{1,0:T(8,128)(2,1)S(1)} %copy-done.55), kind=kOutput, calls=%fused_computation.27 | convolution fusion | flops 2195716096 | bytes 15745024 | tf_op jit(solution)/shard_map/dot_general | solution.py:419
  127.5 2.9 multiply_reduce_fusion
  133.3 3.9 reshape.281
  137.2 3.7 copy.105
  140.9 2.1 convolution_bitcast_fusion.1
  144.6 2.4 multiply_convert_fusion.3
  147.1 2.6 convolution_add_fusion
  152.9 2.7 fusion.75
  159.0 34.0 %all-reduce = f32[16]{0:T(128)S(1)} all-reduce(f32[16]{0:T(128)S(1)} %fusion.64), channel_id=2, replica_groups=mesh['dp'=4,'seq'=8] {'seq'}, use_global_device_ids=true, to_apply=%add | all-reduce | flops 16 | bytes 128
  193.0 3.3 copy.143
  198.2 3.9 reshape.300
  202.1 3.3 copy.142
  205.4 4.4 reshape.286
  209.8 3.9 copy.132
  215.5 2.5 multiply_convert_fusion.2
  218.0 2.7 fusion.46
  223.5 30.7 %all_gather.15 = f32[8,2,8,64]{3,2,1,0:T(8,128)S(1)} all-gather(f32[1,2,8,64]{3,2,1,0:T(8,128)S(1)} %all_gather_reshape_squeeze.3), channel_id=1, replica_groups=mesh['dp'=4,'seq'=8] {'seq'}, dimensions={0}, use_global_device_ids=true | all-gather | bytes 36864 | tf_op jit(solution)/shard_map/all_gather | solution.py:385
  254.3 30.7 %all_gather.16 = f32[8,2,8,64]{3,2,1,0:T(8,128)S(1)} all-gather(f32[1,2,8,64]{3,2,1,0:T(8,128)S(1)} %bitcast_multiply_fusion.6), channel_id=1, replica_groups=mesh['dp'=4,'seq'=8] {'seq'}, dimensions={0}, use_global_device_ids=true | all-gather | bytes 36864 | tf_op jit(solution)/shard_map/all_gather | solution.py:385
  285.0 3.5 fusion.85
  290.2 2.1 fusion.50
  292.3 2.0 fusion.47
  294.3 2.9 fusion.84
  297.3 4.4 fusion.89
  301.7 4.7 fusion.71
  307.2 17.3 %while.18 = (s32[]{:T(128)}, f32[2,8,64]{2,1,0:T(8,128)S(1)}, f32[2,8,64]{2,1,0:T(8,128)S(1)}, f32[2,8,64,128]{3,2,1,0:T(8,128)}, s32[]{:T(128)}, /*index=5*/f32...) while((s32[]{:T(128)}, f32[2,8,64]{2,1,0:T(8,128)S(1)}, ...), condition=%wide.region_9.0_spmd, body=%wide.region_8.0_spmd.sunk | while | flops 400392 | bytes 1614039 | solution.py:394
  307.3 2.3 fusion.149
  309.7 2.3 fusion.149
  312.1 2.3 fusion.149
  314.5 2.3 fusion.149
  316.9 2.3 fusion.149
  319.3 2.3 fusion.149
  321.8 2.3 fusion.149
  324.5 7.9 %convolution_bitcast_fusion = f32[2,512,8,128]{1,3,2,0:T(8,128)} fusion(f32[2,512,8,64]{1,3,2,0:T(8,128)} %copy.132, f32[2,8,64,128]{3,2,1,0:T(8,128)} %get-tuple-element.184, f32[2,8,64]{2,1,0:T(8,128)S(1)} %get-tuple-element.236), kind=kOutput, calls=%fused_computation.37 | convolution fusion | flops 805437440 | bytes 6819840 | tf_op jit(solution)/shard_map/bthn,bhnd->bthd/dot_general | solution.py:402
  332.4 7.4 %fusion.32 = bf16[2,512,8,64]{1,3,2,0:T(8,128)(2,1)} fusion(f32[2,512,8,128]{1,3,2,0:T(8,128)} %convolution_bitcast_fusion, bf16[2,512,8,64]{1,3,2,0:T(8,128)(2,1)} %copy.105, f32[512,512]{1,0:T(8,128)S(1)} %fusion.48, bf16[2,512,8,64]{1,3,2,0:T(8,128)(2,1)} %copy.129, bf16[2,512,8,64]{1,3,2,0:T(8,128)(2,1)} %copy.110), kind=kOutput, calls=%fused_computation.50 | convolution fusion | flops 1083179008 | bytes 7340032 | tf_op jit(solution)/shard_map/bhts,bthd->bshd/dot_general | solution.py:398
  339.8 6.8 %fusion.33 = bf16[2,512,8,64]{1,3,2,0:T(8,128)(2,1)} fusion(f32[2,512,8,128]{1,3,2,0:T(8,128)} %convolution_bitcast_fusion, bf16[2,512,8,64]{1,3,2,0:T(8,128)(2,1)} %copy.121, bf16[2,8,512,512]{3,2,1,0:T(8,128)(2,1)} %copy-done.3), kind=kOutput, calls=%fused_computation.52 | convolution fusion | flops 537919488 | bytes 12582912 | tf_op jit(solution)/shard_map/bhts,bthd->bshd/dot_general | solution.py:398
  346.6 4.1 fusion.34
  350.8 10.6 %fusion.39 = bf16[2,512,8,64]{1,3,2,0:T(8,128)(2,1)} fusion(f32[2,512,8,64]{1,3,2,0:T(8,128)} %copy.132, f32[2,8,512,64]{2,3,1,0:T(8,128)} %fusion.34, f32[2,8,64,512]{3,2,1,0:T(8,128)} %fusion.50, f32[2,8,64,512]{3,2,1,0:T(8,128)} %fusion.47, f32[2,8,64,512]{3,2,1,0:T(8,128)} %fusion.84, bf16[2,512,8,64]{1,3,2,0:T(8,128)(2,1)} %copy-done.14, ...), kind=kOutput, calls=%fused_computation.59 | convolution fusion | flops 1086849024 | bytes 15736832 | tf_op jit(solution)/shard_map/bhts,bthn->bshn/dot_general | solution.py:398
  361.4 2.4 copy.145
  377.5 2.3 fusion.81
  379.8 5.9 add_convert_fusion.1
  388.5 3.0 fusion.29
  391.5 38.6 %all-reduce.1 = (f32[512]{0:T(512)}, f32[512]{0:T(512)}, f32[512]{0:T(512)}, f32[512]{0:T(512)}, f32[2048]{0:T(1024)}, /*index=5*/f32[512]{0:T(512)}, f32[8,64]{1,0:T(8,128)S(1)}) all-reduce(f32[512]{0:T(512)S(1)} %get-tuple-element.191, f32[512]{0:T(512)S(1)} %get-tuple-element.196, ...), channel_id=1, replica_groups=mesh['dp'=4,'seq'=8] {'dp','seq'}, use_global_device_ids=true, to_apply=%region_13.0 | all-reduce | flops 5120 | bytes 40960 | tf_op jit(solution)/shard_map/psum | solution.py:635
  430.8 3.1 fusion.28
  433.9 185.7 %all-reduce.5.cloned.1.call-done = (f32[512,512]{1,0:T(8,128)}, f32[512,512]{1,0:T(8,128)}, f32[512,512]{1,0:T(8,128)}, f32[512,512]{1,0:T(8,128)}, f32[512,512]...) async-done(((f32[512,512]{1,0:T(8,128)}, f32[512,512]{1,0:T(8,128)}, f32[512,512]{1,0:T(8,128)}, f32[512,512]{1,0:T(8,128)}, f32[512,512]{1,0:T(8,128)}, ...) | async-done | bytes 13631504 | tf_op jit(solution)/shard_map/psum | solution.py:635
  619.5 2.4 copy.200
  626.1 2.1 copy.205
  629.8 2.1 copy.206
  (210 shorter events, 51.7 us)
Async XLA Ops:
  7.2 104.9 %copy-start = (bf16[512,2048]{1,0:T(8,128)(2,1)S(1)}, bf16[512,2048]{1,0:T(8,128)(2,1)}, u32[]{:S(2)}) copy-start(bf16[512,2048]{1,0:T(8,128)(2,1)} %param.30) | copy-start | bytes 6291460
  7.2 299.1 %all-gather.3.cloned.1.call-start = ((), (), s32[]{:S(2)}) async-start(), calls=%async_computation | async-start | bytes 4718592 | tf_op jit(solution)/shard_map/all_gather | solution.py:385
  85.4 1.3 copy-start.4
  108.0 4.0 copy-start.51
  108.0 4.0 copy-start.53
  108.0 4.1 copy-start.58
  112.1 7.4 %copy-start.32 = (bf16[2,512,512]{2,1,0:T(8,128)(2,1)S(1)}, bf16[2,512,512]{2,1,0:T(8,128)(2,1)}, u32[]{:S(2)}) copy-start(bf16[2,512,512]{2,1,0:T(8,128)(2,1)} %param.35) | copy-start | bytes 3145732
  112.1 7.4 %copy-start.55 = (bf16[2048,512]{1,0:T(8,128)(2,1)S(1)}, bf16[2048,512]{1,0:T(8,128)(2,1)}, u32[]{:S(2)}) copy-start(bf16[2048,512]{1,0:T(8,128)(2,1)} %param.32) | copy-start | bytes 6291460
  119.5 8.0 %copy-start.5 = (f32[1024,512]{1,0:T(8,128)S(1)}, f32[1024,512]{1,0:T(8,128)}, u32[]{:S(2)}) copy-start(f32[1024,512]{1,0:T(8,128)} %copy-done.4) | copy-start | bytes 6291460
  127.5 3.0 copy-start.18
  131.6 156.9 %copy-start.8 = (f32[1024,512]{1,0:T(8,128)}, f32[1024,512]{1,0:T(8,128)S(1)}, u32[]{:S(2)}) copy-start(f32[1024,512]{1,0:T(8,128)S(1)} %multiply_add_fusion) | copy-start | bytes 6291460
  140.9 2.1 copy-start.16
  140.9 2.1 copy-start.49
  143.0 1.6 copy-start.12
  144.6 2.4 copy-start.20
  147.0 4.3 copy-start.2
  147.1 4.2 copy-start.37
  147.1 5.2 copy-start.38
  147.1 5.9 copy-start.39
  152.9 2.7 copy-start.13
  155.6 2.0 copy-start.61
  155.6 3.3 copy-start.60
  157.6 461.9 %all-reduce.5.cloned.1.call-start = ((), (), s32[]{:S(2)}) async-start(), calls=%async_computation.1 | async-start | bytes 27262976 | tf_op jit(solution)/shard_map/psum | solution.py:635
  209.8 3.9 copy-start.50
  213.6 1.8 copy-start.15
  213.6 1.9 copy-start.21
  215.5 2.5 copy-start.10
  218.0 3.2 copy-start.3
  223.5 64.9 %copy-start.34 = (bf16[1024,512]{1,0:T(8,128)(2,1)S(1)}, bf16[1024,512]{1,0:T(8,128)(2,1)}, u32[]{:S(2)}) copy-start(bf16[1024,512]{1,0:T(8,128)(2,1)} %get-tuple-element.172) | copy-start | bytes 3145732
  285.0 9.3 %slice-start = ((s8[8388608]{0:T(1024)(128)(4,1)}), s8[4194304]{0:T(1024)(128)(4,1)S(1)}, s32[]{:S(2)}) async-start(s8[8388608]{0:T(1024)(128)(4,1)} %bitcast.175), calls=%async_computation.2 | async-start | bytes 8388608
  288.5 1.7 copy-start.22
  290.2 4.1 slice-start.1
  292.3 2.0 copy-start.17
  294.3 3.0 copy-start.33
  294.3 3.0 copy-start.62
  297.3 4.4 copy-start.6
  297.3 4.4 copy-start.19
  339.8 6.8 %copy-start.11 = (f32[2,8,64,128]{3,2,1,0:T(8,128)S(1)}, f32[2,8,64,128]{3,2,1,0:T(8,128)}, u32[]{:S(2)}) copy-start(f32[2,8,64,128]{3,2,1,0:T(8,128)} %get-tuple-element.184) | copy-start | bytes 1572868
  339.8 6.8 %copy-start.23 = (bf16[2,512,8,64]{3,1,2,0:T(8,128)(2,1)S(1)}, bf16[2,512,8,64]{3,1,2,0:T(8,128)(2,1)}, u32[]{:S(2)}) copy-start(bf16[2,512,8,64]{3,1,2,0:T(8,128)(2,1)} %copy.143) | copy-start | bytes 3145732
  339.8 6.8 %copy-start.24 = (bf16[2,512,8,64]{3,1,2,0:T(8,128)(2,1)S(1)}, bf16[2,512,8,64]{3,1,2,0:T(8,128)(2,1)}, u32[]{:S(2)}) copy-start(bf16[2,512,8,64]{3,1,2,0:T(8,128)(2,1)} %copy.142) | copy-start | bytes 3145732
  361.4 3.6 copy-start.57
  364.0 2.7 copy-start.48
  368.1 2.8 copy-start.25
  368.1 1.7 copy-start.29
  371.2 1.7 copy-start.27
  372.9 1.2 copy-start.7
  377.5 2.3 copy-start.56
  377.5 2.3 copy-start.59
  379.8 6.0 copy-start.26
  379.8 6.0 copy-start.40
  385.8 1.2 copy-start.28
  385.8 1.4 copy-start.41
  387.1 1.2 copy-start.36
  387.1 1.4 copy-start.42
  387.2 1.4 copy-start.52
  388.5 41.6 %copy-start.54 = (f32[8,64]{1,0:T(8,128)S(1)}, f32[8,64]{1,0:T(8,128)}, u32[]{:S(2)}) copy-start(f32[8,64]{1,0:T(8,128)} %param.34) | copy-start | bytes 6148
  388.5 42.2 %copy-start.9 = (f32[1024,512]{1,0:T(8,128)S(1)}, f32[1024,512]{1,0:T(8,128)}, u32[]{:S(2)}) copy-start(f32[1024,512]{1,0:T(8,128)} %copy-done.8) | copy-start | bytes 6291460
  619.5 2.4 copy-start.47
  619.5 3.4 copy-start.46
  621.9 2.0 copy-start.45
  621.9 2.9 copy-start.44
  622.9 3.2 copy-start.31
  626.1 3.7 copy-start.30
  629.8 3.1 copy-start.1
  (3 other events, 3.0 us)
Sparse Core Ops, SparseCore 0:
  157.7 87.2 all-gather.2
  373.0 246.4 all-reduce.4

commit v3 on v2

v3 whole, which is shorter than its diff:
```python
import types

import jax
import jax.numpy as jnp
from jax import lax
from jax.experimental import pallas as pl
from jax.experimental.pallas import tpu as pltpu
from jax.sharding import PartitionSpec as P

HEADS = 8
HEAD = 64
SLOTS = 64
EPSILON = 1e-05
HUGE_VALUE = 1e30
MESH = pl.DeviceIdType.MESH
F32 = jnp.float32
BF16 = jnp.bfloat16
LANES = 128
HALF = 256
DP, SEQ = "dp", "seq"
CORE, LINE, NEAR, FAR = range(4)


def mm(left, right):
    return lax.dot_general(left, right, (((1,), (0,)), ((), ())), preferred_element_type=F32)


def mm_lanes(left, right):
    return lax.dot_general(left, right, (((1,), (1,)), ((), ())), preferred_element_type=F32)


def mm_rows(left, right):
    return lax.dot_general(left, right, (((0,), (0,)), ((), ())), preferred_element_type=F32)


def iota(shape, axis):
    return lax.broadcasted_iota(jnp.int32, shape, axis)


def first_head(shape):
    return iota(shape, len(shape) - 1) < HEAD


def only_head(values, head):
    keep = first_head(values.shape) if head == 0 else jnp.logical_not(first_head(values.shape))
    return jnp.where(keep, values, jnp.zeros_like(values))


def both_blocks(rows):
    doubled = jnp.concatenate([rows, rows], axis=0)
    inside = (iota(doubled.shape, 0) < HEAD) == first_head(doubled.shape)
    return jnp.where(inside, doubled, jnp.zeros_like(doubled))


def one_block(square):
    return jnp.where(first_head((HEAD, LANES)), square[:HEAD], square[HEAD:])


def lower(shape=(HALF, HALF)):
    return iota(shape, 0) >= iota(shape, 1)


def upper(shape=(HALF, HALF)):
    return iota(shape, 0) <= iota(shape, 1)


def head_reduce(values, operation, empty):
    here = first_head(values.shape)
    one = operation(jnp.where(here, values, empty), axis=1, keepdims=True)
    two = operation(jnp.where(here, empty, values), axis=1, keepdims=True)
    return jnp.where(here, one, two)


def parts_of(values):
    high = values.astype(BF16)
    return jnp.concatenate([high, (values - high.astype(F32)).astype(BF16)], axis=1)


def add_parts(product):
    return product[:, :LANES] + product[:, LANES:]


def normalized(values):
    centre = values - jnp.mean(values, axis=-1, keepdims=True)
    inverse = lax.rsqrt(jnp.mean(centre * centre, axis=-1, keepdims=True) + EPSILON)
    return centre * inverse, inverse


class Exchange:
    def __init__(self, size, sent, landed, send_sem, recv_sem):
        self.size, self.sent, self.landed = size, sent, landed
        self.send_sem, self.recv_sem = send_sem, recv_sem
        self.me = lax.axis_index(SEQ)

    def copy(self, source, target, to):
        return pltpu.make_async_remote_copy(
            src_ref=source,
            dst_ref=target,
            send_sem=self.send_sem,
            recv_sem=self.recv_sem,
            device_id={SEQ: to},
            device_id_type=MESH,
        )

    def send(self, to):
        @pl.when(to != self.me)
        def _():
            self.copy(self.sent.at[to], self.landed.at[self.me], to).start()

        @pl.when(to == self.me)
        def _():
            self.landed[self.me] = self.sent[self.me]

    def send_all(self):
        self.landed[self.me] = self.sent[self.me]
        for step in range(1, self.size):
            to = lax.rem(self.me + step, self.size)
            self.copy(self.sent.at[to], self.landed.at[self.me], to).start()

    def receive(self):
        others = self.landed.at[pl.ds(0, self.size - 1)]
        self.copy(others, others, lax.rem(self.me + 1, self.size)).wait_recv()

    def finish(self):
        others = self.sent.at[pl.ds(0, self.size - 1)]
        self.copy(others, others, lax.rem(self.me + 1, self.size)).wait_send()


class Reduction:
    def __init__(self, dp, seq, held, landed, full, send_sem, recv_sem, keep_sem):
        self.held, self.landed, self.full = held, landed, full
        self.send_sem, self.recv_sem, self.keep_sem = send_sem, recv_sem, keep_sem
        dp_at, seq_at = lax.axis_index(DP), lax.axis_index(SEQ)
        slow, fast = 4, seq // 4
        core, line = lax.rem(dp_at, 2), dp_at // 2
        near, far = lax.rem(seq_at, fast), seq_at // fast
        self.groups = {
            CORE: (2, core, lambda m: {DP: line * 2 + m}),
            LINE: (dp // 2, line, lambda m: {DP: m * 2 + core}),
            NEAR: (fast, near, lambda m: {SEQ: far * fast + m}),
            FAR: (slow, far, lambda m: {SEQ: m * fast + near}),
        }
        self.ways = dp // 2 * fast * slow

    def orders(self, rows, index):
        half = rows // 2
        ways = [(LINE, NEAR, FAR), (NEAR, LINE, FAR)]
        if half % (2 * self.ways * 8) == 0:
            return [(0, half // 2, ways[0]), (half // 2, half // 2, ways[1])]
        return [(0, half, ways[index % 2])]

    def steps(self, chunk, level):
        base, rows, land, index = chunk
        core = self.groups[CORE][1]
        if level == 0:
            return [(base, rows // 2, CORE, land)], rows // 2
        orders = self.orders(rows, index)
        place = land + rows // 2
        sizes = [size for _, size, _ in orders]
        starts = [base + core * (rows // 2) + offset for offset, _, _ in orders]
        for depth in range(level):
            found = []
            first = place
            for at, (_, _, axes) in enumerate(orders):
                name = axes[depth]
                count, mine, _ = self.groups[name]
                sizes[at] //= count
                found.append((starts[at], sizes[at], name, place))
                starts[at] = starts[at] + mine * sizes[at]
                place = place + sizes[at] * (count - 1)
        return found, sum(size * (self.groups[name][0] - 1) for _, size, name, _ in found)

    def rows_sent(self, chunk):
        return 2 * sum(self.steps(chunk, level)[1] for level in range(4))

    def copy(self, chunk, slot, source, target, device):
        return pltpu.make_async_remote_copy(
            src_ref=source,
            dst_ref=target,
            send_sem=self.send_sem.at[chunk[3]],
            recv_sem=self.recv_sem.at[chunk[3], slot],
            device_id=device,
            device_id_type=MESH,
        )

    def start(self, chunk, level, gather):
        for start, size, name, land in self.steps(chunk, level)[0]:
            count, at, device = self.groups[name]
            for k in range(1, count):
                to = lax.rem(at + k, count)
                if gather:
                    rows = pl.ds(pl.multiple_of(start + at * size, 8), size)
                    source = (self.held if level == 3 else self.full).at[rows]
                    target = self.full.at[rows]
                else:
                    source = self.held.at[pl.ds(pl.multiple_of(start + to * size, 8), size)]
                    target = self.landed.at[pl.ds(pl.multiple_of(land + (k - 1) * size, 8), size)]
                self.copy(chunk, level + 4 * gather, source, target, device(to)).start()
            if gather and level == 3:
                rows = pl.ds(pl.multiple_of(start + at * size, 8), size)
                pltpu.make_async_copy(
                    self.held.at[rows], self.full.at[rows], self.keep_sem.at[chunk[3]]
                ).start()

    def wait(self, chunk, level, gather):
        steps, rows = self.steps(chunk, level)
        at = pl.ds(chunk[0], rows) if gather else pl.ds(steps[0][3], rows)
        ref = (self.full if gather else self.landed).at[at]
        self.copy(chunk, level + 4 * gather, ref, ref, self.groups[CORE][2](0)).wait_recv()
        if gather and level == 3:
            at = pl.ds(chunk[0], sum(size for _, size, _, _ in steps))
            pltpu.make_async_copy(
                self.held.at[at], self.full.at[at], self.keep_sem.at[chunk[3]]
            ).wait()

    def finish(self, chunk):
        ref = self.held.at[pl.ds(0, self.rows_sent(chunk))]
        self.copy(chunk, 0, ref, ref, self.groups[CORE][2](0)).wait_send()

    def add(self, chunk, level):
        for start, size, name, land in self.steps(chunk, level)[0]:
            count, at, _ = self.groups[name]
            block = min(size, 512)

            def one(step, unused, start=start, size=size, land=land, at=at, count=count, block=block):
                rows = pl.ds(pl.multiple_of(start + at * size + step * block, 8), block)
                total = self.held[rows]
                for k in range(1, count):
                    found = pl.ds(pl.multiple_of(land + (k - 1) * size + step * block, 8), block)
                    total = total + self.landed[found]
                self.held[rows] = total
                return unused

            if size == block:
                one(0, 0)
            else:
                lax.fori_loop(0, size // block, one, 0)

    def stage(self, chunk, number):
        if number:
            level, gather = (number - 1, False) if number <= 4 else (8 - number, True)
            self.wait(chunk, level, gather)
            if not gather:
                self.add(chunk, level)
        if number < 8:
            self.start(chunk, *((number, False) if number < 4 else (7 - number, True)))


def timetable(costs, begins):
    line = {0: (0, 0.9), 1: (1, 2.9), 2: (1, 1.5), 3: (2, 2.9)}
    now, free, ready, following = 0.0, [0.0] * 3, {}, {}
    table = [[] for _ in costs] + [[]]

    def take(chunk, number, place):
        nonlocal now
        now += EVENT
        place.append((chunk, number))
        following[chunk] = number + 1
        if number == 8:
            del following[chunk], ready[chunk]
            return
        link, cost = line[min(number, 7 - number)]
        free[link] = max(now, free[link]) + (cost if chunk < 13 else cost / 4)
        ready[chunk] = free[link] + LATENCY

    for moment, cost in enumerate(costs):
        now += cost
        for chunk, begin in enumerate(begins):
            if begin == moment:
                take(chunk, 0, table[moment])
        while True:
            able = [chunk for chunk in following if ready[chunk] <= now]
            if not able:
                break
            take(min(able), following[min(able)], table[moment])
    while following:
        chunk = min(following, key=lambda at: (ready[at], at))
        now = max(now, ready[chunk])
        take(chunk, following[chunk], table[-1])
    return table


def block_of(combo):
    stream, pair = combo // 4, lax.rem(combo, 4)
    return (
        pl.multiple_of(stream * 512, 512),
        pl.multiple_of(pair * LANES, LANES),
    )


def gelu_parts(raised):
    root = 0.7978845608028654
    square = raised * raised
    bent = jnp.tanh(root * raised * (1.0 + 0.044715 * square))
    half = 0.5 * (1.0 + bent)
    slope = half + (0.5 * root) * raised * (1.0 - bent * bent) * (1.0 + 0.134145 * square)
    return raised * half, slope


def norm_pull(upstream, scaled, inverse, gain):
    inside = upstream * gain
    first = jnp.mean(inside, axis=-1, keepdims=True)
    second = jnp.mean(inside * scaled, axis=-1, keepdims=True)
    return inverse * (inside - first - scaled * second)


def column_sum(values):
    return jnp.sum(values, axis=0, keepdims=True)


LOADS = 8
ATTN_GAIN, ATTN_SHIFT, FFN_GAIN, FFN_SHIFT, DOWN_BIAS, WRITES, UP_BIAS = range(0, 28, 4)
CHUNK = 2048
EVENT = 0.2
LATENCY = 3.0
COSTS = [0.85] * 24 + [0.5] * 4 + [0.8, 1.0] + [1.7, 1.7, 1.2, 1.2, 0.4, 0.1] * 3
COSTS += [1.7, 1.7, 1.2, 1.2, 1.6, 0.1, 1.7, 1.7, 1.2, 1.2, 0.4, 0.1] * 2
COSTS += [1.7, 1.7, 1.2, 1.2, 1.6, 0.1] + [0.0, 1.0, 0.0, 1.6] + [1.0] * 4 + [0.3]
BEGINS = [4, 5, 10, 11, 16, 17, 22, 23, 28, 52, 64, 76, 81, 86]
TABLE = timetable(COSTS, BEGINS)


class Sizes:
    def __init__(self, dp, seq):
        self.dp, self.seq = dp, seq
        self.groups = seq // 8
        self.part = LANES // self.groups
        self.tiny = max(512, dp // 2 * seq * 16)
        self.rows = 13 * CHUNK + self.tiny
        self.landing = 9 * CHUNK

    def chunk(self, index):
        land = index - 9 * (index >= 9) if isinstance(index, int) else jnp.where(index >= 9, index - 9, index)
        return (index * CHUNK, CHUNK, land * CHUNK, index)

    def last(self):
        return (13 * CHUNK, self.tiny, 4 * CHUNK, 13)


def layer_kernel(sizes, refs):
    r = refs
    seq, groups, part = sizes.seq, sizes.groups, sizes.part
    dp_at, me = lax.axis_index(DP), lax.axis_index(SEQ)

    sources = (r.in_tokens, r.in_wc, r.in_wk, r.in_wv, r.in_wq, r.in_wo, r.in_down, r.in_pull)
    targets = (r.tokens, r.wc, r.wk, r.wv, r.wq, r.wo, r.down, r.pull)
    loads = [
        pltpu.make_async_copy(source, target, r.load_sem.at[at])
        for at, (source, target) in enumerate(zip(sources, targets))
    ]
    for copy in loads:
        copy.start()
    early_loads, load_wq, load_wo, load_down, load_pull = loads[:4], *loads[4:]
    up_loads = [
        pltpu.make_async_copy(
            r.in_up.at[:, pl.ds(512 * at, 512)], r.up.at[at], r.up_sem.at[at]
        )
        for at in range(4)
    ]
    for copy in up_loads:
        copy.start()

    barrier = pltpu.get_barrier_semaphore()
    count = 0
    for step in range(1, seq):
        pl.semaphore_signal(
            barrier, inc=1, device_id={SEQ: lax.rem(me + step, seq)}, device_id_type=MESH
        )
        count += 1
    core, line = lax.rem(dp_at, 2), dp_at // 2
    pl.semaphore_signal(
        barrier, inc=1, device_id={DP: line * 2 + 1 - core}, device_id_type=MESH
    )
    count += 1
    for step in range(1, sizes.dp // 2):
        other = lax.rem(line + step, sizes.dp // 2) * 2 + core
        pl.semaphore_signal(barrier, inc=1, device_id={DP: other}, device_id_type=MESH)
        count += 1

    tokens, normed, queries, keys, values = (
        r.tokens, r.normed, r.queries, r.keys, r.values
    )
    local, weights, sums, logits, chances, shares, mixed = (
        r.local, r.weights, r.sums, r.logits, r.chances, r.shares, r.mixed
    )
    notes, prior, hidden, held, small = r.notes, r.prior, r.hidden, r.held, r.small
    there = Exchange(seq, r.box0, r.box1, r.box_sem.at[0], r.box_sem.at[1])
    back = Exchange(seq, r.box2, r.box3, r.box_sem.at[2], r.box_sem.at[3])
    theres = [
        Exchange(seq, r.box4.at[at], r.box5.at[at], r.pair_sem.at[0, at], r.pair_sem.at[1, at])
        for at in range(4)
    ]
    backs = [
        Exchange(seq, r.box6.at[at], r.box7.at[at], r.pair_sem.at[2, at], r.pair_sem.at[3, at])
        for at in range(4)
    ]
    reduction = Reduction(
        sizes.dp, seq, held, r.landed, r.out_full, r.reduce_send, r.reduce_recv, r.keep_sem
    )

    def chunk_of(index):
        return sizes.last() if index == 13 else sizes.chunk(index)

    def events(moment):
        for index, number in TABLE[moment]:
            reduction.stage(chunk_of(index), number)

    def events_in(moments, *at):
        for indices, moment in moments.items():
            if TABLE[moment]:
                here = at[0] == indices[0]
                for index, value in zip(at[1:], indices[1:]):
                    here = here & (index == value)
                pl.when(here)(lambda moment=moment: events(moment))

    def put_small(at, values):
        for column in range(values.shape[1] // LANES):
            row = pl.ds(at + column, 1)
            small[row, :] = small[row, :] + values[:, column * LANES : (column + 1) * LANES]

    small[...] = jnp.zeros_like(small)

    for copy in early_loads:
        copy.wait()

    def project(step, unused):
        rows = pl.ds(pl.multiple_of(step * HALF, HALF), HALF)
        scaled, _ = normalized(tokens[rows, :].astype(F32))
        low = (scaled * r.attn_gain[...] + r.attn_shift[...]).astype(BF16)
        normed[rows, :] = low
        local[rows, :] = mm(low, r.wc[...])
        keys[rows, :] = mm(low, r.wk[...]).astype(BF16)
        values[rows, :] = mm(low, r.wv[...]).astype(BF16)
        return unused

    def summarize(combo, unused):
        row, col = block_of(combo)
        rows, cols = pl.ds(row, 512), pl.ds(col, LANES)
        control = local[rows, cols]
        block_max = jnp.floor(jnp.max(control, axis=0, keepdims=True))
        spread = jnp.exp(control - block_max)
        local[rows, cols] = spread
        pair_rows = jnp.concatenate([keys[rows, cols], values[rows, cols]], axis=1)
        memory = add_parts(mm_rows(pair_rows, parts_of(spread)))
        memory = jnp.concatenate([one_block(memory[:LANES]), one_block(memory[LANES:])], axis=0)
        total = column_sum(spread)
        flag = jnp.broadcast_to(r.starts[pl.ds(combo // 4, 1), :].astype(F32), (1, LANES))
        line = iota((8, LANES), 0)
        notes[combo] = jnp.where(line == 0, block_max, jnp.where(line == 1, total, flag))
        for group in range(groups):
            to = combo * groups + group
            there.sent[to, :part] = memory[group * part : (group + 1) * part]
            there.sent[to, part:] = notes[combo]
            there.send(to)
        return unused

    for stream in range(2):
        lax.fori_loop(2 * stream, 2 * stream + 2, project, 0)
        if stream == 0:
            pl.semaphore_wait(barrier, count)
        lax.fori_loop(4 * stream, 4 * stream + 4, summarize, 0)

    load_wq.wait()

    def project_query(step, unused):
        rows = pl.ds(pl.multiple_of(step * HALF, HALF), HALF)
        queries[rows, :] = mm(normed[rows, :], r.wq[...]).astype(BF16)
        return unused

    lax.fori_loop(0, 4, project_query, 0)

    def inside(combo, unused):
        row, col = block_of(combo)
        cols = pl.ds(col, LANES)
        spread = local[pl.ds(row, 512), cols]
        low = spread.astype(BF16)
        triangle = lower()
        ones = jnp.where(triangle, 1.0, 0.0).astype(BF16)
        first = add_parts(mm(ones, parts_of(spread[:HALF])))
        second = add_parts(mm(ones, parts_of(spread[HALF:]))) + first[HALF - 1 :]
        sums[pl.ds(row, HALF), cols] = first
        sums[pl.ds(row + HALF, HALF), cols] = second
        for at in range(2):
            rows = pl.ds(row + at * HALF, HALF)
            width = (at + 1) * HALF
            total = None
            for head in range(2):
                query = only_head(queries[rows, cols], head)
                found = []
                for other in range(at + 1):
                    score = mm_lanes(query, keys[pl.ds(row + other * HALF, HALF), cols])
                    if other == at:
                        score = jnp.where(triangle, score, 0.0)
                    found.append(score.astype(BF16))
                score = found[0] if at == 0 else jnp.concatenate(found, axis=1)
                term = mm(score, only_head(low[:width], head))
                total = term if total is None else total + term
            logits[rows, cols] = total
        return unused

    lax.fori_loop(0, 4, inside, 0)

    prior_max = jnp.full((1, LANES), -HUGE_VALUE, F32)
    raw_total = jnp.zeros((1, LANES), F32)
    raw_memory = jnp.zeros((part, LANES), F32)
    line = iota((8, LANES), 0)
    there.receive()
    for source in range(seq):
        back.sent[source, :part] = raw_memory
        back.sent[source, part:] = jnp.where(line == 0, prior_max, raw_total)
        back.send(source)
        if source < seq - 1:
            block_max = there.landed[source, part : part + 1]
            total = there.landed[source, part + 1 : part + 2]
            flag = there.landed[source, part + 2 : part + 3]
            ceiling = jnp.maximum(prior_max, block_max)
            old = (1.0 - flag) * jnp.exp(prior_max - ceiling)
            new = jnp.exp(block_max - ceiling)
            raw_total = old * raw_total + new * total
            raw_memory = old * raw_memory + new * there.landed[source, :part]
            prior_max = ceiling

    lax.fori_loop(4, 8, inside, 0)

    def returned(exchange, combo):
        pieces = [exchange.landed[combo * groups + group, :part] for group in range(groups)]
        memory = pieces[0] if groups == 1 else jnp.concatenate(pieces, axis=0)
        first = combo * groups
        return (
            memory,
            exchange.landed[first, part : part + 1],
            exchange.landed[first, part + 1 : part + 2],
        )

    def attend(combo, unused):
        row, col = block_of(combo)
        cols = pl.ds(col, LANES)
        memory, past_max, past_total = returned(back, combo)
        block_max = notes[combo, 0:1]
        flag = notes[combo, 2:3]
        ceiling = jnp.maximum(past_max, block_max)
        carried = (1.0 - flag) * jnp.exp(past_max - ceiling)
        factor = jnp.exp(block_max - ceiling)
        notes[combo, 1:2] = ceiling
        notes[combo, 3:4] = factor
        memory = (carried * memory).astype(BF16)
        prior[combo] = memory
        prior_keys = both_blocks(memory[:HEAD])
        prior_values = both_blocks(memory[HEAD:])
        triangle = lower()
        written = jnp.zeros((1, LANES), F32)
        for at in range(2):
            rows = pl.ds(row + at * HALF, HALF)
            weight = local[rows, cols] * factor
            weights[rows, cols] = weight.astype(BF16)
            inverse = 1.0 / (carried * past_total + factor * sums[rows, cols])
            sums[rows, cols] = inverse
            written = written + column_sum(weight * inverse)
            logit = (mm(queries[rows, cols], prior_keys) + factor * logits[rows, cols]) * inverse
            logits[rows, cols] = logit
            top = head_reduce(logit, jnp.max, -HUGE_VALUE)
            raised = jnp.exp(logit - top)
            chance = raised / head_reduce(raised, jnp.sum, 0.0)
            chances[rows, cols] = chance
            share = (chance * inverse).astype(BF16)
            shares[rows, cols] = share
            attended = mm_lanes(share, prior_values)
            for head in range(2):
                own = only_head(share, head)
                for other in range(at + 1):
                    these = pl.ds(row + other * HALF, HALF)
                    mixing = mm_lanes(own, weights[these, cols])
                    if other == at:
                        mixing = jnp.where(triangle, mixing, 0.0)
                    attended = attended + mm(
                        mixing.astype(BF16), only_head(values[these, cols], head)
                    )
            mixed[rows, cols] = attended.astype(BF16)
        place = pl.ds(WRITES + lax.rem(combo, 4), 1)
        small[place, :] = small[place, :] + written
        return unused

    back.receive()
    lax.fori_loop(0, 8, attend, 0)

    load_wo.wait()
    load_pull.wait()
    pull, branch, turned = r.pull, r.branch, r.turned

    def project_out(step, unused):
        rows = pl.ds(pl.multiple_of(step * HALF, HALF), HALF)
        wide = tokens[rows, :].astype(F32) + mm(mixed[rows, :], r.wo[...])
        hidden[rows, :] = wide
        scaled, _ = normalized(wide)
        low = (scaled * r.ffn_gain[...] + r.ffn_shift[...]).astype(BF16)
        branch[rows, :] = low
        turned[:, rows] = low.T
        put_small(DOWN_BIAS, column_sum(pull[rows, :].astype(F32)))
        return unused

    lax.fori_loop(0, 4, project_out, 0)

    load_down.wait()
    for copy in up_loads:
        copy.wait()
    up, down, active, pushed = r.up, r.down, r.active, r.pushed
    after = 9 * CHUNK

    def running(base, rows_at, values, first):
        for column in range(4):
            place = pl.ds(pl.multiple_of(base + column * 1024 + rows_at, 8), HALF)
            block = values[:, column * LANES : (column + 1) * LANES]
            held[place] = jnp.where(first, block, held[place] + block)

    def collected(base, rows_at):
        return jnp.concatenate(
            [
                held[pl.ds(pl.multiple_of(base + column * 1024 + rows_at, 8), HALF)]
                for column in range(4)
            ],
            axis=1,
        )

    def store_block(base, square, rows_at):
        for column in range(square.shape[1] // LANES):
            place = pl.ds(pl.multiple_of(base + column * 512 + rows_at, 8), square.shape[0])
            held[place] = square[:, column * LANES : (column + 1) * LANES]

    def feed_forward(part_at, unused):
        base = part_at * 2 * CHUNK

        def rows_of(step, unused):
            rows_at = pl.multiple_of(step * HALF, HALF)
            rows = pl.ds(rows_at, HALF)
            raised = mm(branch[rows, :], up[part_at]) + r.up_bias[:, pl.ds(pl.multiple_of(part_at * 512, 512), 512)]
            value, slope = gelu_parts(raised)
            low = value.astype(BF16)
            active[rows, :] = low
            along = pl.ds(pl.multiple_of(part_at * 512, 512), 512)
            grad = (mm_lanes(pull[rows, :], down[along, :]) * slope).astype(BF16)
            pushed[rows, :] = grad
            running(after, rows_at, mm(low, down[along, :]), part_at == 0)
            running(after + 4096, rows_at, mm_lanes(grad, up[part_at]), part_at == 0)
            total = column_sum(grad.astype(F32))
            for column in range(4):
                place = pl.ds(UP_BIAS + part_at * 4 + column, 1)
                small[place, :] = small[place, :] + total[:, column * LANES : (column + 1) * LANES]
            events_in(
                {(p, q): 6 * p + q for p in range(4) for q in range(4)}, part_at, step
            )
            return unused

        lax.fori_loop(0, 4, rows_of, 0)
        for block in range(2):
            wide = mm_rows(active[:, block * HALF : (block + 1) * HALF], pull[...])
            store_block(base, wide, block * HALF)
        events_in({(p,): 6 * p + 4 for p in range(4)}, part_at)
        for block in range(2):
            wide = mm(turned[block * HALF : (block + 1) * HALF, :], pushed[...])
            store_block(base + CHUNK, wide, block * HALF)
        events_in({(p,): 6 * p + 5 for p in range(4)}, part_at)
        return unused

    lax.fori_loop(0, 4, feed_forward, 0)

    def finish_rows(step, unused):
        rows_at = pl.multiple_of(step * HALF, HALF)
        rows = pl.ds(rows_at, HALF)
        wide = hidden[rows, :]
        r.result[rows, :] = (wide + collected(after, rows_at) + r.down_bias[...]).astype(BF16)
        scaled, inverse = normalized(wide)
        upstream = collected(after + 4096, rows_at)
        put_small(FFN_GAIN, column_sum(upstream * scaled))
        put_small(FFN_SHIFT, column_sum(upstream))
        grad = pull[rows, :].astype(F32) + norm_pull(upstream, scaled, inverse, r.ffn_gain[...])
        hidden[rows, :] = grad
        branch[rows, :] = grad.astype(BF16)
        events_in({(q,): 24 + q for q in range(4)}, step)
        return unused

    lax.fori_loop(0, 4, finish_rows, 0)
    result_copy = pltpu.make_async_copy(r.result, r.out_result, r.load_sem.at[LOADS])
    result_copy.start()
    for block in range(2):
        wide = mm_rows(mixed[:, block * HALF : (block + 1) * HALF], branch[...])
        store_block(8 * CHUNK, wide, block * HALF)
    events(28)

    def into_attention(step, unused):
        rows = pl.ds(pl.multiple_of(step * HALF, HALF), HALF)
        mixed[rows, :] = mm_lanes(branch[rows, :], r.wo[...]).astype(BF16)
        turned[:, rows] = normed[rows, :].T
        return unused

    lax.fori_loop(0, 4, into_attention, 0)
    events(29)

    late, outgoing = 256 // seq, r.box4
    pulled, near_grad, total_grad, query_low = mixed, r.near_grad, r.total_grad, active

    def backward(combo, step):
        row, col = block_of(combo)
        cols = pl.ds(col, LANES)
        memory = prior[combo]
        prior_keys = both_blocks(memory[:HEAD])
        prior_values = both_blocks(memory[HEAD:])
        triangle = lower()
        early = upper()
        all_rows = [pl.ds(row, HALF), pl.ds(row + HALF, HALF)]
        for at in range(2):
            rows = all_rows[at]
            pulls = pulled[rows, cols]
            share_grad = mm(pulls, prior_values)
            for head in range(2):
                own = only_head(pulls, head)
                for other in range(at + 1):
                    these = all_rows[other]
                    grad = mm_lanes(own, values[these, cols])
                    if other == at:
                        grad = jnp.where(triangle, grad, 0.0)
                    share_grad = share_grad + mm(
                        grad.astype(BF16), only_head(weights[these, cols], head)
                    )
            inverse, chance = sums[rows, cols], chances[rows, cols]
            chance_grad = share_grad * inverse
            middle = head_reduce(chance * chance_grad, jnp.sum, 0.0)
            logit_grad = chance * (chance_grad - middle)
            number_grad = logit_grad * inverse
            total_grad[pl.ds(at * HALF, HALF), :] = -(
                chance_grad * chance * inverse + number_grad * logits[rows, cols]
            )
            low = number_grad.astype(BF16)
            near_grad[pl.ds(at * HALF, HALF), :] = low
            query_grad = mm_lanes(low, prior_keys)
            for head in range(2):
                own = only_head(low, head)
                for other in range(at + 1):
                    these = all_rows[other]
                    grad = mm_lanes(own, weights[these, cols])
                    if other == at:
                        grad = jnp.where(triangle, grad, 0.0)
                    query_grad = query_grad + mm(
                        grad.astype(BF16), only_head(keys[these, cols], head)
                    )
            query_low[rows, cols] = query_grad.astype(BF16)
            events_in({(q,): 30 + 6 * q + at for q in range(8)}, step)
        ones = jnp.where(early, 1.0, 0.0).astype(BF16)
        late_sum = add_parts(mm(ones, parts_of(total_grad[HALF:, :])))
        early_sum = add_parts(mm(ones, parts_of(total_grad[:HALF, :]))) + late_sum[:1]
        prior_total_grad = early_sum[:1]
        for at in range(2):
            rows = all_rows[at]
            weight_grad = early_sum if at == 0 else late_sum
            key_grad = value_grad = None
            for head in range(2):
                own_value = only_head(values[rows, cols], head)
                own_weight = only_head(weights[rows, cols], head)
                own_key = only_head(keys[rows, cols], head)
                for other in range(at, 2):
                    these = all_rows[other]
                    near = near_grad[pl.ds(other * HALF, HALF), :]

                    def masked(square, other=other):
                        if other == at:
                            square = jnp.where(early, square, 0.0)
                        return square.astype(BF16)

                    pulls = pulled[these, cols]
                    share = shares[these, cols]
                    query = queries[these, cols]
                    weight_grad = weight_grad + mm(
                        masked(mm_lanes(own_value, pulls)), only_head(share, head)
                    )
                    weight_grad = weight_grad + mm(
                        masked(mm_lanes(own_key, query)), only_head(near, head)
                    )
                    term = mm(masked(mm_lanes(own_weight, share)), only_head(pulls, head))
                    value_grad = term if value_grad is None else value_grad + term
                    term = mm(masked(mm_lanes(own_weight, near)), only_head(query, head))
                    key_grad = term if key_grad is None else key_grad + term
            sums[rows, cols] = weight_grad * (local[rows, cols] * notes[combo, 3:4])
            logits[rows, cols] = key_grad
            chances[rows, cols] = value_grad
            if at == 0:
                events_in({(q,): 32 + 6 * q for q in range(8)}, step)
        whole = pl.ds(row, 512)
        key_memory = mm_rows(queries[whole, cols], near_grad[...])
        value_memory = mm_rows(pulled[whole, cols], shares[whole, cols])
        keep = 1.0 - notes[combo, 2:3]
        memory = keep * jnp.concatenate([one_block(key_memory), one_block(value_memory)], axis=0)
        line = iota((8, LANES), 0)
        extra = jnp.where(
            line == 0,
            notes[combo, 1:2],
            jnp.where(line == 1, keep * prior_total_grad, notes[combo, 2:3]),
        )
        stream = combo // 4
        for group in range(seq // 2):
            to = stream * (seq // 2) + group
            outgoing[step // 2, to, :late] = memory[group * late : (group + 1) * late]
            outgoing[step // 2, to, late:] = extra

    def handle(pair):
        arrived, answers = theres[pair], backs[pair]
        arrived.receive()
        floor = jnp.full((1, LANES), HUGE_VALUE, F32)
        total = jnp.zeros((1, LANES), F32)
        memory = jnp.zeros((late, LANES), F32)
        line = iota((8, LANES), 0)
        for source in reversed(range(seq)):
            answers.sent[source, :late] = memory
            answers.sent[source, late:] = jnp.where(line == 0, floor, total)
            if source > 0:
                ceiling = arrived.landed[source, late : late + 1]
                flag = arrived.landed[source, late + 2 : late + 3]
                lowest = jnp.minimum(floor, ceiling)
                near = jnp.exp(lowest - ceiling)
                far = (1.0 - flag) * jnp.exp(lowest - floor)
                total = near * arrived.landed[source, late + 1 : late + 2] + far * total
                memory = near * arrived.landed[source, :late] + far * memory
                floor = lowest
        answers.send_all()

    def for_pair(pair, act):
        for at in range(4):
            pl.when(pair == at)(lambda at=at: act(at))

    def finalize(pair):
        if isinstance(pair, int):
            backs[pair].receive()
        else:
            for_pair(pair, lambda at: backs[at].receive())

        def one(stream, unused):
            combo = stream * 4 + pair
            row, col = block_of(combo)
            cols = pl.ds(col, LANES)
            first = stream * (seq // 2)
            memory = jnp.concatenate(
                [r.box7[pair, first + group, :late] for group in range(seq // 2)], axis=0
            )
            floor = r.box7[pair, first, late : late + 1]
            total = r.box7[pair, first, late + 1 : late + 2]
            reach = jnp.exp(notes[combo, 0:1] - floor)
            total = reach * total
            memory = (reach * memory).astype(BF16)
            key_memory, value_memory = both_blocks(memory[:HEAD]), both_blocks(memory[HEAD:])
            for at in range(2):
                rows = pl.ds(row + at * HALF, HALF)
                spread = local[rows, cols]
                low = spread.astype(BF16)
                inner = mm(keys[rows, cols], key_memory) + mm(values[rows, cols], value_memory)
                weights[rows, cols] = (sums[rows, cols] + spread * (inner + total)).astype(BF16)
                key_grad = logits[rows, cols] + mm_lanes(low, key_memory)
                value_grad = chances[rows, cols] + mm_lanes(low, value_memory)
                keys[rows, cols] = key_grad.astype(BF16)
                values[rows, cols] = value_grad.astype(BF16)
            return unused

        lax.fori_loop(0, 2, one, 0)
        cols = pl.ds(pl.multiple_of(pair * LANES, LANES), LANES)
        base = (9 + pair) * CHUNK
        for at, (left, right) in enumerate(((query_low, keys), (values, weights))):
            both = jnp.concatenate([left[:, cols], right[:, cols]], axis=1)
            for block in range(2):
                wide = mm(turned[block * HALF : (block + 1) * HALF, :], both)
                store_block(base + at * 1024, wide, block * HALF)

    def iteration(step, unused):
        backward((lax.rem(step, 2)) * 4 + step // 2, step)
        events_in({(q,): 33 + 6 * q for q in range(8)}, step)

        @pl.when(lax.rem(step, 2) == 1)
        def _():
            for_pair(step // 2, lambda at: theres[at].send_all())

        @pl.when((step >= 2) & (lax.rem(step, 2) == 0))
        def _():
            for_pair(step // 2 - 1, handle)

        @pl.when((step >= 3) & (lax.rem(step, 2) == 1))
        def _():
            finalize((step - 3) // 2)

        events_in({(q,): 34 + 6 * q for q in range(8)}, step)
        events_in({(q,): 35 + 6 * q for q in range(8)}, step)
        return unused

    lax.fori_loop(0, 8, iteration, 0)
    events(78)

    handle(3)
    events(79)
    events(80)
    finalize(3)
    events(81)

    def input_rows(step, unused):
        rows = pl.ds(pl.multiple_of(step * HALF, HALF), HALF)
        upstream = mm_lanes(query_low[rows, :], r.wq[...])
        upstream = upstream + mm_lanes(keys[rows, :], r.wk[...])
        upstream = upstream + mm_lanes(values[rows, :], r.wv[...])
        upstream = upstream + mm_lanes(weights[rows, :], r.wc[...])
        scaled, inverse = normalized(tokens[rows, :].astype(F32))
        put_small(ATTN_GAIN, column_sum(upstream * scaled))
        put_small(ATTN_SHIFT, column_sum(upstream))
        hidden[rows, :] = hidden[rows, :] + norm_pull(
            upstream, scaled, inverse, r.attn_gain[...]
        )
        events_in({(q,): 82 + q for q in range(4)}, step)
        return unused

    lax.fori_loop(0, 4, input_rows, 0)
    grad_copy = pltpu.make_async_copy(
        hidden, r.out_input_grad, r.load_sem.at[LOADS + 1]
    )
    grad_copy.start()
    last = sizes.last()
    held[pl.ds(last[0], last[1])] = jnp.zeros((last[1], LANES), F32)
    held[pl.ds(last[0], small.shape[0])] = small[...]
    events(86)
    events(87)
    for copy in (result_copy, grad_copy):
        copy.wait()
    for exchange in (there, back, *theres, *backs):
        exchange.finish()
    for index in range(14):
        reduction.finish(chunk_of(index))


def deliver_kernel(full, result, input_grad, slot_means, count, *outs):
    (
        out_result, out_input_grad, attn_gain, attn_shift, wq, wk, wv, wc, wo,
        ffn_gain, ffn_shift, up, up_bias, down, down_bias, means, held, held_result, held_grad, in_sem, out_sem,
    ) = outs
    loads = [
        pltpu.make_async_copy(full.at[rows], held.at[rows], in_sem.at[at])
        for at, rows in enumerate(
            [pl.ds(13 * CHUNK, 40)] + [pl.ds(at * CHUNK, CHUNK) for at in range(13)]
        )
    ]
    loads.append(pltpu.make_async_copy(result, held_result, in_sem.at[14]))
    loads.append(pltpu.make_async_copy(input_grad, held_grad, in_sem.at[15]))
    for copy in loads:
        copy.start()
    stores = []

    def store(source, target):
        copy = pltpu.make_async_copy(source, target, out_sem.at[len(stores)])
        copy.start()
        stores.append(copy)

    for index in range(13):
        loads[1 + index].wait()
        for column in range(4):
            lanes = pl.ds(column * LANES, LANES)
            source = held.at[pl.ds(index * CHUNK + column * 512, 512)]
            if index == 8:
                store(source, wo.at[:, lanes])
            elif index > 8:
                store(source, (wq, wk, wv, wc)[column].at[:, pl.ds((index - 9) * LANES, LANES)])
            elif index % 2:
                store(source, up.at[:, pl.ds(index // 2 * 512 + column * LANES, LANES)])
            else:
                store(source, down.at[pl.ds(index // 2 * 512, 512), lanes])
    loads[14].wait()
    store(held_result, out_result)
    loads[15].wait()
    store(held_grad, out_input_grad)
    loads[0].wait()
    small = held.at[pl.ds(13 * CHUNK, 40)]
    for at, target in (
        (ATTN_GAIN, attn_gain),
        (ATTN_SHIFT, attn_shift),
        (FFN_GAIN, ffn_gain),
        (FFN_SHIFT, ffn_shift),
        (DOWN_BIAS, down_bias),
        (UP_BIAS, up_bias),
    ):
        for column in range(target.shape[1] // LANES):
            row = pl.ds(at + column, 1)
            target[:, column * LANES : (column + 1) * LANES] = small[row, :]
    for pair in range(4):
        row = small[pl.ds(WRITES + pair, 1), :]
        for head in range(2):
            line = pl.ds(2 * pair + head, 1)
            written = row[:, head * SLOTS : (head + 1) * SLOTS]
            means[line, :] = 0.9 * slot_means[line, :] + 0.1 * written / count
    for copy in stores:
        copy.wait()


def deliver_call(count, full, result, input_grad, slot_means):
    square = jax.ShapeDtypeStruct((512, 512), F32)
    vector = jax.ShapeDtypeStruct((1, 512), F32)
    long = jax.ShapeDtypeStruct((1, 2048), F32)
    shapes = [result, input_grad, vector, vector, square, square, square, square, square]
    shapes += [vector, vector, jax.ShapeDtypeStruct((512, 2048), F32), long]
    shapes += [jax.ShapeDtypeStruct((2048, 512), F32), vector, slot_means]
    anywhere = pl.BlockSpec(memory_space=pl.ANY)
    near = pl.BlockSpec(memory_space=pltpu.VMEM)

    def kernel(full, result, input_grad, slot_means, *outs):
        deliver_kernel(full, result, input_grad, slot_means, count, *outs)

    return pl.pallas_call(
        kernel,
        out_shape=[jax.ShapeDtypeStruct(shape.shape, shape.dtype) for shape in shapes],
        in_specs=[anywhere, anywhere, anywhere, near],
        out_specs=[near if shape is vector or shape is long or shape is slot_means else anywhere for shape in shapes],
        scratch_shapes=[
            pltpu.VMEM((13 * CHUNK + 40, LANES), F32),
            pltpu.VMEM(result.shape, BF16),
            pltpu.VMEM(input_grad.shape, F32),
            pltpu.SemaphoreType.DMA((16,)),
            pltpu.SemaphoreType.DMA((54,)),
        ],
        compiler_params=pltpu.CompilerParams(vmem_limit_bytes=60 * 2**20),
        name="deliver",
    )(full, result, input_grad, slot_means)


def layer_call(sizes, **arrays):
    rows, width, hidden = 1024, 512, 2048
    outputs = dict(
        out_result=jax.ShapeDtypeStruct((rows, width), BF16),
        out_input_grad=jax.ShapeDtypeStruct((rows, width), F32),
        out_full=jax.ShapeDtypeStruct((sizes.rows, LANES), F32),
    )
    low, wide = pltpu.VMEM((rows, width), BF16), pltpu.VMEM((rows, width), F32)
    weight = pltpu.VMEM((width, width), BF16)
    box = pltpu.VMEM((sizes.seq, sizes.part + 8, LANES), F32)
    pair_box = pltpu.VMEM((4, sizes.seq, 256 // sizes.seq + 8, LANES), F32)
    semaphores = pltpu.SemaphoreType.DMA
    scratch = dict(
        tokens=low, wc=weight, wk=weight, wv=weight, wq=weight, wo=weight,
        up=pltpu.VMEM((4, width, 512), BF16), down=pltpu.VMEM((hidden, width), BF16), pull=low,
        normed=low, queries=low, keys=low, values=low, local=wide, weights=low,
        sums=wide, logits=wide, chances=wide, shares=low, mixed=low, hidden=wide,
        branch=low, turned=pltpu.VMEM((width, rows), BF16), active=low, pushed=low, result=low,
        near_grad=pltpu.VMEM((512, LANES), BF16), total_grad=pltpu.VMEM((512, LANES), F32),
        prior=pltpu.VMEM((8, LANES, LANES), BF16), notes=pltpu.VMEM((8, 8, LANES), F32),
        small=pltpu.VMEM((40, LANES), F32),
        held=pltpu.VMEM((sizes.rows, LANES), F32), landed=pltpu.VMEM((sizes.landing, LANES), F32),
        box0=box, box1=box, box2=box, box3=box, box4=pair_box, box5=pair_box, box6=pair_box, box7=pair_box,
        box_sem=semaphores((4,)), pair_sem=semaphores((4, 4)), load_sem=semaphores((LOADS + 2,)), up_sem=semaphores((4,)),
        keep_sem=semaphores((14,)), reduce_send=semaphores((14,)),
        reduce_recv=semaphores((14, 8)),
    )
    names = list(arrays) + list(outputs) + list(scratch)

    def kernel(*refs):
        layer_kernel(sizes, types.SimpleNamespace(**dict(zip(names, refs, strict=True))))

    anywhere = pl.BlockSpec(memory_space=pl.ANY)
    near = pl.BlockSpec(memory_space=pltpu.VMEM)
    found = pl.pallas_call(
        kernel,
        out_shape=list(outputs.values()),
        in_specs=[anywhere if name.startswith("in_") else near for name in arrays],
        out_specs=[anywhere] * len(outputs),
        scratch_shapes=list(scratch.values()),
        compiler_params=pltpu.CompilerParams(
            collective_id=1, has_side_effects=True, vmem_limit_bytes=63 * 2**20
        ),
        name="layer",
    )(*arrays.values())
    return types.SimpleNamespace(**dict(zip(outputs, found, strict=True)))


def solution(mesh):
    sizes = Sizes(mesh.shape[DP], mesh.shape[SEQ])

    def shards(
        inputs, starts, attn_gain, attn_shift, query_weight, key_weight, value_weight, control_weight, output_weight,
        ffn_gain, ffn_shift, up_weight, up_bias, down_weight, down_bias, slot_means, cotangent,
    ):
        streams, length, width = inputs.shape
        rows = streams * length
        found = layer_call(
            sizes,
            in_tokens=inputs.reshape(rows, width),
            in_wc=control_weight,
            in_wk=key_weight,
            in_wv=value_weight,
            in_wq=query_weight,
            in_wo=output_weight,
            in_up=up_weight,
            in_down=down_weight,
            in_pull=cotangent.reshape(rows, width),
            starts=starts,
            attn_gain=attn_gain[None],
            attn_shift=attn_shift[None],
            ffn_gain=ffn_gain[None],
            ffn_shift=ffn_shift[None],
            up_bias=up_bias[None],
            down_bias=down_bias[None],
        )
        outs = list(deliver_call(
            streams * sizes.dp, found.out_full, found.out_result, found.out_input_grad, slot_means)
        )
        outs[0], outs[1] = outs[0].reshape(inputs.shape), outs[1].reshape(inputs.shape)
        for at in (2, 3, 9, 10, 12, 14):
            outs[at] = outs[at].reshape(-1)
        return tuple(outs)

    split = P(DP, SEQ, None)
    return jax.shard_map(
        shards,
        mesh=mesh,
        in_specs=(split, P(DP, SEQ)) + (P(),) * 14 + (split,),
        out_specs=(split, split) + (P(),) * 14,
        check_vma=False,
    )
```

time: 645 us -> 230 us (0.36)
  waiting for transfers between devices: 186 us -> 0 us
  Pallas kernels: 42.1 us -> 228 us
  blocking collectives: 134 us -> 0 us
  local copies, waits for them, and re-layouts: 119 us -> 1.3 us
  matrix products: 113 us -> 0 us
  other arithmetic: 30 us -> 0 us
  between operations: 15.6 us -> 0.81 us
    pallas_call x1 -> x2, Pallas kernels: 42.1 us -> 228 us  [the longest x1 214 us: layer_call(): pl.pallas_call(kernel, out_shape=list(outputs.values()), in_specs=[anywhe...]
    psum x1 -> x0, waiting for transfers between devices: 186 us -> none  [shards(): lax.psum((attn_gain_grad, attn_shift_grad, query_weight_grad, key_weight_...]
    dot_general x33 -> x0, matrix products: 113 us -> none  [the longest x14 46.7 us: product(): return jnp.einsum(form, left, right, preferred_element_type=jnp.float32)]
    reshape x21 -> x0, local copies, waits for them, and re-layouts: 78.6 us -> none  [the longest x18 69 us: split(): return a.reshape(streams, length, heads, head_size)]
    all_gather x2 -> x0, blocking collectives: 61.4 us -> none  [carried_in(): gathered = jax.tree.map(lambda a: lax.all_gather(a, axis), part)]
    psum x1 -> x0, blocking collectives: 38.6 us -> none  [shards(): lax.psum((attn_gain_grad, attn_shift_grad, query_weight_grad, key_weight_...]
    unnamed x1 -> x0, blocking collectives: 34 us -> none
    unnamed x145 -> x1, local copies, waits for them, and re-layouts: 26.3 us -> 1.3 us
  transfers between devices with their start and end apart: 2 -> 0, of which waited for: 1 -> 0; matrix products, arithmetic and copies ran while one was open for 11% -> 0% of each run, Pallas kernels for 0% -> 0%
where the time goes in v3:
time: 230 us
  Pallas kernels  228 us (99%)
    pallas_call x1, Pallas kernels, layer_call(): pl.pallas_call(kernel, out_shape=list(outputs.values()), in_specs=[anywhe...  214 us
    pallas_call x1, Pallas kernels, deliver_call(): pl.pallas_call(kernel, out_shape=[jax.ShapeDtypeStruct(shape.shape, shape...  14 us

profile of v3, /device:TPU:0, one launch (start us, length us, event | category | flops | bytes accessed | tf_op | source)
XLA Modules:
  0.0 230.1 jit_solution(15228349817296409515)
XLA Ops:
  0.6 1.3 copy.33.refs_9_
  1.9 213.9 %layer.1 = (bf16[1024,512]{1,0:T(8,128)(2,1)}, f32[1024,512]{1,0:T(8,128)}, f32[27136,128]{1,0:T(8,128)}) custom-call(bf16[1024,512]{1,0:T(8,128)(2,1)} %bitcast.16, bf16[512,512]{1,0:T(8,128)(2,1)} %refs_1_.1, bf16[512,512]{1,0:T(8,128)(2,1)} %refs_2_.1, bf16[512,512]{1,0:T(8,128)(2,1)} %refs_3_.1, bf16[512,512]{1,0:T(8,128)(2,1)} %refs_4_.1, ...), custom_call_target="tpu_custom_call" | custom-call | tf_op jit(solution)/shard_map/layer/pallas_call | solution.py:1057
  215.9 14.0 %deliver.1 = (bf16[1024,512]{1,0:T(8,128)(2,1)}, f32[1024,512]{1,0:T(8,128)}, f32[1,512]{1,0:T(1,128)}, f32[1,512]{1,0:T(1,128)}, f32[512,512]{1,0:T(8,128)}, /*...) custom-call(f32[27136,128]{1,0:T(8,128)} %get-tuple-element.35.full,, ...), custom_call_target="tpu_custom_call" | custom-call | tf_op jit(solution)/shard_map/deliver/pallas_call | solution.py:1006

commit v4 on v3

--- a/solution.py
+++ b/solution.py
@@ -1,3 +1,4 @@
+import functools
 import types
 
 import jax
@@ -17,8 +18,10 @@
 BF16 = jnp.bfloat16
 LANES = 128
 HALF = 256
+SHARE = 8
 DP, SEQ = "dp", "seq"
-CORE, LINE, NEAR, FAR = range(4)
+CORE, LINE, NEAR, LOW, HIGH = range(5)
+LEVELS = 5
 
 
 def mm(left, right):
@@ -56,12 +59,25 @@
     return jnp.where(first_head((HEAD, LANES)), square[:HEAD], square[HEAD:])
 
 
-def lower(shape=(HALF, HALF)):
-    return iota(shape, 0) >= iota(shape, 1)
-
-
-def upper(shape=(HALF, HALF)):
-    return iota(shape, 0) <= iota(shape, 1)
+def stacked(values):
+    return jnp.concatenate([only_head(values, 0), only_head(values, 1)], axis=0)
+
+
+def masked(square, earlier):
+    row = iota(square.shape, 0)
+    column = jnp.bitwise_and(iota(square.shape, 1), LANES - 1)
+    keep = row >= column if earlier else row <= column
+    return jnp.where(keep, square, 0.0).astype(BF16)
+
+
+def own_blocks(square):
+    inside = (iota(square.shape, 0) < HEAD) == first_head(square.shape)
+    return jnp.where(inside, square, 0.0)
+
+
+def triangle(earlier):
+    row, column = iota((LANES, LANES), 0), iota((LANES, LANES), 1)
+    return jnp.where(row >= column if earlier else row <= column, 1.0, 0.0).astype(BF16)
 
 
 def head_reduce(values, operation, empty):
@@ -138,16 +154,18 @@
             CORE: (2, core, lambda m: {DP: line * 2 + m}),
             LINE: (dp // 2, line, lambda m: {DP: m * 2 + core}),
             NEAR: (fast, near, lambda m: {SEQ: far * fast + m}),
-            FAR: (slow, far, lambda m: {SEQ: m * fast + near}),
+            LOW: (2, lax.rem(far, 2), lambda m: {SEQ: (far // 2 * 2 + m) * fast + near}),
+            HIGH: (2, far // 2, lambda m: {SEQ: (m * 2 + lax.rem(far, 2)) * fast + near}),
         }
         self.ways = dp // 2 * fast * slow
 
     def orders(self, rows, index):
         half = rows // 2
-        ways = [(LINE, NEAR, FAR), (NEAR, LINE, FAR)]
-        if half % (2 * self.ways * 8) == 0:
-            return [(0, half // 2, ways[0]), (half // 2, half // 2, ways[1])]
-        return [(0, half, ways[index % 2])]
+        least = self.ways * 8
+        if half >= 2 * least:
+            first = max(half // least * SHARE // 16, 1) * least
+            return [(0, first, (LINE, NEAR, LOW, HIGH)), (first, half - first, (NEAR, LINE, LOW, HIGH))]
+        return [(0, half, (LINE, NEAR, LOW, HIGH))]
 
     def steps(self, chunk, level):
         base, rows, land, index = chunk
@@ -171,7 +189,7 @@
         return found, sum(size * (self.groups[name][0] - 1) for _, size, name, _ in found)
 
     def rows_sent(self, chunk):
-        return 2 * sum(self.steps(chunk, level)[1] for level in range(4))
+        return 2 * sum(self.steps(chunk, level)[1] for level in range(LEVELS))
 
     def copy(self, chunk, slot, source, target, device):
         return pltpu.make_async_remote_copy(
@@ -190,13 +208,13 @@
                 to = lax.rem(at + k, count)
                 if gather:
                     rows = pl.ds(pl.multiple_of(start + at * size, 8), size)
-                    source = (self.held if level == 3 else self.full).at[rows]
+                    source = (self.held if level == LEVELS - 1 else self.full).at[rows]
                     target = self.full.at[rows]
                 else:
                     source = self.held.at[pl.ds(pl.multiple_of(start + to * size, 8), size)]
                     target = self.landed.at[pl.ds(pl.multiple_of(land + (k - 1) * size, 8), size)]
-                self.copy(chunk, level + 4 * gather, source, target, device(to)).start()
-            if gather and level == 3:
+                self.copy(chunk, level + LEVELS * gather, source, target, device(to)).start()
+            if gather and level == LEVELS - 1:
                 rows = pl.ds(pl.multiple_of(start + at * size, 8), size)
                 pltpu.make_async_copy(
                     self.held.at[rows], self.full.at[rows], self.keep_sem.at[chunk[3]]
@@ -206,8 +224,8 @@
         steps, rows = self.steps(chunk, level)
         at = pl.ds(chunk[0], rows) if gather else pl.ds(steps[0][3], rows)
         ref = (self.full if gather else self.landed).at[at]
-        self.copy(chunk, level + 4 * gather, ref, ref, self.groups[CORE][2](0)).wait_recv()
-        if gather and level == 3:
+        self.copy(chunk, level + LEVELS * gather, ref, ref, self.groups[CORE][2](0)).wait_recv()
+        if gather and level == LEVELS - 1:
             at = pl.ds(chunk[0], sum(size for _, size, _, _ in steps))
             pltpu.make_async_copy(
                 self.held.at[at], self.full.at[at], self.keep_sem.at[chunk[3]]
@@ -238,16 +256,19 @@
 
     def stage(self, chunk, number):
         if number:
-            level, gather = (number - 1, False) if number <= 4 else (8 - number, True)
-            self.wait(chunk, level, gather)
-            if not gather:
+            summing = number <= LEVELS
+            level = number - 1 if summing else 2 * LEVELS - number
+            self.wait(chunk, level, not summing)
+            if summing:
                 self.add(chunk, level)
-        if number < 8:
-            self.start(chunk, *((number, False) if number < 4 else (7 - number, True)))
+        if number < LEVELS:
+            self.start(chunk, number, False)
+        elif number < 2 * LEVELS:
+            self.start(chunk, 2 * LEVELS - 1 - number, True)
 
 
 def timetable(costs, begins):
-    line = {0: (0, 0.9), 1: (1, 2.9), 2: (1, 1.5), 3: (2, 2.9)}
+    line = [(0, 0.9), (1, 2.9), (1, 1.5), (2, 1.5), (2, 1.5)]
     now, free, ready, following = 0.0, [0.0] * 3, {}, {}
     table = [[] for _ in costs] + [[]]
 
@@ -256,10 +277,10 @@
         now += EVENT
         place.append((chunk, number))
         following[chunk] = number + 1
-        if number == 8:
+        if number == 2 * LEVELS:
             del following[chunk], ready[chunk]
             return
-        link, cost = line[min(number, 7 - number)]
+        link, cost = line[min(number, 2 * LEVELS - 1 - number)]
         free[link] = max(now, free[link]) + (cost if chunk < 13 else cost / 4)
         ready[chunk] = free[link] + LATENCY
 
@@ -304,6 +325,17 @@
     return inverse * (inside - first - scaled * second)
 
 
+def quarters(values):
+    return [values[at * LANES : (at + 1) * LANES] for at in range(4)]
+
+
+def running(blocks):
+    sums = [blocks[0]]
+    for block in blocks[1:]:
+        sums.append(sums[-1] + block)
+    return sums
+
+
 def column_sum(values):
     return jnp.sum(values, axis=0, keepdims=True)
 
@@ -311,20 +343,17 @@
 LOADS = 8
 ATTN_GAIN, ATTN_SHIFT, FFN_GAIN, FFN_SHIFT, DOWN_BIAS, WRITES, UP_BIAS = range(0, 28, 4)
 CHUNK = 2048
-EVENT = 0.2
+EVENT = 0.35
 LATENCY = 3.0
-COSTS = [0.85] * 24 + [0.5] * 4 + [0.8, 1.0] + [1.7, 1.7, 1.2, 1.2, 0.4, 0.1] * 3
-COSTS += [1.7, 1.7, 1.2, 1.2, 1.6, 0.1, 1.7, 1.7, 1.2, 1.2, 0.4, 0.1] * 2
-COSTS += [1.7, 1.7, 1.2, 1.2, 1.6, 0.1] + [0.0, 1.0, 0.0, 1.6] + [1.0] * 4 + [0.3]
-BEGINS = [4, 5, 10, 11, 16, 17, 22, 23, 28, 52, 64, 76, 81, 86]
+COSTS = [0.85] * 24 + [0.5] * 4 + [0.8, 1.0] + [0.9, 0.9, 1.1, 0.7, 0.3, 0.0] * 8
+COSTS += [0.9, 0.8, 0.8, 0.8, 1.0, 1.8, 0.9, 0.9] + [1.0] * 4 + [0.3]
+BEGINS = [4, 5, 10, 11, 16, 17, 22, 23, 28, 78, 83, 84, 85, 90]
 TABLE = timetable(COSTS, BEGINS)
 
 
 class Sizes:
     def __init__(self, dp, seq):
         self.dp, self.seq = dp, seq
-        self.groups = seq // 8
-        self.part = LANES // self.groups
         self.tiny = max(512, dp // 2 * seq * 16)
         self.rows = 13 * CHUNK + self.tiny
         self.landing = 9 * CHUNK
@@ -339,7 +368,7 @@
 
 def layer_kernel(sizes, refs):
     r = refs
-    seq, groups, part = sizes.seq, sizes.groups, sizes.part
+    seq = sizes.seq
     dp_at, me = lax.axis_index(DP), lax.axis_index(SEQ)
 
     sources = (r.in_tokens, r.in_wc, r.in_wk, r.in_wv, r.in_wq, r.in_wo, r.in_down, r.in_pull)
@@ -384,8 +413,15 @@
         r.local, r.weights, r.sums, r.logits, r.chances, r.shares, r.mixed
     )
     notes, prior, hidden, held, small = r.notes, r.prior, r.hidden, r.held, r.small
-    there = Exchange(seq, r.box0, r.box1, r.box_sem.at[0], r.box_sem.at[1])
-    back = Exchange(seq, r.box2, r.box3, r.box_sem.at[2], r.box_sem.at[3])
+    early = 512 // seq
+    there = [
+        Exchange(seq, r.box0.at[at], r.box1.at[at], r.box_sem.at[0, at], r.box_sem.at[1, at])
+        for at in range(2)
+    ]
+    back = [
+        Exchange(seq, r.box2.at[at], r.box3.at[at], r.box_sem.at[2, at], r.box_sem.at[3, at])
+        for at in range(2)
+    ]
     theres = [
         Exchange(seq, r.box4.at[at], r.box5.at[at], r.pair_sem.at[0, at], r.pair_sem.at[1, at])
         for at in range(4)
@@ -419,6 +455,7 @@
             small[row, :] = small[row, :] + values[:, column * LANES : (column + 1) * LANES]
 
     small[...] = jnp.zeros_like(small)
+    pull, down = r.pull, r.down
 
     for copy in early_loads:
         copy.wait()
@@ -433,7 +470,8 @@
         values[rows, :] = mm(low, r.wv[...]).astype(BF16)
         return unused
 
-    def summarize(combo, unused):
+    def summarize(stream, pair, unused):
+        combo = 4 * stream + pair
         row, col = block_of(combo)
         rows, cols = pl.ds(row, 512), pl.ds(col, LANES)
         control = local[rows, cols]
@@ -444,21 +482,21 @@
         memory = add_parts(mm_rows(pair_rows, parts_of(spread)))
         memory = jnp.concatenate([one_block(memory[:LANES]), one_block(memory[LANES:])], axis=0)
         total = column_sum(spread)
-        flag = jnp.broadcast_to(r.starts[pl.ds(combo // 4, 1), :].astype(F32), (1, LANES))
+        flag = jnp.broadcast_to(r.starts[stream : stream + 1, :].astype(F32), (1, LANES))
         line = iota((8, LANES), 0)
         notes[combo] = jnp.where(line == 0, block_max, jnp.where(line == 1, total, flag))
-        for group in range(groups):
-            to = combo * groups + group
-            there.sent[to, :part] = memory[group * part : (group + 1) * part]
-            there.sent[to, part:] = notes[combo]
-            there.send(to)
+        for group in range(seq // 4):
+            to = pair * (seq // 4) + group
+            there[stream].sent[to, :early] = memory[group * early : (group + 1) * early]
+            there[stream].sent[to, early:] = notes[combo]
+            there[stream].send(to)
         return unused
 
     for stream in range(2):
         lax.fori_loop(2 * stream, 2 * stream + 2, project, 0)
         if stream == 0:
             pl.semaphore_wait(barrier, count)
-        lax.fori_loop(4 * stream, 4 * stream + 4, summarize, 0)
+        lax.fori_loop(0, 4, functools.partial(summarize, stream), 0)
 
     load_wq.wait()
 
@@ -469,73 +507,93 @@
 
     lax.fori_loop(0, 4, project_query, 0)
 
+    def accumulate(base, rows_at, values, first):
+        for column in range(4):
+            place = pl.ds(pl.multiple_of(base + column * 1024 + rows_at, 8), HALF)
+            block = values[:, column * LANES : (column + 1) * LANES]
+            held[place] = jnp.where(first, block, held[place] + block)
+
+    def collected(base, rows_at):
+        return jnp.concatenate(
+            [
+                held[pl.ds(pl.multiple_of(base + column * 1024 + rows_at, 8), HALF)]
+                for column in range(4)
+            ],
+            axis=1,
+        )
+
+    def store_block(base, square, rows_at):
+        for column in range(square.shape[1] // LANES):
+            place = pl.ds(pl.multiple_of(base + column * 512 + rows_at, 8), square.shape[0])
+            held[place] = square[:, column * LANES : (column + 1) * LANES]
+
     def inside(combo, unused):
         row, col = block_of(combo)
-        cols = pl.ds(col, LANES)
-        spread = local[pl.ds(row, 512), cols]
-        low = spread.astype(BF16)
-        triangle = lower()
-        ones = jnp.where(triangle, 1.0, 0.0).astype(BF16)
-        first = add_parts(mm(ones, parts_of(spread[:HALF])))
-        second = add_parts(mm(ones, parts_of(spread[HALF:]))) + first[HALF - 1 :]
-        sums[pl.ds(row, HALF), cols] = first
-        sums[pl.ds(row + HALF, HALF), cols] = second
-        for at in range(2):
-            rows = pl.ds(row + at * HALF, HALF)
-            width = (at + 1) * HALF
-            total = None
-            for head in range(2):
-                query = only_head(queries[rows, cols], head)
-                found = []
-                for other in range(at + 1):
-                    score = mm_lanes(query, keys[pl.ds(row + other * HALF, HALF), cols])
-                    if other == at:
-                        score = jnp.where(triangle, score, 0.0)
-                    found.append(score.astype(BF16))
-                score = found[0] if at == 0 else jnp.concatenate(found, axis=1)
-                term = mm(score, only_head(low[:width], head))
-                total = term if total is None else total + term
-            logits[rows, cols] = total
+        rows, cols = pl.ds(row, 512), pl.ds(col, LANES)
+        spread = local[rows, cols]
+        low = quarters(spread.astype(BF16))
+        query, key = quarters(queries[rows, cols]), quarters(keys[rows, cols])
+        ones = triangle(True)
+        totals = [add_parts(mm(ones, part)) for part in quarters(parts_of(spread))]
+        scores = [mm_lanes(query[at], stacked(key[at])) for at in range(4)]
+        added = [own_blocks(mm_rows(key[at], low[at])) for at in range(3)]
+        scores = [masked(score, True) for score in scores]
+        numbers = [mm(scores[at], stacked(low[at])) for at in range(4)]
+        memories = [memory.astype(BF16) for memory in running(added)]
+        for at in range(1, 4):
+            numbers[at] = numbers[at] + mm(query[at], memories[at - 1])
+            totals[at] = totals[at] + totals[at - 1][LANES - 1 :]
+        sums[rows, cols] = jnp.concatenate(totals, axis=0)
+        logits[rows, cols] = jnp.concatenate(numbers, axis=0)
         return unused
 
+    def hand_out(stream):
+        arrived, answers = there[stream], back[stream]
+        arrived.receive()
+        prior_max = jnp.full((1, LANES), -HUGE_VALUE, F32)
+        raw_total = jnp.zeros((1, LANES), F32)
+        raw_memory = jnp.zeros((early, LANES), F32)
+        line = iota((8, LANES), 0)
+        for source in range(seq):
+            answers.sent[source, :early] = raw_memory
+            answers.sent[source, early:] = jnp.where(line == 0, prior_max, raw_total)
+            if source < seq - 1:
+                block_max = arrived.landed[source, early : early + 1]
+                total = arrived.landed[source, early + 1 : early + 2]
+                flag = arrived.landed[source, early + 2 : early + 3]
+                ceiling = jnp.maximum(prior_max, block_max)
+                old = (1.0 - flag) * jnp.exp(prior_max - ceiling)
+                new = jnp.exp(block_max - ceiling)
+                raw_total = old * raw_total + new * total
+                raw_memory = old * raw_memory + new * arrived.landed[source, :early]
+                prior_max = ceiling
+        answers.send_all()
+
+    def pull_back(step, unused):
+        rows_at = pl.multiple_of(lax.rem(step, 4) * HALF, HALF)
+        along = pl.ds(pl.multiple_of(step // 4 * 512, 512), 512)
+        grad = mm_lanes(pull[pl.ds(rows_at, HALF), :], down[along, :])
+        accumulate(step // 4 * 2 * CHUNK, rows_at, grad, True)
+        return unused
+
     lax.fori_loop(0, 4, inside, 0)
-
-    prior_max = jnp.full((1, LANES), -HUGE_VALUE, F32)
-    raw_total = jnp.zeros((1, LANES), F32)
-    raw_memory = jnp.zeros((part, LANES), F32)
-    line = iota((8, LANES), 0)
-    there.receive()
-    for source in range(seq):
-        back.sent[source, :part] = raw_memory
-        back.sent[source, part:] = jnp.where(line == 0, prior_max, raw_total)
-        back.send(source)
-        if source < seq - 1:
-            block_max = there.landed[source, part : part + 1]
-            total = there.landed[source, part + 1 : part + 2]
-            flag = there.landed[source, part + 2 : part + 3]
-            ceiling = jnp.maximum(prior_max, block_max)
-            old = (1.0 - flag) * jnp.exp(prior_max - ceiling)
-            new = jnp.exp(block_max - ceiling)
-            raw_total = old * raw_total + new * total
-            raw_memory = old * raw_memory + new * there.landed[source, :part]
-            prior_max = ceiling
-
+    hand_out(0)
     lax.fori_loop(4, 8, inside, 0)
-
-    def returned(exchange, combo):
-        pieces = [exchange.landed[combo * groups + group, :part] for group in range(groups)]
-        memory = pieces[0] if groups == 1 else jnp.concatenate(pieces, axis=0)
-        first = combo * groups
-        return (
-            memory,
-            exchange.landed[first, part : part + 1],
-            exchange.landed[first, part + 1 : part + 2],
-        )
+    load_pull.wait()
+    load_down.wait()
+    lax.fori_loop(0, 8, pull_back, 0)
+    hand_out(1)
+    lax.fori_loop(8, 16, pull_back, 0)
 
     def attend(combo, unused):
         row, col = block_of(combo)
         cols = pl.ds(col, LANES)
-        memory, past_max, past_total = returned(back, combo)
+        stream, first = combo // 4, lax.rem(combo, 4) * (seq // 4)
+        memory = jnp.concatenate(
+            [r.box3[stream, first + group, :early] for group in range(seq // 4)], axis=0
+        )
+        past_max = r.box3[stream, first, early : early + 1]
+        past_total = r.box3[stream, first, early + 1 : early + 2]
         block_max = notes[combo, 0:1]
         flag = notes[combo, 2:3]
         ceiling = jnp.maximum(past_max, block_max)
@@ -547,45 +605,42 @@
         prior[combo] = memory
         prior_keys = both_blocks(memory[:HEAD])
         prior_values = both_blocks(memory[HEAD:])
-        triangle = lower()
-        written = jnp.zeros((1, LANES), F32)
-        for at in range(2):
-            rows = pl.ds(row + at * HALF, HALF)
-            weight = local[rows, cols] * factor
-            weights[rows, cols] = weight.astype(BF16)
-            inverse = 1.0 / (carried * past_total + factor * sums[rows, cols])
-            sums[rows, cols] = inverse
-            written = written + column_sum(weight * inverse)
-            logit = (mm(queries[rows, cols], prior_keys) + factor * logits[rows, cols]) * inverse
-            logits[rows, cols] = logit
-            top = head_reduce(logit, jnp.max, -HUGE_VALUE)
-            raised = jnp.exp(logit - top)
-            chance = raised / head_reduce(raised, jnp.sum, 0.0)
-            chances[rows, cols] = chance
-            share = (chance * inverse).astype(BF16)
-            shares[rows, cols] = share
-            attended = mm_lanes(share, prior_values)
-            for head in range(2):
-                own = only_head(share, head)
-                for other in range(at + 1):
-                    these = pl.ds(row + other * HALF, HALF)
-                    mixing = mm_lanes(own, weights[these, cols])
-                    if other == at:
-                        mixing = jnp.where(triangle, mixing, 0.0)
-                    attended = attended + mm(
-                        mixing.astype(BF16), only_head(values[these, cols], head)
-                    )
-            mixed[rows, cols] = attended.astype(BF16)
+        rows = pl.ds(row, 512)
+        weight = local[rows, cols] * factor
+        low = weight.astype(BF16)
+        weights[rows, cols] = low
+        inverse = 1.0 / (carried * past_total + factor * sums[rows, cols])
+        sums[rows, cols] = inverse
+        written = column_sum(weight * inverse)
+        logit = (mm(queries[rows, cols], prior_keys) + factor * logits[rows, cols]) * inverse
+        logits[rows, cols] = logit
+        top = head_reduce(logit, jnp.max, -HUGE_VALUE)
+        raised = jnp.exp(logit - top)
+        chance = raised / head_reduce(raised, jnp.sum, 0.0)
+        chances[rows, cols] = chance
+        share = (chance * inverse).astype(BF16)
+        shares[rows, cols] = share
+        attended = quarters(mm_lanes(share, prior_values))
+        share, low, value = quarters(share), quarters(low), quarters(values[rows, cols])
+        mixing = [mm_lanes(share[at], stacked(low[at])) for at in range(4)]
+        added = [own_blocks(mm_rows(value[at], low[at])) for at in range(3)]
+        mixing = [masked(square, True) for square in mixing]
+        memories = [memory.astype(BF16) for memory in running(added)]
+        for at in range(4):
+            attended[at] = attended[at] + mm(mixing[at], stacked(value[at]))
+            if at:
+                attended[at] = attended[at] + mm_lanes(share[at], memories[at - 1])
+        mixed[rows, cols] = jnp.concatenate(attended, axis=0).astype(BF16)
         place = pl.ds(WRITES + lax.rem(combo, 4), 1)
         small[place, :] = small[place, :] + written
         return unused
 
-    back.receive()
-    lax.fori_loop(0, 8, attend, 0)
+    for stream in range(2):
+        back[stream].receive()
+        lax.fori_loop(4 * stream, 4 * stream + 4, attend, 0)
 
     load_wo.wait()
-    load_pull.wait()
-    pull, branch, turned = r.pull, r.branch, r.turned
+    branch, turned = r.branch, r.turned
 
     def project_out(step, unused):
         rows = pl.ds(pl.multiple_of(step * HALF, HALF), HALF)
@@ -600,31 +655,10 @@
 
     lax.fori_loop(0, 4, project_out, 0)
 
-    load_down.wait()
     for copy in up_loads:
         copy.wait()
-    up, down, active, pushed = r.up, r.down, r.active, r.pushed
+    up, active, pushed = r.up, r.active, r.pushed
     after = 9 * CHUNK
-
-    def running(base, rows_at, values, first):
-        for column in range(4):
-            place = pl.ds(pl.multiple_of(base + column * 1024 + rows_at, 8), HALF)
-            block = values[:, column * LANES : (column + 1) * LANES]
-            held[place] = jnp.where(first, block, held[place] + block)
-
-    def collected(base, rows_at):
-        return jnp.concatenate(
-            [
-                held[pl.ds(pl.multiple_of(base + column * 1024 + rows_at, 8), HALF)]
-                for column in range(4)
-            ],
-            axis=1,
-        )
-
-    def store_block(base, square, rows_at):
-        for column in range(square.shape[1] // LANES):
-            place = pl.ds(pl.multiple_of(base + column * 512 + rows_at, 8), square.shape[0])
-            held[place] = square[:, column * LANES : (column + 1) * LANES]
 
     def feed_forward(part_at, unused):
         base = part_at * 2 * CHUNK
@@ -637,10 +671,10 @@
             low = value.astype(BF16)
             active[rows, :] = low
             along = pl.ds(pl.multiple_of(part_at * 512, 512), 512)
-            grad = (mm_lanes(pull[rows, :], down[along, :]) * slope).astype(BF16)
+            grad = (collected(base, rows_at) * slope).astype(BF16)
             pushed[rows, :] = grad
-            running(after, rows_at, mm(low, down[along, :]), part_at == 0)
-            running(after + 4096, rows_at, mm_lanes(grad, up[part_at]), part_at == 0)
+            accumulate(after, rows_at, mm(low, down[along, :]), part_at == 0)
+            accumulate(after + 4096, rows_at, mm_lanes(grad, up[part_at]), part_at == 0)
             total = column_sum(grad.astype(F32))
             for column in range(4):
                 place = pl.ds(UP_BIAS + part_at * 4 + column, 1)
@@ -667,7 +701,7 @@
         rows_at = pl.multiple_of(step * HALF, HALF)
         rows = pl.ds(rows_at, HALF)
         wide = hidden[rows, :]
-        r.result[rows, :] = (wide + collected(after, rows_at) + r.down_bias[...]).astype(BF16)
+        pushed[rows, :] = (wide + collected(after, rows_at) + r.down_bias[...]).astype(BF16)
         scaled, inverse = normalized(wide)
         upstream = collected(after + 4096, rows_at)
         put_small(FFN_GAIN, column_sum(upstream * scaled))
@@ -679,7 +713,7 @@
         return unused
 
     lax.fori_loop(0, 4, finish_rows, 0)
-    result_copy = pltpu.make_async_copy(r.result, r.out_result, r.load_sem.at[LOADS])
+    result_copy = pltpu.make_async_copy(pushed, r.out_result, r.load_sem.at[LOADS])
     result_copy.start()
     for block in range(2):
         wide = mm_rows(mixed[:, block * HALF : (block + 1) * HALF], branch[...])
@@ -704,88 +738,70 @@
         memory = prior[combo]
         prior_keys = both_blocks(memory[:HEAD])
         prior_values = both_blocks(memory[HEAD:])
-        triangle = lower()
-        early = upper()
-        all_rows = [pl.ds(row, HALF), pl.ds(row + HALF, HALF)]
-        for at in range(2):
-            rows = all_rows[at]
-            pulls = pulled[rows, cols]
-            share_grad = mm(pulls, prior_values)
-            for head in range(2):
-                own = only_head(pulls, head)
-                for other in range(at + 1):
-                    these = all_rows[other]
-                    grad = mm_lanes(own, values[these, cols])
-                    if other == at:
-                        grad = jnp.where(triangle, grad, 0.0)
-                    share_grad = share_grad + mm(
-                        grad.astype(BF16), only_head(weights[these, cols], head)
-                    )
-            inverse, chance = sums[rows, cols], chances[rows, cols]
-            chance_grad = share_grad * inverse
-            middle = head_reduce(chance * chance_grad, jnp.sum, 0.0)
-            logit_grad = chance * (chance_grad - middle)
-            number_grad = logit_grad * inverse
-            total_grad[pl.ds(at * HALF, HALF), :] = -(
-                chance_grad * chance * inverse + number_grad * logits[rows, cols]
-            )
-            low = number_grad.astype(BF16)
-            near_grad[pl.ds(at * HALF, HALF), :] = low
-            query_grad = mm_lanes(low, prior_keys)
-            for head in range(2):
-                own = only_head(low, head)
-                for other in range(at + 1):
-                    these = all_rows[other]
-                    grad = mm_lanes(own, weights[these, cols])
-                    if other == at:
-                        grad = jnp.where(triangle, grad, 0.0)
-                    query_grad = query_grad + mm(
-                        grad.astype(BF16), only_head(keys[these, cols], head)
-                    )
-            query_low[rows, cols] = query_grad.astype(BF16)
-            events_in({(q,): 30 + 6 * q + at for q in range(8)}, step)
-        ones = jnp.where(early, 1.0, 0.0).astype(BF16)
-        late_sum = add_parts(mm(ones, parts_of(total_grad[HALF:, :])))
-        early_sum = add_parts(mm(ones, parts_of(total_grad[:HALF, :]))) + late_sum[:1]
-        prior_total_grad = early_sum[:1]
-        for at in range(2):
-            rows = all_rows[at]
-            weight_grad = early_sum if at == 0 else late_sum
-            key_grad = value_grad = None
-            for head in range(2):
-                own_value = only_head(values[rows, cols], head)
-                own_weight = only_head(weights[rows, cols], head)
-                own_key = only_head(keys[rows, cols], head)
-                for other in range(at, 2):
-                    these = all_rows[other]
-                    near = near_grad[pl.ds(other * HALF, HALF), :]
-
-                    def masked(square, other=other):
-                        if other == at:
-                            square = jnp.where(early, square, 0.0)
-                        return square.astype(BF16)
-
-                    pulls = pulled[these, cols]
-                    share = shares[these, cols]
-                    query = queries[these, cols]
-                    weight_grad = weight_grad + mm(
-                        masked(mm_lanes(own_value, pulls)), only_head(share, head)
-                    )
-                    weight_grad = weight_grad + mm(
-                        masked(mm_lanes(own_key, query)), only_head(near, head)
-                    )
-                    term = mm(masked(mm_lanes(own_weight, share)), only_head(pulls, head))
-                    value_grad = term if value_grad is None else value_grad + term
-                    term = mm(masked(mm_lanes(own_weight, near)), only_head(query, head))
-                    key_grad = term if key_grad is None else key_grad + term
-            sums[rows, cols] = weight_grad * (local[rows, cols] * notes[combo, 3:4])
-            logits[rows, cols] = key_grad
-            chances[rows, cols] = value_grad
-            if at == 0:
-                events_in({(q,): 32 + 6 * q for q in range(8)}, step)
-        whole = pl.ds(row, 512)
-        key_memory = mm_rows(queries[whole, cols], near_grad[...])
-        value_memory = mm_rows(pulled[whole, cols], shares[whole, cols])
+        rows = pl.ds(row, 512)
+        inverse, chance = sums[rows, cols], chances[rows, cols]
+        weight, share = quarters(weights[rows, cols]), quarters(shares[rows, cols])
+        pulls, query = quarters(pulled[rows, cols]), quarters(queries[rows, cols])
+        key, value = quarters(keys[rows, cols]), quarters(values[rows, cols])
+        wide_weight = [stacked(block) for block in weight]
+        squares = [mm_lanes(pulls[at], stacked(value[at])) for at in range(4)]
+        added = [own_blocks(mm_rows(value[at], weight[at])) for at in range(3)]
+        squares = [masked(square, True) for square in squares]
+        inner = [memory.astype(BF16) for memory in running(added)]
+        grads = [mm(pulls[at], prior_values) + mm(squares[at], wide_weight[at]) for at in range(4)]
+        for at in range(1, 4):
+            grads[at] = grads[at] + mm(pulls[at], inner[at - 1])
+        events_in({(q,): 30 + 6 * q for q in range(8)}, step)
+        chance_grad = jnp.concatenate(grads, axis=0) * inverse
+        middle = head_reduce(chance * chance_grad, jnp.sum, 0.0)
+        number_grad = chance * (chance_grad - middle) * inverse
+        total_grad[...] = -(chance_grad * chance * inverse + number_grad * logits[rows, cols])
+        low = number_grad.astype(BF16)
+        near_grad[...] = low
+        near = quarters(low)
+        squares = [mm_lanes(near[at], wide_weight[at]) for at in range(4)]
+        added = [own_blocks(mm_rows(key[at], weight[at])) for at in range(3)]
+        squares = [masked(square, True) for square in squares]
+        inner = [memory.astype(BF16) for memory in running(added)]
+        grads = [mm_lanes(near[at], prior_keys) + mm(squares[at], stacked(key[at])) for at in range(4)]
+        for at in range(1, 4):
+            grads[at] = grads[at] + mm_lanes(near[at], inner[at - 1])
+        query_low[rows, cols] = jnp.concatenate(grads, axis=0).astype(BF16)
+        events_in({(q,): 31 + 6 * q for q in range(8)}, step)
+
+        near = quarters(near_grad[...])
+        wide_share, wide_near = [stacked(block) for block in share], [stacked(block) for block in near]
+        wide_pulls, wide_query = [stacked(block) for block in pulls], [stacked(block) for block in query]
+        added = [own_blocks(mm_rows(query[at], near[at])) for at in reversed(range(4))]
+        later_keys = running(added)
+        added = [own_blocks(mm_rows(pulls[at], share[at])) for at in reversed(range(4))]
+        later_values = running(added)
+        key_memory, value_memory = later_keys[3], later_values[3]
+        later_keys = [memory.astype(BF16) for memory in reversed(later_keys[:3])]
+        later_values = [memory.astype(BF16) for memory in reversed(later_values[:3])]
+        ones = triangle(False)
+        totals = [add_parts(mm(ones, part)) for part in quarters(parts_of(total_grad[...]))]
+        for at in reversed(range(3)):
+            totals[at] = totals[at] + totals[at + 1][:1]
+        carry = totals[0][:1]
+        one = [masked(mm_lanes(value[at], wide_pulls[at]), False) for at in range(4)]
+        two = [masked(mm_lanes(key[at], wide_query[at]), False) for at in range(4)]
+        for at in range(4):
+            totals[at] = totals[at] + mm(one[at], wide_share[at]) + mm(two[at], wide_near[at])
+            if at < 3:
+                totals[at] = totals[at] + mm(value[at], later_values[at]) + mm(key[at], later_keys[at])
+        sums[rows, cols] = jnp.concatenate(totals, axis=0) * (local[rows, cols] * notes[combo, 3:4])
+        events_in({(q,): 32 + 6 * q for q in range(8)}, step)
+        one = [masked(mm_lanes(weight[at], wide_share[at]), False) for at in range(4)]
+        two = [masked(mm_lanes(weight[at], wide_near[at]), False) for at in range(4)]
+        one = [mm(one[at], wide_pulls[at]) for at in range(4)]
+        two = [mm(two[at], wide_query[at]) for at in range(4)]
+        for at in range(3):
+            one[at] = one[at] + mm_lanes(weight[at], later_values[at])
+            two[at] = two[at] + mm_lanes(weight[at], later_keys[at])
+        logits[rows, cols] = jnp.concatenate(two, axis=0)
+        chances[rows, cols] = jnp.concatenate(one, axis=0)
+        prior_total_grad = carry
         keep = 1.0 - notes[combo, 2:3]
         memory = keep * jnp.concatenate([one_block(key_memory), one_block(value_memory)], axis=0)
         line = iota((8, LANES), 0)
@@ -826,15 +842,12 @@
             pl.when(pair == at)(lambda at=at: act(at))
 
     def finalize(pair):
-        if isinstance(pair, int):
-            backs[pair].receive()
-        else:
-            for_pair(pair, lambda at: backs[at].receive())
+        backs[pair].receive()
 
         def one(stream, unused):
             combo = stream * 4 + pair
             row, col = block_of(combo)
-            cols = pl.ds(col, LANES)
+            rows, cols = pl.ds(row, 512), pl.ds(col, LANES)
             first = stream * (seq // 2)
             memory = jnp.concatenate(
                 [r.box7[pair, first + group, :late] for group in range(seq // 2)], axis=0
@@ -845,26 +858,22 @@
             total = reach * total
             memory = (reach * memory).astype(BF16)
             key_memory, value_memory = both_blocks(memory[:HEAD]), both_blocks(memory[HEAD:])
-            for at in range(2):
-                rows = pl.ds(row + at * HALF, HALF)
-                spread = local[rows, cols]
-                low = spread.astype(BF16)
-                inner = mm(keys[rows, cols], key_memory) + mm(values[rows, cols], value_memory)
-                weights[rows, cols] = (sums[rows, cols] + spread * (inner + total)).astype(BF16)
-                key_grad = logits[rows, cols] + mm_lanes(low, key_memory)
-                value_grad = chances[rows, cols] + mm_lanes(low, value_memory)
-                keys[rows, cols] = key_grad.astype(BF16)
-                values[rows, cols] = value_grad.astype(BF16)
+            spread = local[rows, cols]
+            low = spread.astype(BF16)
+            inner = mm(keys[rows, cols], key_memory) + mm(values[rows, cols], value_memory)
+            weights[rows, cols] = (sums[rows, cols] + spread * (inner + total)).astype(BF16)
+            key_grad = logits[rows, cols] + mm_lanes(low, key_memory)
+            value_grad = chances[rows, cols] + mm_lanes(low, value_memory)
+            queries[rows, cols] = key_grad.astype(BF16)
+            shares[rows, cols] = value_grad.astype(BF16)
             return unused
 
         lax.fori_loop(0, 2, one, 0)
-        cols = pl.ds(pl.multiple_of(pair * LANES, LANES), LANES)
-        base = (9 + pair) * CHUNK
-        for at, (left, right) in enumerate(((query_low, keys), (values, weights))):
-            both = jnp.concatenate([left[:, cols], right[:, cols]], axis=1)
-            for block in range(2):
-                wide = mm(turned[block * HALF : (block + 1) * HALF, :], both)
-                store_block(base + at * 1024, wide, block * HALF)
+
+    def weight_grad(index, right):
+        for block in range(2):
+            wide = mm(turned[block * HALF : (block + 1) * HALF, :], right[...])
+            store_block(index * CHUNK, wide, block * HALF)
 
     def iteration(step, unused):
         backward((lax.rem(step, 2)) * 4 + step // 2, step)
@@ -874,40 +883,41 @@
         def _():
             for_pair(step // 2, lambda at: theres[at].send_all())
 
-        @pl.when((step >= 2) & (lax.rem(step, 2) == 0))
+        @pl.when((step >= 3) & (lax.rem(step, 2) == 1))
         def _():
             for_pair(step // 2 - 1, handle)
-
-        @pl.when((step >= 3) & (lax.rem(step, 2) == 1))
-        def _():
-            finalize((step - 3) // 2)
 
         events_in({(q,): 34 + 6 * q for q in range(8)}, step)
         events_in({(q,): 35 + 6 * q for q in range(8)}, step)
         return unused
 
     lax.fori_loop(0, 8, iteration, 0)
+    weight_grad(9, query_low)
     events(78)
-
+    for pair in range(3):
+        finalize(pair)
+        events(79 + pair)
     handle(3)
-    events(79)
-    events(80)
+    events(82)
     finalize(3)
-    events(81)
+    key_low, value_low, control_low = queries, shares, weights
+    for index, right in ((10, key_low), (11, value_low), (12, control_low)):
+        weight_grad(index, right)
+        events(73 + index)
 
     def input_rows(step, unused):
         rows = pl.ds(pl.multiple_of(step * HALF, HALF), HALF)
         upstream = mm_lanes(query_low[rows, :], r.wq[...])
-        upstream = upstream + mm_lanes(keys[rows, :], r.wk[...])
-        upstream = upstream + mm_lanes(values[rows, :], r.wv[...])
-        upstream = upstream + mm_lanes(weights[rows, :], r.wc[...])
+        upstream = upstream + mm_lanes(key_low[rows, :], r.wk[...])
+        upstream = upstream + mm_lanes(value_low[rows, :], r.wv[...])
+        upstream = upstream + mm_lanes(control_low[rows, :], r.wc[...])
         scaled, inverse = normalized(tokens[rows, :].astype(F32))
         put_small(ATTN_GAIN, column_sum(upstream * scaled))
         put_small(ATTN_SHIFT, column_sum(upstream))
         hidden[rows, :] = hidden[rows, :] + norm_pull(
             upstream, scaled, inverse, r.attn_gain[...]
         )
-        events_in({(q,): 82 + q for q in range(4)}, step)
+        events_in({(q,): 86 + q for q in range(4)}, step)
         return unused
 
     lax.fori_loop(0, 4, input_rows, 0)
@@ -918,11 +928,11 @@
     last = sizes.last()
     held[pl.ds(last[0], last[1])] = jnp.zeros((last[1], LANES), F32)
     held[pl.ds(last[0], small.shape[0])] = small[...]
-    events(86)
-    events(87)
+    events(90)
+    events(91)
     for copy in (result_copy, grad_copy):
         copy.wait()
-    for exchange in (there, back, *theres, *backs):
+    for exchange in (*there, *back, *theres, *backs):
         exchange.finish()
     for index in range(14):
         reduction.finish(chunk_of(index))
@@ -955,10 +965,8 @@
         for column in range(4):
             lanes = pl.ds(column * LANES, LANES)
             source = held.at[pl.ds(index * CHUNK + column * 512, 512)]
-            if index == 8:
-                store(source, wo.at[:, lanes])
-            elif index > 8:
-                store(source, (wq, wk, wv, wc)[column].at[:, pl.ds((index - 9) * LANES, LANES)])
+            if index >= 8:
+                store(source, (wo, wq, wk, wv, wc)[index - 8].at[:, lanes])
             elif index % 2:
                 store(source, up.at[:, pl.ds(index // 2 * 512 + column * LANES, LANES)])
             else:
@@ -1029,7 +1037,7 @@
     )
     low, wide = pltpu.VMEM((rows, width), BF16), pltpu.VMEM((rows, width), F32)
     weight = pltpu.VMEM((width, width), BF16)
-    box = pltpu.VMEM((sizes.seq, sizes.part + 8, LANES), F32)
+    box = pltpu.VMEM((2, sizes.seq, 512 // sizes.seq + 8, LANES), F32)
     pair_box = pltpu.VMEM((4, sizes.seq, 256 // sizes.seq + 8, LANES), F32)
     semaphores = pltpu.SemaphoreType.DMA
     scratch = dict(
@@ -1037,15 +1045,15 @@
         up=pltpu.VMEM((4, width, 512), BF16), down=pltpu.VMEM((hidden, width), BF16), pull=low,
         normed=low, queries=low, keys=low, values=low, local=wide, weights=low,
         sums=wide, logits=wide, chances=wide, shares=low, mixed=low, hidden=wide,
-        branch=low, turned=pltpu.VMEM((width, rows), BF16), active=low, pushed=low, result=low,
+        branch=low, turned=pltpu.VMEM((width, rows), BF16), active=low, pushed=low,
         near_grad=pltpu.VMEM((512, LANES), BF16), total_grad=pltpu.VMEM((512, LANES), F32),
         prior=pltpu.VMEM((8, LANES, LANES), BF16), notes=pltpu.VMEM((8, 8, LANES), F32),
         small=pltpu.VMEM((40, LANES), F32),
         held=pltpu.VMEM((sizes.rows, LANES), F32), landed=pltpu.VMEM((sizes.landing, LANES), F32),
         box0=box, box1=box, box2=box, box3=box, box4=pair_box, box5=pair_box, box6=pair_box, box7=pair_box,
-        box_sem=semaphores((4,)), pair_sem=semaphores((4, 4)), load_sem=semaphores((LOADS + 2,)), up_sem=semaphores((4,)),
+        box_sem=semaphores((4, 2)), pair_sem=semaphores((4, 4)), load_sem=semaphores((LOADS + 2,)), up_sem=semaphores((4,)),
         keep_sem=semaphores((14,)), reduce_send=semaphores((14,)),
-        reduce_recv=semaphores((14, 8)),
+        reduce_recv=semaphores((14, 2 * LEVELS)),
     )
     names = list(arrays) + list(outputs) + list(scratch)
 

time: 230 us -> 215 us (0.935)
  Pallas kernels: 228 us -> 213 us
    pallas_call x1, Pallas kernels: 214 us -> 199 us  [layer_call(): pl.pallas_call(kernel, out_shape=list(outputs.values()), in_specs=[anywhe...]
where the time goes in v4:
time: 215 us
  Pallas kernels  213 us (99%)
    pallas_call x1, Pallas kernels, layer_call(): pl.pallas_call(kernel, out_shape=list(outputs.values()), in_specs=[anywhe...  199 us
    pallas_call x1, Pallas kernels, deliver_call(): pl.pallas_call(kernel, out_shape=[jax.ShapeDtypeStruct(shape.shape, shape...  14 us

profile of v4, /device:TPU:0, one launch (start us, length us, event | category | flops | bytes accessed | tf_op | source)
XLA Modules:
  0.0 214.7 jit_solution(6910960092693193829)
XLA Ops:
  0.6 1.3 copy.33.refs_9_
  1.9 198.5 %layer.1 = (bf16[1024,512]{1,0:T(8,128)(2,1)}, f32[1024,512]{1,0:T(8,128)}, f32[27136,128]{1,0:T(8,128)}) custom-call(bf16[1024,512]{1,0:T(8,128)(2,1)} %bitcast.16, bf16[512,512]{1,0:T(8,128)(2,1)} %refs_1_.1, bf16[512,512]{1,0:T(8,128)(2,1)} %refs_2_.1, bf16[512,512]{1,0:T(8,128)(2,1)} %refs_3_.1, bf16[512,512]{1,0:T(8,128)(2,1)} %refs_4_.1, ...), custom_call_target="tpu_custom_call" | custom-call | tf_op jit(solution)/shard_map/layer/pallas_call | solution.py:1065
  200.5 14.0 %deliver.1 = (bf16[1024,512]{1,0:T(8,128)(2,1)}, f32[1024,512]{1,0:T(8,128)}, f32[1,512]{1,0:T(1,128)}, f32[1,512]{1,0:T(1,128)}, f32[512,512]{1,0:T(8,128)}, /*...) custom-call(f32[27136,128]{1,0:T(8,128)} %get-tuple-element.35.full,, ...), custom_call_target="tpu_custom_call" | custom-call | tf_op jit(solution)/shard_map/deliver/pallas_call | solution.py:1014

commit v5 on v4

--- a/solution.py
+++ b/solution.py
@@ -18,10 +18,8 @@
 BF16 = jnp.bfloat16
 LANES = 128
 HALF = 256
-SHARE = 8
 DP, SEQ = "dp", "seq"
-CORE, LINE, NEAR, LOW, HIGH = range(5)
-LEVELS = 5
+CORE, LINE, NEAR, FAR = range(4)
 
 
 def mm(left, right):
@@ -154,25 +152,22 @@
             CORE: (2, core, lambda m: {DP: line * 2 + m}),
             LINE: (dp // 2, line, lambda m: {DP: m * 2 + core}),
             NEAR: (fast, near, lambda m: {SEQ: far * fast + m}),
-            LOW: (2, lax.rem(far, 2), lambda m: {SEQ: (far // 2 * 2 + m) * fast + near}),
-            HIGH: (2, far // 2, lambda m: {SEQ: (m * 2 + lax.rem(far, 2)) * fast + near}),
+            FAR: (slow, far, lambda m: {SEQ: m * fast + near}),
         }
         self.ways = dp // 2 * fast * slow
 
-    def orders(self, rows, index):
+    def orders(self, rows):
         half = rows // 2
-        least = self.ways * 8
-        if half >= 2 * least:
-            first = max(half // least * SHARE // 16, 1) * least
-            return [(0, first, (LINE, NEAR, LOW, HIGH)), (first, half - first, (NEAR, LINE, LOW, HIGH))]
-        return [(0, half, (LINE, NEAR, LOW, HIGH))]
+        if half % (2 * self.ways * 8) == 0:
+            return [(0, half // 2, (LINE, NEAR, FAR)), (half // 2, half // 2, (NEAR, LINE, FAR))]
+        return [(0, half, (LINE, NEAR, FAR))]
 
     def steps(self, chunk, level):
-        base, rows, land, index = chunk
+        base, rows, land, _ = chunk
         core = self.groups[CORE][1]
         if level == 0:
             return [(base, rows // 2, CORE, land)], rows // 2
-        orders = self.orders(rows, index)
+        orders = self.orders(rows)
         place = land + rows // 2
         sizes = [size for _, size, _ in orders]
         starts = [base + core * (rows // 2) + offset for offset, _, _ in orders]
@@ -189,7 +184,7 @@
         return found, sum(size * (self.groups[name][0] - 1) for _, size, name, _ in found)
 
     def rows_sent(self, chunk):
-        return 2 * sum(self.steps(chunk, level)[1] for level in range(LEVELS))
+        return 2 * sum(self.steps(chunk, level)[1] for level in range(4))
 
     def copy(self, chunk, slot, source, target, device):
         return pltpu.make_async_remote_copy(
@@ -208,13 +203,13 @@
                 to = lax.rem(at + k, count)
                 if gather:
                     rows = pl.ds(pl.multiple_of(start + at * size, 8), size)
-                    source = (self.held if level == LEVELS - 1 else self.full).at[rows]
+                    source = (self.held if level == 3 else self.full).at[rows]
                     target = self.full.at[rows]
                 else:
                     source = self.held.at[pl.ds(pl.multiple_of(start + to * size, 8), size)]
                     target = self.landed.at[pl.ds(pl.multiple_of(land + (k - 1) * size, 8), size)]
-                self.copy(chunk, level + LEVELS * gather, source, target, device(to)).start()
-            if gather and level == LEVELS - 1:
+                self.copy(chunk, level + 4 * gather, source, target, device(to)).start()
+            if gather and level == 3:
                 rows = pl.ds(pl.multiple_of(start + at * size, 8), size)
                 pltpu.make_async_copy(
                     self.held.at[rows], self.full.at[rows], self.keep_sem.at[chunk[3]]
@@ -224,8 +219,8 @@
         steps, rows = self.steps(chunk, level)
         at = pl.ds(chunk[0], rows) if gather else pl.ds(steps[0][3], rows)
         ref = (self.full if gather else self.landed).at[at]
-        self.copy(chunk, level + LEVELS * gather, ref, ref, self.groups[CORE][2](0)).wait_recv()
-        if gather and level == LEVELS - 1:
+        self.copy(chunk, level + 4 * gather, ref, ref, self.groups[CORE][2](0)).wait_recv()
+        if gather and level == 3:
             at = pl.ds(chunk[0], sum(size for _, size, _, _ in steps))
             pltpu.make_async_copy(
                 self.held.at[at], self.full.at[at], self.keep_sem.at[chunk[3]]
@@ -256,19 +251,16 @@
 
     def stage(self, chunk, number):
         if number:
-            summing = number <= LEVELS
-            level = number - 1 if summing else 2 * LEVELS - number
-            self.wait(chunk, level, not summing)
-            if summing:
+            level, gather = (number - 1, False) if number <= 4 else (8 - number, True)
+            self.wait(chunk, level, gather)
+            if not gather:
                 self.add(chunk, level)
-        if number < LEVELS:
-            self.start(chunk, number, False)
-        elif number < 2 * LEVELS:
-            self.start(chunk, 2 * LEVELS - 1 - number, True)
+        if number < 8:
+            self.start(chunk, *((number, False) if number < 4 else (7 - number, True)))
 
 
 def timetable(costs, begins):
-    line = [(0, 0.9), (1, 2.9), (1, 1.5), (2, 1.5), (2, 1.5)]
+    line = {0: (0, 0.9), 1: (1, 2.9), 2: (1, 1.5), 3: (2, 2.9)}
     now, free, ready, following = 0.0, [0.0] * 3, {}, {}
     table = [[] for _ in costs] + [[]]
 
@@ -277,11 +269,11 @@
         now += EVENT
         place.append((chunk, number))
         following[chunk] = number + 1
-        if number == 2 * LEVELS:
+        if number == 8:
             del following[chunk], ready[chunk]
             return
-        link, cost = line[min(number, 2 * LEVELS - 1 - number)]
-        free[link] = max(now, free[link]) + (cost if chunk < 13 else cost / 4)
+        link, cost = line[min(number, 7 - number)]
+        free[link] = max(now, free[link]) + (cost * SCALES[chunk])
         ready[chunk] = free[link] + LATENCY
 
     for moment, cost in enumerate(costs):
@@ -298,6 +290,9 @@
         chunk = min(following, key=lambda at: (ready[at], at))
         now = max(now, ready[chunk])
         take(chunk, following[chunk], table[-1])
+    order = [event for moment in table for event in moment]
+    for early, late in ((0, 9), (1, 11), (2, 13), (3, 15), (4, 17)):
+        assert order.index((early, 8)) < order.index((late, 0))
     return table
 
 
@@ -344,26 +339,31 @@
 ATTN_GAIN, ATTN_SHIFT, FFN_GAIN, FFN_SHIFT, DOWN_BIAS, WRITES, UP_BIAS = range(0, 28, 4)
 CHUNK = 2048
 EVENT = 0.35
-LATENCY = 3.0
+LATENCY = 1.5
 COSTS = [0.85] * 24 + [0.5] * 4 + [0.8, 1.0] + [0.9, 0.9, 1.1, 0.7, 0.3, 0.0] * 8
 COSTS += [0.9, 0.8, 0.8, 0.8, 1.0, 1.8, 0.9, 0.9] + [1.0] * 4 + [0.3]
-BEGINS = [4, 5, 10, 11, 16, 17, 22, 23, 28, 78, 83, 84, 85, 90]
+BEGINS = [4, 5, 10, 11, 16, 17, 22, 23, 28, 78, 78, 83, 83, 84, 84, 85, 85, 90]
+SCALES = [1.0] * 9 + [0.5] * 8 + [0.25]
 TABLE = timetable(COSTS, BEGINS)
 
 
 class Sizes:
     def __init__(self, dp, seq):
         self.dp, self.seq = dp, seq
-        self.tiny = max(512, dp // 2 * seq * 16)
+        ways = dp // 2 * seq
+        self.halves = CHUNK // 4 % (ways * 8) == 0
+        self.tiny = max(512, ways * 16)
         self.rows = 13 * CHUNK + self.tiny
         self.landing = 9 * CHUNK
+        self.chunks = [at for at in range(18) if self.halves or at < 9 or at % 2]
 
     def chunk(self, index):
-        land = index - 9 * (index >= 9) if isinstance(index, int) else jnp.where(index >= 9, index - 9, index)
-        return (index * CHUNK, CHUNK, land * CHUNK, index)
-
-    def last(self):
-        return (13 * CHUNK, self.tiny, 4 * CHUNK, 13)
+        if index < 9:
+            return (index * CHUNK, CHUNK, index * CHUNK, index)
+        if index == 17:
+            return (13 * CHUNK, self.tiny, 4 * CHUNK, 17)
+        first = (index - 9) * CHUNK // 2
+        return (9 * CHUNK + first, CHUNK // 2 if self.halves else CHUNK, first, index)
 
 
 def layer_kernel(sizes, refs):
@@ -434,12 +434,10 @@
         sizes.dp, seq, held, r.landed, r.out_full, r.reduce_send, r.reduce_recv, r.keep_sem
     )
 
-    def chunk_of(index):
-        return sizes.last() if index == 13 else sizes.chunk(index)
-
     def events(moment):
         for index, number in TABLE[moment]:
-            reduction.stage(chunk_of(index), number)
+            if index in sizes.chunks:
+                reduction.stage(sizes.chunk(index), number)
 
     def events_in(moments, *at):
         for indices, moment in moments.items():
@@ -872,8 +870,8 @@
 
     def weight_grad(index, right):
         for block in range(2):
-            wide = mm(turned[block * HALF : (block + 1) * HALF, :], right[...])
-            store_block(index * CHUNK, wide, block * HALF)
+            wide = mm(turned[...], right[:, block * HALF : (block + 1) * HALF])
+            store_block(index * CHUNK + block * 1024, wide, 0)
 
     def iteration(step, unused):
         backward((lax.rem(step, 2)) * 4 + step // 2, step)
@@ -925,7 +923,7 @@
         hidden, r.out_input_grad, r.load_sem.at[LOADS + 1]
     )
     grad_copy.start()
-    last = sizes.last()
+    last = sizes.chunk(17)
     held[pl.ds(last[0], last[1])] = jnp.zeros((last[1], LANES), F32)
     held[pl.ds(last[0], small.shape[0])] = small[...]
     events(90)
@@ -934,8 +932,8 @@
         copy.wait()
     for exchange in (*there, *back, *theres, *backs):
         exchange.finish()
-    for index in range(14):
-        reduction.finish(chunk_of(index))
+    for index in sizes.chunks:
+        reduction.finish(sizes.chunk(index))
 
 
 def deliver_kernel(full, result, input_grad, slot_means, count, *outs):
@@ -1052,8 +1050,8 @@
         held=pltpu.VMEM((sizes.rows, LANES), F32), landed=pltpu.VMEM((sizes.landing, LANES), F32),
         box0=box, box1=box, box2=box, box3=box, box4=pair_box, box5=pair_box, box6=pair_box, box7=pair_box,
         box_sem=semaphores((4, 2)), pair_sem=semaphores((4, 4)), load_sem=semaphores((LOADS + 2,)), up_sem=semaphores((4,)),
-        keep_sem=semaphores((14,)), reduce_send=semaphores((14,)),
-        reduce_recv=semaphores((14, 2 * LEVELS)),
+        keep_sem=semaphores((18,)), reduce_send=semaphores((18,)),
+        reduce_recv=semaphores((18, 8)),
     )
     names = list(arrays) + list(outputs) + list(scratch)
 

time: 215 us -> 208 us (0.967)
  Pallas kernels: 213 us -> 205 us
    pallas_call x1, Pallas kernels: 199 us -> 191 us  [layer_call(): pl.pallas_call(kernel, out_shape=list(outputs.values()), in_specs=[anywhe...]
where the time goes in v5:
time: 208 us; the launch traced here: 207 us
  Pallas kernels  205 us (99%)
    pallas_call x1, Pallas kernels, layer_call(): pl.pallas_call(kernel, out_shape=list(outputs.values()), in_specs=[anywhe...  191 us
    pallas_call x1, Pallas kernels, deliver_call(): pl.pallas_call(kernel, out_shape=[jax.ShapeDtypeStruct(shape.shape, shape...  14 us

profile of v5, /device:TPU:0, one launch (start us, length us, event | category | flops | bytes accessed | tf_op | source)
XLA Modules:
  0.0 207.3 jit_solution(5924640098763555518)
XLA Ops:
  0.6 1.3 copy.33.refs_9_
  1.9 191.2 %layer.1 = (bf16[1024,512]{1,0:T(8,128)(2,1)}, f32[1024,512]{1,0:T(8,128)}, f32[27136,128]{1,0:T(8,128)}) custom-call(bf16[1024,512]{1,0:T(8,128)(2,1)} %bitcast.16, bf16[512,512]{1,0:T(8,128)(2,1)} %refs_1_.1, bf16[512,512]{1,0:T(8,128)(2,1)} %refs_2_.1, bf16[512,512]{1,0:T(8,128)(2,1)} %refs_3_.1, bf16[512,512]{1,0:T(8,128)(2,1)} %refs_4_.1, ...), custom_call_target="tpu_custom_call" | custom-call | tf_op jit(solution)/shard_map/layer/pallas_call | solution.py:1063
  193.1 14.0 %deliver.1 = (bf16[1024,512]{1,0:T(8,128)(2,1)}, f32[1024,512]{1,0:T(8,128)}, f32[1,512]{1,0:T(1,128)}, f32[1,512]{1,0:T(1,128)}, f32[512,512]{1,0:T(8,128)}, /*...) custom-call(f32[27136,128]{1,0:T(8,128)} %get-tuple-element.35.full,, ...), custom_call_target="tpu_custom_call" | custom-call | tf_op jit(solution)/shard_map/deliver/pallas_call | solution.py:1012

commit v6 on v5

--- a/solution.py
+++ b/solution.py
@@ -480,7 +480,7 @@
         memory = add_parts(mm_rows(pair_rows, parts_of(spread)))
         memory = jnp.concatenate([one_block(memory[:LANES]), one_block(memory[LANES:])], axis=0)
         total = column_sum(spread)
-        flag = jnp.broadcast_to(r.starts[stream : stream + 1, :].astype(F32), (1, LANES))
+        flag = jnp.broadcast_to(r.starts[:, stream : stream + 1].astype(F32), (1, LANES))
         line = iota((8, LANES), 0)
         notes[combo] = jnp.where(line == 0, block_max, jnp.where(line == 1, total, flag))
         for group in range(seq // 4):
@@ -944,11 +944,11 @@
     loads = [
         pltpu.make_async_copy(full.at[rows], held.at[rows], in_sem.at[at])
         for at, rows in enumerate(
-            [pl.ds(13 * CHUNK, 40)] + [pl.ds(at * CHUNK, CHUNK) for at in range(13)]
+            [pl.ds(13 * CHUNK, 40)] + [pl.ds(at * 1024, 1024) for at in range(26)]
         )
     ]
-    loads.append(pltpu.make_async_copy(result, held_result, in_sem.at[14]))
-    loads.append(pltpu.make_async_copy(input_grad, held_grad, in_sem.at[15]))
+    loads.append(pltpu.make_async_copy(result, held_result, in_sem.at[27]))
+    loads.append(pltpu.make_async_copy(input_grad, held_grad, in_sem.at[28]))
     for copy in loads:
         copy.start()
     stores = []
@@ -959,8 +959,9 @@
         stores.append(copy)
 
     for index in range(13):
-        loads[1 + index].wait()
         for column in range(4):
+            if column % 2 == 0:
+                loads[1 + 2 * index + column // 2].wait()
             lanes = pl.ds(column * LANES, LANES)
             source = held.at[pl.ds(index * CHUNK + column * 512, 512)]
             if index >= 8:
@@ -969,9 +970,9 @@
                 store(source, up.at[:, pl.ds(index // 2 * 512 + column * LANES, LANES)])
             else:
                 store(source, down.at[pl.ds(index // 2 * 512, 512), lanes])
-    loads[14].wait()
+    loads[27].wait()
     store(held_result, out_result)
-    loads[15].wait()
+    loads[28].wait()
     store(held_grad, out_input_grad)
     loads[0].wait()
     small = held.at[pl.ds(13 * CHUNK, 40)]
@@ -1018,7 +1019,7 @@
             pltpu.VMEM((13 * CHUNK + 40, LANES), F32),
             pltpu.VMEM(result.shape, BF16),
             pltpu.VMEM(input_grad.shape, F32),
-            pltpu.SemaphoreType.DMA((16,)),
+            pltpu.SemaphoreType.DMA((29,)),
             pltpu.SemaphoreType.DMA((54,)),
         ],
         compiler_params=pltpu.CompilerParams(vmem_limit_bytes=60 * 2**20),
@@ -1094,7 +1095,7 @@
             in_up=up_weight,
             in_down=down_weight,
             in_pull=cotangent.reshape(rows, width),
-            starts=starts,
+            starts=starts.reshape(1, streams),
             attn_gain=attn_gain[None],
             attn_shift=attn_shift[None],
             ffn_gain=ffn_gain[None],

time: 208 us -> 206 us (level)
  no operation moved by 1% of the time
where the time goes in v6:
time: 206 us
  Pallas kernels  205 us (100%)
    pallas_call x1, Pallas kernels, layer_call(): pl.pallas_call(kernel, out_shape=list(outputs.values()), in_specs=[anywhe...  191 us
    pallas_call x1, Pallas kernels, deliver_call(): pl.pallas_call(kernel, out_shape=[jax.ShapeDtypeStruct(shape.shape, shape...  13.9 us

profile of v6, /device:TPU:0, one launch (start us, length us, event | category | flops | bytes accessed | tf_op | source)
XLA Modules:
  0.0 206.0 jit_solution(7700618444801089833)
XLA Ops:
  0.7 191.3 %layer.1 = (bf16[1024,512]{1,0:T(8,128)(2,1)}, f32[1024,512]{1,0:T(8,128)}, f32[27136,128]{1,0:T(8,128)}) custom-call(bf16[1024,512]{1,0:T(8,128)(2,1)} %bitcast.17, bf16[512,512]{1,0:T(8,128)(2,1)} %refs_1_.1, bf16[512,512]{1,0:T(8,128)(2,1)} %refs_2_.1, bf16[512,512]{1,0:T(8,128)(2,1)} %refs_3_.1, bf16[512,512]{1,0:T(8,128)(2,1)} %refs_4_.1, ...), custom_call_target="tpu_custom_call" | custom-call | tf_op jit(solution)/shard_map/layer/pallas_call | solution.py:1064
  191.9 13.9 %deliver.1 = (bf16[1024,512]{1,0:T(8,128)(2,1)}, f32[1024,512]{1,0:T(8,128)}, f32[1,512]{1,0:T(1,128)}, f32[1,512]{1,0:T(1,128)}, f32[512,512]{1,0:T(8,128)}, /*...) custom-call(f32[27136,128]{1,0:T(8,128)} %get-tuple-element.35.full,, ...), custom_call_target="tpu_custom_call" | custom-call | tf_op jit(solution)/shard_map/deliver/pallas_call | solution.py:1013
